TPU v7x, 256 devices: a whole 4x4x8 slice. The times are simulated.
256 devices in a mesh: pool: 64 (over z, x, core), head: 4 (over y).
Axes of the slice: x: 4, y: 4, z: 8, core: 2. Of those that a mesh axis runs over, the one named last changes fastest.
Arguments:
- hidden_rows: bfloat16 [256, 8192], P(None, 'pool'), may hold values from -48 to 48
- cache_kv: bfloat16 [64, 512, 2, 1024], P(None, 'pool', None, 'head'), may hold values from -16 to 16
- sel_index: int32 [192], replicated, may hold values from 0 to 32767, as said below
- doc_order: int32 [64], replicated, may hold values from 0 to 63, each once
- attn_gain: bfloat16 [8192], P('pool'), may hold values from 0.099609375 to 1.8984375
- w_query: bfloat16 [8192, 8192], P('pool', 'head'), may hold values from -1 to 1
- w_keyval: bfloat16 [8192, 2, 1024], P('pool', None, 'head'), may hold values from -0.1875 to 0.1875
- w_output: bfloat16 [8192, 8192], P('head', 'pool'), may hold values from -0.0625 to 0.0625
- ffn_gain: bfloat16 [8192], P('pool'), may hold values from 0.099609375 to 1.8984375
- w_in: bfloat16 [8192, 2, 28672], P(None, None, ('pool', 'head')), may hold values from -0.0625 to 0.0625
- w_out: bfloat16 [28672, 8192], P(('pool', 'head')), may hold values from -0.15625 to 0.15625
Outputs:
- layer_out: bfloat16 [256, 8192], P('head', 'pool')
- joined_cache: bfloat16 [32768, 2, 1024], P('pool', None, 'head')
Inputs may be any that keep to these rules, and one draw needn't show every extreme that they name: `sel_index`: distinct values; 0 and 32767 are always present; the count per document varies.
All inputs are finite; a program needn't handle non-finite values.
Results may differ from a plain program's by a relative error of at most 0.017.
Values may be sent and summed in bfloat16 or wider, within the bound.
No kernel may reach another device: no remote copies, remote signals or barrier semaphores. Data moves between devices by JAX's collectives and lax.ppermute only.
A program may use at most 64 MiB of HBM per device.

v0:
```python
import jax
import jax.numpy as jnp
from jax import lax
from jax.sharding import PartitionSpec as P

D = 8192
HEAD_DIM = 128
DOC_LEN = 512
SEL_DEV = 3
QRY_DEV = 1


EPS = 1e-05
NEG = -1e30


def row_positions(sel_index, doc_order, pool):
    docs = jnp.arange(pool, dtype=jnp.int32)
    slot_of_doc = jnp.sum(jnp.where(doc_order[:, None] == docs[None, :], docs[:, None], 0), axis=0)
    sel_doc = sel_index // DOC_LEN
    sel_tok = sel_index % DOC_LEN
    sel_slot = jnp.sum(
        jnp.where(sel_doc[:, None] == docs[None, :], slot_of_doc[None, :], 0), axis=1
    )
    sel_pos = sel_slot * DOC_LEN + sel_tok
    query_pos = DOC_LEN * pool + jnp.arange(pool * QRY_DEV, dtype=jnp.int32)
    row_pos = jnp.concatenate(
        [sel_pos.reshape(pool, SEL_DEV), query_pos.reshape(pool, QRY_DEV)], axis=1
    ).reshape(-1)
    return (sel_slot, sel_tok, row_pos)


def normalize(values, squares, gain):
    factor = lax.rsqrt(squares[:, None] / D + EPS)
    return (values * factor * gain.astype(jnp.float32)[None, :]).astype(jnp.bfloat16)


def shards(
    hidden_rows,
    cache_kv,
    sel_index,
    doc_order,
    attn_gain,
    w_query,
    w_keyval,
    w_output,
    ffn_gain,
    w_in,
    w_out,
):
    pool = lax.axis_size("pool")
    mine = lax.axis_index("pool")
    head_index = lax.axis_index("head")
    heads_count = lax.axis_size("head")
    rows, cols = hidden_rows.shape
    rows_dev = rows // pool
    query_width = w_query.shape[1]
    kv_width = w_keyval.shape[2]
    kv_dev = kv_width // HEAD_DIM
    heads_dev = query_width // HEAD_DIM
    group = heads_dev // kv_dev
    local_len = DOC_LEN
    inputs = hidden_rows.astype(jnp.float32)
    squares = lax.psum(jnp.sum(inputs * inputs, axis=1), "pool")
    normed = normalize(inputs, squares, attn_gain)
    keyval_flat = w_keyval.reshape(cols, 2 * kv_width)
    first = jnp.dot(normed, w_query, preferred_element_type=jnp.float32)
    second = jnp.dot(normed, keyval_flat, preferred_element_type=jnp.float32)
    owned = lax.psum_scatter(
        jnp.concatenate([first, second], axis=1), "pool", scatter_dimension=0, tiled=True
    )
    q_mine = owned[:, :query_width].astype(jnp.bfloat16)
    kv_mine = owned[:, query_width:].astype(jnp.bfloat16).reshape(rows_dev, 2, kv_width)
    sel_mine = kv_mine[:SEL_DEV]
    extra_kv = kv_mine[SEL_DEV:]
    queries, sel_kv = (
        lax.all_gather(q_mine, "pool", axis=0, tiled=True),
        lax.all_gather(sel_mine, "pool", axis=0, tiled=True),
    )
    reordered = jnp.take(cache_kv, doc_order, axis=0)
    slot_cache = lax.all_to_all(reordered, "pool", split_axis=0, concat_axis=1, tiled=True).reshape(
        local_len, 2, kv_width
    )
    sel_slot, sel_tok, row_pos = row_positions(sel_index, doc_order, pool)
    token_ids = jnp.arange(local_len, dtype=jnp.int32)
    hits = (sel_slot[:, None] == mine) & (sel_tok[:, None] == token_ids[None, :])
    covered = jnp.any(hits, axis=0)
    placed = jnp.einsum(
        "st,sc->tc",
        hits.astype(jnp.bfloat16),
        sel_kv.reshape(sel_kv.shape[0], 2 * kv_width),
        preferred_element_type=jnp.float32,
    )
    placed = placed.astype(jnp.bfloat16).reshape(local_len, 2, kv_width)
    joined_local = jnp.where(covered[:, None, None], placed, slot_cache)
    cache_pos = mine * local_len + token_ids
    extra_pos = DOC_LEN * pool + mine * QRY_DEV + jnp.arange(QRY_DEV, dtype=jnp.int32)
    scale = 1.0 / HEAD_DIM**0.5
    rep_pos = jnp.repeat(row_pos, group)
    head_queries = queries.reshape(rows, kv_dev, group, HEAD_DIM)
    kept_c = cache_pos[None, :] <= rep_pos[:, None]
    kept_e = extra_pos[None, :] <= rep_pos[:, None]
    tops, totals, accs = ([], [], [])
    for kv_head in range(kv_dev):
        lower = kv_head * HEAD_DIM
        q_rows = head_queries[:, kv_head].reshape(rows * group, HEAD_DIM)
        keys_c = joined_local[:, 0, lower : lower + HEAD_DIM]
        values_c = joined_local[:, 1, lower : lower + HEAD_DIM]
        keys_e = extra_kv[:, 0, lower : lower + HEAD_DIM]
        values_e = extra_kv[:, 1, lower : lower + HEAD_DIM]
        scores_c = (
            jnp.einsum("qd,kd->qk", q_rows, keys_c, preferred_element_type=jnp.float32) * scale
        )
        scores_e = (
            jnp.einsum("qd,kd->qk", q_rows, keys_e, preferred_element_type=jnp.float32) * scale
        )
        scores_c = jnp.where(kept_c, scores_c, NEG)
        scores_e = jnp.where(kept_e, scores_e, NEG)
        top = jnp.maximum(jnp.max(scores_c, axis=1), jnp.max(scores_e, axis=1))
        probs_c = jnp.where(kept_c, jnp.exp(scores_c - top[:, None]), 0.0)
        probs_e = jnp.where(kept_e, jnp.exp(scores_e - top[:, None]), 0.0)
        total = jnp.sum(probs_c, axis=1) + jnp.sum(probs_e, axis=1)
        acc = jnp.dot(probs_c.astype(jnp.bfloat16), values_c, preferred_element_type=jnp.float32)
        acc = acc + jnp.dot(
            probs_e.astype(jnp.bfloat16), values_e, preferred_element_type=jnp.float32
        )
        tops.append(top.reshape(rows, group))
        totals.append(total.reshape(rows, group))
        accs.append(acc.reshape(rows, group * HEAD_DIM))
    top_all = jnp.concatenate(tops, axis=1)
    total_all = jnp.concatenate(totals, axis=1)
    acc_all = jnp.concatenate(accs, axis=1)
    top_m = lax.pmax(top_all, "pool")
    factor = jnp.exp(top_all - top_m)
    scaled = (acc_all.reshape(rows, heads_dev, HEAD_DIM) * factor[..., None]).reshape(
        rows, query_width
    )
    total_m, acc_m = lax.psum((total_all * factor, scaled), "pool")
    attended = (
        (acc_m.reshape(rows, heads_dev, HEAD_DIM) / total_m[..., None])
        .reshape(rows, query_width)
        .astype(jnp.bfloat16)
    )
    projected = jnp.dot(attended, w_output, preferred_element_type=jnp.float32)
    mid = inputs + lax.psum(projected.astype(jnp.bfloat16), "head").astype(jnp.float32)
    mid_squares = lax.psum(jnp.sum(mid * mid, axis=1), "pool")
    ffn_in = normalize(mid, mid_squares, ffn_gain)
    hidden_dev = w_in.shape[2]
    in_flat = w_in.reshape(w_in.shape[0], 2 * hidden_dev)
    both = jnp.dot(
        lax.all_gather(ffn_in, "pool", axis=1, tiled=True),
        in_flat,
        preferred_element_type=jnp.float32,
    )
    act = (jax.nn.silu(both[:, :hidden_dev]) * both[:, hidden_dev:]).astype(jnp.bfloat16)
    rows_head = rows // heads_count
    term = jnp.dot(act, w_out, preferred_element_type=jnp.float32)
    by_cols = lax.psum_scatter(term, "pool", scatter_dimension=1, tiled=True)
    down = lax.psum_scatter(
        by_cols.astype(jnp.bfloat16), "head", scatter_dimension=0, tiled=True
    ).astype(jnp.float32)
    mid_rows = lax.dynamic_slice_in_dim(mid, head_index * rows_head, rows_head, 0)
    layer_out = (mid_rows + down).astype(jnp.bfloat16)
    return (layer_out, joined_local)


def solution(mesh):
    return jax.shard_map(
        shards,
        mesh=mesh,
        in_specs=(
            P(None, "pool"),
            P(None, "pool", None, "head"),
            P(),
            P(),
            P("pool"),
            P("pool", "head"),
            P("pool", None, "head"),
            P("head", "pool"),
            P("pool"),
            P(None, None, ("pool", "head")),
            P(("pool", "head"), None),
        ),
        out_specs=(P("head", "pool"), P("pool", None, "head")),
        check_vma=False,
    )
```

profile of v0, /device:TPU:4, one launch (start us, length us, event | category | flops | bytes accessed | tf_op | source)
XLA Modules:
  0.0 1473.0 jit_solution(1430014342349120251)
XLA Ops:
  8.7 2.7 gather_fusion
  11.3 1.4 broadcast_select_fusion
  12.7 12.0 all-to-all-start
  27.3 119.4 %psum.35 = f32[256]{0:T(256)S(1)} all-reduce(f32[256]{0:T(256)S(1)} %fusion.37), channel_id=1, replica_groups=mesh['pool'=64,'head'=4] {'pool'}, use_global_device_ids=true, to_apply=%region_3.4 | all-reduce | flops 256 | bytes 2048 | tf_op jit(solution)/shard_map/psum | solution.py:64
  146.7 1.1 fusion.44
  147.8 1.5 fusion.46
  149.4 1.7 pad_maximum_fusion
  151.1 272.9 %all-reduce.8 = bf16[256,2560]{1,0:T(8,128)(2,1)} all-reduce(f32[256,2560]{1,0:T(8,128)} %pad_maximum_fusion), channel_id=2, replica_groups=mesh['pool'=64,'head'=4] {'pool'}, use_global_device_ids=true, to_apply=%region_4.5.clone | all-reduce | flops 655360 | bytes 3932160
  427.6 52.0 %all_gather.10 = bf16[192,2,256]{2,1,0:T(2,128)(2,1)S(1)} all-gather(bf16[3,2,256]{2,1,0:T(2,128)(2,1)S(1)} %slice.59), channel_id=1, replica_groups=mesh['pool'=64,'head'=4] {'pool'}, dimensions={0}, use_global_device_ids=true | all-gather | bytes 199680 | tf_op jit(solution)/shard_map/all_gather | solution.py:78
  480.6 32.5 %all-gather.6.cloned.1.call-done = bf16[64,4,2048]{2,1,0:T(4,128)(2,1)} async-done(((bf16[1,4,2048]{2,1,0:T(4,128)(2,1)}), bf16[64,4,2048]{2,1,0:T(4,128)(2,1)}) %all-gather.6.cloned.1.call-update) | async-done | bytes 1048592 | tf_op jit(solution)/shard_map/all_gather | solution.py:77
  513.1 1.7 reshape.166
  515.3 2.7 fusion
  518.8 4.8 fusion.2
  523.7 3.4 fusion.4
  527.6 239.6 %pmax.7 = f32[256,16]{0,1:T(8,128)S(1)} all-reduce(f32[256,16]{0,1:T(8,128)S(1)} %pad_maximum_fusion.1), channel_id=1, replica_groups=mesh['pool'=64,'head'=4] {'pool'}, use_global_device_ids=true, to_apply=%region_8.9 | all-reduce | flops 4096 | bytes 32768 | tf_op jit(solution)/shard_map/pmax | solution.py:133
  767.4 3.8 fusion.24
  771.2 1.5 fusion.21
  773.5 2.2 copy.45
  775.8 246.3 %psum.37 = f32[256,16]{0,1:T(8,128)S(1)} all-reduce(f32[256,16]{0,1:T(8,128)S(1)} %get-tuple-element.10), channel_id=1, replica_groups=mesh['pool'=64,'head'=4] {'pool'}, use_global_device_ids=true, to_apply=%region_12.13 | all-reduce | flops 4096 | bytes 32768 | tf_op jit(solution)/shard_map/psum | solution.py:138
  1022.8 3.1 convolution_convert_fusion.1
  1026.1 53.7 %all-reduce.7.cloned.1.call-done = bf16[256,128]{1,0:T(8,128)(2,1)} async-done(((bf16[256,128]{1,0:T(8,128)(2,1)}), bf16[256,128]{1,0:T(8,128)(2,1)}) %all-reduce.7.cloned.1.call-update) | async-done | bytes 65552 | tf_op jit(solution)/shard_map/psum | solution.py:145
  1079.8 1.0 convert_add_fusion
  1080.7 116.9 %psum.39 = f32[256]{0:T(256)S(1)} all-reduce(f32[256]{0:T(256)S(1)} %get-tuple-element.17), channel_id=1, replica_groups=mesh['pool'=64,'head'=4] {'pool'}, use_global_device_ids=true, to_apply=%region_15.16 | all-reduce | flops 256 | bytes 2048 | tf_op jit(solution)/shard_map/psum | solution.py:146
  1197.6 1.6 multiply_convert_fusion
  1199.3 82.2 %all-gather.4.cloned.1.call-done = bf16[256,8192]{1,0:T(8,128)(2,1)} async-done(((bf16[256,128]{1,0:T(8,128)(2,1)}), bf16[256,8192]{1,0:T(8,128)(2,1)}) %all-gather.4.cloned.1.call-update) | async-done | bytes 4194320 | tf_op jit(solution)/shard_map/all_gather | solution.py:151
  1281.4 4.7 fusion.61
  1286.2 4.5 fusion.41
  1290.7 149.8 %reduce-scatter.3.cloned.1.call-done = f32[256,128]{1,0:T(8,128)} async-done(((f32[256,8192]{1,0:T(8,128)}), f32[256,128]{1,0:T(8,128)}) %reduce-scatter.3.cloned.1.call-update) | async-done | bytes 131088 | tf_op jit(solution)/shard_map/reduce_scatter | solution.py:158
  1440.5 1.5 convert_element_type.70
  1442.1 1.3 copy.36
  1443.4 21.4 %reduce-scatter.5.cloned.1.call-done = bf16[64,128]{1,0:T(8,128)(2,1)} async-done(((bf16[256,128]{1,0:T(8,128)(2,1)}), bf16[64,128]{1,0:T(8,128)(2,1)}) %reduce-scatter.5.cloned.1.call-update) | async-done | bytes 16400 | tf_op jit(solution)/shard_map/reduce_scatter | solution.py:159
  1464.9 1.3 add_convert_fusion
  (86 shorter events, 11.6 us)
Async XLA Ops:
  7.2 1279.0 %copy-start = (bf16[112,8192]{1,0:T(8,128)(2,1)S(1)}, bf16[112,8192]{1,0:T(8,128)(2,1)}, u32[]{:S(2)}) copy-start(bf16[112,8192]{1,0:T(8,128)(2,1)} %param.21) | copy-start | bytes 5505028
  7.2 140.6 %copy-start.1 = (bf16[256,128]{1,0:T(8,128)(2,1)S(1)}, bf16[256,128]{1,0:T(8,128)(2,1)}, u32[]{:S(2)}) copy-start(bf16[256,128]{1,0:T(8,128)(2,1)} %param.11) | copy-start | bytes 196612
  12.7 467.8 %all-to-all-start = ((bf16[64,8,2,256]{3,2,1,0:T(2,128)(2,1)}), bf16[64,8,2,256]{3,2,1,0:T(2,128)(2,1)S(1)}, u32[]{:S(2)}, u32[]{:S(2)}) async-start(bf16[64,8,2,256]{3,2,1,0:T(2,128)(2,1)} %broadcast_select_fusion), calls=%async_computation | async-start | bytes 1048576 | tf_op jit(solution)/shard_map/all_to_all | solution.py:81
  24.7 488.4 %all-gather.6.cloned.1.call-start = ((), (), s32[]{:S(2)}) async-start(), calls=%async_computation.8 | async-start | bytes 1064960 | tf_op jit(solution)/shard_map/all_gather | solution.py:77
  149.3 274.7 %copy-start.7 = (u32[256]{0:T(256)S(1)}, u32[256]{0:T(256)}, u32[]{:S(2)}) copy-start(u32[256]{0:T(256)} %constant.85) | copy-start | bytes 3076
  149.4 277.4 %copy-start.3 = (s32[192]{0:T(256)S(1)}, s32[192]{0:T(256)}, u32[]{:S(2)}) copy-start(s32[192]{0:T(256)} %param.13) | copy-start | bytes 2308
  149.4 277.4 %copy-start.5 = (s32[64]{0:T(128)S(1)}, s32[64]{0:T(128)}, u32[]{:S(2)}) copy-start(s32[64]{0:T(128)} %param.14) | copy-start | bytes 772
  426.7 595.5 %all-reduce.5.cloned.1.call-start = ((), (), s32[]{:S(2)}) async-start(), calls=%async_computation.3 | async-start | bytes 4194304 | tf_op jit(solution)/shard_map/psum | solution.py:138
  523.6 3.9 copy-start.2
  767.4 3.9 copy-start.8
  773.5 249.3 %copy-start.4 = (bf16[2048,128]{1,0:T(8,128)(2,1)S(1)}, bf16[2048,128]{1,0:T(8,128)(2,1)}, u32[]{:S(2)}) copy-start(bf16[2048,128]{1,0:T(8,128)(2,1)} %param.18) | copy-start | bytes 1572868
  775.7 304.1 %all-reduce.7.cloned.1.call-start = ((), (), s32[]{:S(2)}) async-start(), calls=%async_computation.4 | async-start | bytes 131072 | tf_op jit(solution)/shard_map/psum | solution.py:145
  1022.8 3.2 copy-start.6
  1026.0 255.4 %all-gather.4.cloned.1.call-start = ((), (), s32[]{:S(2)}) async-start(), calls=%async_computation.5 | async-start | bytes 4259840 | tf_op jit(solution)/shard_map/all_gather | solution.py:151
  1199.2 241.3 %reduce-scatter.3.cloned.1.call-start = ((), (), s32[]{:S(2)}) async-start(), calls=%async_computation.6 | async-start | bytes 8519680 | tf_op jit(solution)/shard_map/reduce_scatter | solution.py:158
  1290.7 174.2 %reduce-scatter.5.cloned.1.call-start = ((), (), s32[]{:S(2)}) async-start(), calls=%async_computation.7 | async-start | bytes 81920 | tf_op jit(solution)/shard_map/reduce_scatter | solution.py:159
Sparse Core Ops, SparseCore 0:
  426.8 86.2 all-gather.5
  775.8 196.8 all-reduce.4
  1026.1 53.6 all-reduce.6
  1199.3 82.0 all-gather.3
  1290.8 149.6 reduce-scatter.2
  1442.9 21.9 reduce-scatter.4
where the time goes:
time: 1470 us
  blocking collectives  1050 us (71%)
  waiting for transfers between devices  340 us (23%)
  matrix products  28.8 us (2%)
  other arithmetic  16.3 us (1%)
  between operations  15.2 us (1%)
    unnamed x1, blocking collectives  273 us
    psum x1, blocking collectives, shards(): total_m, acc_m = lax.psum((total_all * factor, scaled), 'pool')  246 us
    pmax x1, blocking collectives, shards(): top_m = lax.pmax(top_all, 'pool')  240 us
    reduce_scatter x1, waiting for transfers between devices, shards(): by_cols = lax.psum_scatter(term, 'pool', scatter_dimension=1, tiled=True)  150 us
    psum x1, blocking collectives, shards(): squares = lax.psum(jnp.sum(inputs * inputs, axis=1), 'pool')  119 us
    psum x1, blocking collectives, shards(): mid_squares = lax.psum(jnp.sum(mid * mid, axis=1), 'pool')  117 us
    all_gather x1, waiting for transfers between devices, shards(): lax.all_gather(ffn_in, 'pool', axis=1, tiled=True)  82.2 us
    psum x1, waiting for transfers between devices, shards(): lax.psum(projected.astype(jnp.bfloat16), 'head').astype(jnp.float32)  53.7 us
  transfers between devices with their start and end apart: 7, of which 5 were waited for; matrix products, arithmetic and copies ran while one was open for 1% of the time, Pallas kernels for 0%

commit v1 on v0

v1 whole, which is shorter than its diff:
```python
import functools

import jax
import jax.numpy as jnp
from jax import lax
from jax.experimental import pallas as pl
from jax.experimental.pallas import tpu as pltpu
from jax.sharding import Mesh
from jax.sharding import PartitionSpec as P

D = 8192
HEAD_DIM = 128
DOC_LEN = 512
SEL_DEV = 3
EPS = 1e-05
NEG = -1e30
FLOOR = -1e29
NZ, NX, NC, NY = 8, 4, 2, 4
POOL = NZ * NX * NC
ROWS = 256
EXT = 528

BF = jnp.bfloat16
F32 = jnp.float32


def exchange_cores(value):
    return lax.ppermute(value, "c", [(0, 1), (1, 0)])


def shift_y(value, step):
    return lax.ppermute(value, "y", [(i, (i + step) % NY) for i in range(NY)])


def permute_xy(value, target):
    pairs = []
    for x in range(NX):
        for y in range(NY):
            to_x, to_y = target(x, y)
            pairs.append((x * NY + y, (to_x % NX) * NY + to_y % NY))
    return lax.ppermute(value, ("x", "y"), pairs)


def swap_zx(value):
    return lax.all_to_all(value, ("z", "x"), 0, 0, tiled=True)


def parts_of(value):
    high = lax.reduce_precision(value, 8, 7)
    rest = value - high
    middle = lax.reduce_precision(rest, 8, 7)
    low = rest - middle
    return [high.astype(BF), middle.astype(BF), low.astype(BF)]


def positions(sel_index, doc_order, mine):
    docs = jnp.arange(POOL, dtype=jnp.int32)
    slot_of_doc = jnp.sum(jnp.where(doc_order[:, None] == docs[None, :], docs[:, None], 0), axis=0)
    sel_doc = sel_index // DOC_LEN
    sel_tok = sel_index % DOC_LEN
    sel_slot = jnp.sum(
        jnp.where(sel_doc[:, None] == docs[None, :], slot_of_doc[None, :], 0), axis=1
    )
    sel_pos = sel_slot * DOC_LEN + sel_tok
    query_pos = DOC_LEN * POOL + docs
    row_pos = jnp.concatenate([sel_pos.reshape(POOL, SEL_DEV), query_pos[:, None]], axis=1)
    sel_key = jnp.where(sel_slot == mine, sel_tok, -1)
    query_key = jnp.where(docs == mine, DOC_LEN, -1)
    row_key = jnp.concatenate([sel_key.reshape(POOL, SEL_DEV), query_key[:, None]], axis=1)
    both = jnp.stack([row_pos.reshape(ROWS), row_key.reshape(ROWS)])
    return jnp.concatenate([both, jnp.zeros((6, ROWS), jnp.int32)], axis=0)


def attend_kernel(
    place_ref, info_ref, own_ref, other_ref, cache_ref, joined_ref, acc_ref, sent_ref, stat_ref
):
    core = place_ref[0]
    mine = place_ref[1]
    row_pos = info_ref[0:1, :]
    row_key = info_ref[1:2, :]
    token = lax.broadcasted_iota(jnp.int32, (EXT, ROWS), 0)
    hit = token == row_key
    hits = jnp.where(hit, 1.0, 0.0)
    covered = jnp.max(hits, axis=1, keepdims=True) > 0.0
    hits = hits.astype(BF)
    key_pos = jnp.where(
        token < DOC_LEN,
        mine * DOC_LEN + token,
        jnp.where(token == DOC_LEN, DOC_LEN * POOL + mine, DOC_LEN * POOL * 2),
    )
    kept = key_pos <= row_pos
    nt = (((1,), (1,)), ((), ()))
    tn = (((0,), (0,)), ((), ()))
    for rel in range(2):
        new_ref = own_ref if rel == 0 else other_ref
        group = core if rel == 0 else 1 - core
        sides = []
        for side in range(2):
            new = new_ref[1024 + side * 128 : 1152 + side * 128, :]
            placed = lax.dot_general(hits, new, nt, preferred_element_type=F32).astype(BF)
            at = pl.ds(pl.multiple_of(side * 256 + group * 128, 128), 128)
            old = cache_ref[:, at]
            joined = jnp.where(covered[:DOC_LEN], placed[:DOC_LEN], old)
            joined_ref[:, at] = joined
            sides.append(jnp.concatenate([joined, placed[DOC_LEN:]], axis=0))
        keys, values = sides
        for head in range(8):
            query = new_ref[head * 128 : head * 128 + 128, :]
            scores = jnp.dot(keys, query, preferred_element_type=F32) * (HEAD_DIM**-0.5)
            scores = jnp.where(kept, scores, NEG)
            top = jnp.maximum(jnp.max(scores, axis=0, keepdims=True), FLOOR)
            probs = jnp.exp(scores - top)
            total = jnp.sum(probs, axis=0, keepdims=True)
            acc = lax.dot_general(values, probs.astype(BF), tn, preferred_element_type=F32)
            if rel == 0:
                acc_ref[head * 128 : head * 128 + 128, :] = acc
            else:
                sent_ref[head * 128 : head * 128 + 128, :] = acc.astype(BF)
            stat_ref[rel, 0, head : head + 1, :] = top
            stat_ref[rel, 1, head : head + 1, :] = total


def attend(place, info, own, other, cache):
    vmem = pl.BlockSpec(memory_space=pltpu.VMEM)
    return pl.pallas_call(
        attend_kernel,
        out_shape=(
            jax.ShapeDtypeStruct((DOC_LEN, 512), BF),
            jax.ShapeDtypeStruct((1024, ROWS), F32),
            jax.ShapeDtypeStruct((1024, ROWS), BF),
            jax.ShapeDtypeStruct((2, 2, 8, ROWS), F32),
        ),
        in_specs=[pl.BlockSpec(memory_space=pltpu.SMEM), vmem, vmem, vmem, vmem],
        out_specs=(vmem, vmem, vmem, vmem),
        compiler_params=pltpu.CompilerParams(vmem_limit_bytes=40 * 1024 * 1024),
        cost_estimate=pl.CostEstimate(
            flops=2 * 16 * 2 * EXT * 128 * 256, bytes_accessed=6_000_000, transcendentals=0
        ),
        name="attend",
    )(place, info, own, other, cache)


def shards(
    hidden_rows,
    cache_kv,
    sel_index,
    doc_order,
    attn_gain,
    w_query,
    w_keyval,
    w_output,
    ffn_gain,
    w_in,
    w_out,
):
    z, x, c, y = (lax.axis_index(name) for name in ("z", "x", "c", "y"))
    mine = (z * NX + x) * NC + c
    other = 1 - c

    def half(group):
        return jnp.concatenate(
            [
                lax.dynamic_slice_in_dim(w_query, group * 1024, 1024, 1),
                lax.dynamic_slice_in_dim(w_keyval[:, 0], group * 128, 128, 1),
                lax.dynamic_slice_in_dim(w_keyval[:, 1], group * 128, 128, 1),
            ],
            axis=1,
        )

    message = jnp.concatenate(
        [hidden_rows, jnp.broadcast_to(attn_gain[None, :], (16, 128))], axis=0
    )
    theirs = exchange_cores(message)
    weight_theirs = exchange_cores(half(other))
    weight = jnp.concatenate([half(c), weight_theirs], axis=0)
    inputs = jnp.concatenate([hidden_rows, theirs[:ROWS]], axis=1).astype(F32)
    gain = jnp.concatenate([attn_gain, theirs[ROWS]], axis=0).astype(F32)
    squares = jnp.sum(inputs * inputs, axis=1)
    scaled = (inputs * gain[None, :]).astype(BF)
    partial = lax.dot_general(
        weight, scaled, (((0,), (1,)), ((), ())), preferred_element_type=F32
    )
    square_parts = jnp.stack(parts_of(squares) + [jnp.zeros((ROWS,), BF)] * 5)
    payload = jnp.concatenate(
        [
            partial.astype(BF).reshape(32, 40, ROWS),
            jnp.broadcast_to(square_parts[None], (32, 8, ROWS)),
        ],
        axis=1,
    )
    arrived = swap_zx(payload).astype(F32)
    total = jnp.sum(arrived, axis=0)
    square_sum = total[40] + (total[41] + total[42])
    factor = lax.rsqrt(square_sum / D + EPS)
    piece = (total[:40] * factor[None, :]).astype(BF)
    own = swap_zx(jnp.broadcast_to(piece[None], (32, 40, ROWS))).reshape(1280, ROWS)
    others = exchange_cores(own)

    reordered = cache_kv.reshape(POOL, 8, 512).at[doc_order].get(mode="promise_in_bounds")
    slot_cache = lax.all_to_all(
        reordered, ("z", "x", "c"), split_axis=0, concat_axis=0, tiled=True
    ).reshape(DOC_LEN, 512)

    info = positions(sel_index, doc_order, mine)
    place = jnp.stack([c, mine]).astype(jnp.int32)
    joined, acc_own, acc_sent, stats = attend(place, info, own, others, slot_cache)

    acc_theirs = exchange_cores(acc_sent)
    stat_theirs = exchange_cores(stats[1])
    top = jnp.maximum(stats[0, 0], stat_theirs[0])
    mine_by = jnp.exp(stats[0, 0] - top)
    theirs_by = jnp.exp(stat_theirs[0] - top)
    totals = stats[0, 1] * mine_by + stat_theirs[1] * theirs_by
    merged = (
        acc_own.reshape(8, 128, ROWS) * mine_by[:, None, :]
        + acc_theirs.reshape(8, 128, ROWS).astype(F32) * theirs_by[:, None, :]
    ).astype(BF)
    stat_rows = jnp.stack(parts_of(top) + parts_of(totals) + [jnp.zeros((8, ROWS), BF)] * 2, axis=1)
    payload = jnp.concatenate(
        [
            merged.reshape(32, 32, ROWS),
            jnp.broadcast_to(stat_rows[:, None], (8, 4, 8, ROWS)).reshape(32, 8, ROWS),
        ],
        axis=1,
    )
    arrived = swap_zx(payload).astype(F32)
    tops = arrived[:, 32] + (arrived[:, 33] + arrived[:, 34])
    sums = arrived[:, 35] + (arrived[:, 36] + arrived[:, 37])
    by = jnp.exp(tops - jnp.max(tops, axis=0, keepdims=True))
    norm = jnp.sum(sums * by, axis=0)
    summed = jnp.sum(arrived[:, :32] * by[:, None, :], axis=0)
    piece = (summed / norm[None, :]).astype(BF)
    attended = swap_zx(jnp.broadcast_to(piece[None], (32, 32, ROWS))).reshape(1024, ROWS)
    attended_theirs = exchange_cores(attended)

    tn = (((0,), (0,)), ((), ()))
    out_own = lax.dynamic_slice_in_dim(w_output, c * 1024, 1024, 0)
    out_theirs = lax.dynamic_slice_in_dim(w_output, other * 1024, 1024, 0)
    projected = lax.dot_general(attended, out_own, tn, preferred_element_type=F32)
    projected = projected + lax.dot_general(
        attended_theirs, out_theirs, tn, preferred_element_type=F32
    )
    chunks = projected.astype(BF).reshape(4, 64, 128)
    early = jnp.concatenate(
        [
            lax.dynamic_slice_in_dim(hidden_rows, y * 64, 64, 0),
            jnp.broadcast_to(ffn_gain[None, :], (16, 128)),
        ],
        axis=0,
    )
    early = permute_xy(early, lambda a, b: (b, a))
    mid = early[:64].astype(F32)
    for step in range(4):
        sent = lax.dynamic_index_in_dim(chunks, (y + step) % NY, 0, keepdims=False)
        mid = mid + permute_xy(sent, lambda a, b: (b + step, a)).astype(F32)
    feature = (mid * early[64].astype(F32)[None, :]).astype(BF)
    square_parts = jnp.stack(parts_of(jnp.sum(mid * mid, axis=1)) + [jnp.zeros((64,), BF)] * 5)
    payload = jnp.concatenate([feature, jnp.pad(square_parts, ((0, 0), (0, 64)))], axis=0)
    arrived = swap_zx(jnp.broadcast_to(payload[None], (32, 72, 128)))
    arrived_theirs = exchange_cores(arrived)

    flat_in = jnp.transpose(w_in, (1, 2, 0)).reshape(224, D)

    def columns(array, step):
        start = ((y + step) % NY) * 256
        return jnp.concatenate(
            [
                lax.dynamic_slice_in_dim(array, k * 1024 + start + core * 128, 128, 1)
                for core in (c, other)
                for k in range(NZ)
            ],
            axis=1,
        )

    ins = [columns(flat_in, 0)]
    outs = [columns(w_out, 0)]
    for step in range(1, 4):
        ins.append(shift_y(columns(flat_in, step), step))
    for step in range(1, 4):
        outs.append(shift_y(columns(w_out, step), step))

    def features_of(block):
        return jnp.transpose(block[:, :64].reshape(NZ, ROWS, 128), (1, 0, 2)).reshape(ROWS, 1024)

    def squares_of(block):
        parts = jnp.sum(block[:, 64:67, :64].astype(F32), axis=1)
        return jnp.sum(parts.reshape(NZ, ROWS), axis=0)

    nt = (((1,), (1,)), ((), ()))
    feature_own = features_of(arrived)
    feature_theirs = features_of(arrived_theirs)
    square_sum = squares_of(arrived) + squares_of(arrived_theirs)
    square_rows = jnp.stack(parts_of(square_sum) + [jnp.zeros((ROWS,), BF)] * 5)
    hidden = []
    for step in range(4):
        term = lax.dot_general(
            ins[step][:, :1024], feature_own, nt, preferred_element_type=F32
        ) + lax.dot_general(
            ins[step][:, 1024:], feature_theirs, nt, preferred_element_type=F32
        )
        hidden.append(term)
    both = hidden[0]
    for step in range(1, 4):
        sent = jnp.concatenate([hidden[step].astype(BF), square_rows], axis=0)
        got = shift_y(sent, -step).astype(F32)
        both = both + got[:224]
        square_sum = square_sum + (got[224] + (got[225] + got[226]))
    both = both * lax.rsqrt(square_sum / D + EPS)[None, :]
    act = (jax.nn.silu(both[:112]) * both[112:]).astype(BF)
    acts = [act] + [shift_y(act, step) for step in range(1, 4)]
    act_all = jnp.concatenate(acts, axis=0)
    out_all = jnp.concatenate(outs, axis=0)
    term_theirs = lax.dot_general(act_all, out_all[:, 1024:], tn, preferred_element_type=F32)
    got = exchange_cores(term_theirs.astype(BF))
    term = lax.dot_general(act_all, out_all[:, :1024], tn, preferred_element_type=F32)
    term = (term + got.astype(F32)).astype(BF)
    payload = jnp.transpose(term.reshape(ROWS, NZ, 128), (1, 0, 2)).reshape(32, 64, 128)
    down = jnp.sum(swap_zx(payload).astype(F32), axis=0)
    result = permute_xy((mid + down).astype(BF), lambda a, b: (b, a))
    return (result, joined.reshape(DOC_LEN, 2, 256))


def solution(mesh):
    split = Mesh(mesh.devices.reshape(NZ, NX, NC, NY), ("z", "x", "c", "y"))
    pool = ("z", "x", "c")
    return jax.shard_map(
        shards,
        mesh=split,
        in_specs=(
            P(None, pool),
            P(None, pool, None, "y"),
            P(),
            P(),
            P(pool),
            P(pool, "y"),
            P(pool, None, "y"),
            P("y", pool),
            P(pool),
            P(None, None, ("z", "x", "c", "y")),
            P(("z", "x", "c", "y"), None),
        ),
        out_specs=(P("y", pool), P(pool, None, "y")),
        check_vma=False,
    )
```

time: 1470 us -> 285 us (0.19)
  blocking collectives: 1050 us -> 61.1 us
  waiting for transfers between devices: 340 us -> 67.3 us
  starting transfers between devices: 12.2 us -> 71.3 us
  local copies, waits for them, and re-layouts: 13.7 us -> 52.2 us
  matrix products: 28.8 us -> 13.5 us
    psum x3 -> x0, blocking collectives: 483 us -> none  [the longest x1 246 us: shards(): total_m, acc_m = lax.psum((total_all * factor, scaled), 'pool')]
    unnamed x1 -> x0, blocking collectives: 273 us -> none
    pmax x1 -> x0, blocking collectives: 240 us -> none  [shards(): top_m = lax.pmax(top_all, 'pool')]
    reduce_scatter x2 -> x0, waiting for transfers between devices: 171 us -> none  [the longest x1 150 us: shards(): by_cols = lax.psum_scatter(term, 'pool', scatter_dimension=1, tiled=True)]
    all_gather x2 -> x0, waiting for transfers between devices: 115 us -> none  [the longest x1 82.2 us: shards(): lax.all_gather(ffn_in, 'pool', axis=1, tiled=True)]
    all_to_all x0 -> x2, blocking collectives: none -> 61.1 us  [swap_zx(): return lax.all_to_all(value, ('z', 'x'), 0, 0, tiled=True)]
    psum x2 -> x0, waiting for transfers between devices: 53.7 us -> none  [the longest x1 53.7 us: shards(): lax.psum(projected.astype(jnp.bfloat16), 'head').astype(jnp.float32)]
    all_gather x1 -> x0, blocking collectives: 52 us -> none  [shards(): lax.all_gather(sel_mine, 'pool', axis=0, tiled=True)]
  transfers between devices with their start and end apart: 7 -> 31, of which waited for: 5 -> 13; matrix products, arithmetic and copies ran while one was open for 1% -> 22% of each run, Pallas kernels for 0% -> 0%
where the time goes in v1:
time: 285 us; the launch traced here: 282 us
  starting transfers between devices  71.3 us (25%)
  waiting for transfers between devices  67.3 us (24%)
  blocking collectives  61.1 us (21%)
  local copies, waits for them, and re-layouts  52.2 us (18%)
  matrix products  13.5 us (5%)
  Pallas kernels  9.17 us (3%)
  other arithmetic  5.79 us (2%)
    all_to_all x2, blocking collectives, swap_zx(): return lax.all_to_all(value, ('z', 'x'), 0, 0, tiled=True)  61.1 us
    unnamed x58, local copies, waits for them, and re-layouts  37.7 us
    all_to_all x4, waiting for transfers between devices, swap_zx(): return lax.all_to_all(value, ('z', 'x'), 0, 0, tiled=True)  32.8 us
    all_to_all x4, starting transfers between devices, swap_zx(): return lax.all_to_all(value, ('z', 'x'), 0, 0, tiled=True)  29 us
    ppermute x12, starting transfers between devices, shift_y(): return lax.ppermute(value, 'y', [(i, (i + step) % NY) for i in range(NY)])  17.7 us
    ppermute x6, starting transfers between devices, permute_xy(): return lax.ppermute(value, ('x', 'y'), pairs)  17.1 us
    all_to_all x1, waiting for transfers between devices, shards(): lax.all_to_all(reordered, ('z', 'x', 'c'), split_axis=0, concat_axis=0, t...  16.3 us
    pallas_call x1, Pallas kernels, attend(): pl.pallas_call(attend_kernel, out_shape=(jax.ShapeDtypeStruct((DOC_LEN, 5...  9.17 us
  transfers between devices with their start and end apart: 31, of which 13 were waited for; matrix products, arithmetic and copies ran while one was open for 22% of the time, Pallas kernels for 0%

profile of v1, /device:TPU:4, one launch (start us, length us, event | category | flops | bytes accessed | tf_op | source)
XLA Modules:
  0.0 282.4 jit_solution(16519033208548817150)
XLA Ops:
  7.2 34.4 %all_to_all.35 = bf16[32,48,256]{2,1,0:T(8,128)(2,1)S(1)} all-to-all(bf16[32,48,256]{2,1,0:T(8,128)(2,1)S(1)} %pad_maximum_fusion.1), channel_id=1, replica_groups=mesh['z'=8,'x'=4,'c'=2,'y'=4] {'z','x'}, dimensions={0} | all-to-all | bytes 1572864 | tf_op jit(solution)/shard_map/all_to_all | solution.py:45
  42.7 5.7 %all-to-all-start.1 = ((bf16[32,40,256]{2,1,0:T(8,128)(2,1)}), bf16[32,40,256]{2,1,0:T(8,128)(2,1)S(1)}, u32[]{:S(2)}, u32[]{:S(2)}) async-start(bf16[32,40,256]{2,1,0:T(8,128)(2,1)} %broadcast_in_dim.62), calls=%async_computation.1 | async-start | bytes 1310720 | tf_op jit(solution)/shard_map/all_to_all | solution.py:45
  50.2 17.0 %all-to-all-done.1 = bf16[32,40,256]{2,1,0:T(8,128)(2,1)S(1)} async-done(((bf16[32,40,256]{2,1,0:T(8,128)(2,1)}), bf16[32,40,256]{2,1,0:T(8,128)(2,1)S(1)}, u32[]{:S(2)}, u32[]{:S(2)}) %all-to-all-start.1) | async-done | bytes 655392 | tf_op jit(solution)/shard_map/all_to_all | solution.py:45
  67.2 6.0 %all-to-all-start.2 = ((bf16[64,8,512]{2,1,0:T(8,128)(2,1)}), bf16[64,8,512]{2,1,0:T(8,128)(2,1)S(1)}, u32[]{:S(2)}, u32[]{:S(2)}) async-start(bf16[64,8,512]{2,1,0:T(8,128)(2,1)} %gather_fusion), calls=%async_computation.2 | async-start | bytes 1048576 | tf_op jit(solution)/shard_map/all_to_all | solution.py:200
  74.5 16.3 %all-to-all-done.2 = bf16[64,8,512]{2,1,0:T(8,128)(2,1)S(1)} async-done(((bf16[64,8,512]{2,1,0:T(8,128)(2,1)}), bf16[64,8,512]{2,1,0:T(8,128)(2,1)S(1)}, u32[]{:S(2)}, u32[]{:S(2)}) %all-to-all-start.2) | async-done | bytes 524320 | tf_op jit(solution)/shard_map/all_to_all | solution.py:200
  92.7 9.2 %attend.1 = (bf16[512,512]{1,0:T(8,128)(2,1)S(1)}, f32[1024,256]{1,0:T(8,128)S(1)}, bf16[1024,256]{1,0:T(8,128)(2,1)}, f32[2,2,8,256]{3,2,1,0:T(8,128)S(1)}) custom-call(s32[2]{0:T(128)S(1)} %pad_add_fusion.2.place_ref, s32[8,256]{1,0:T(8,128)S(1)} %add_add_fusion.info_ref, bf16[1280,256]{1,0:T(8,128)(2,1)S(1)} %bitcast.150, ...), custom_call_target="tpu_custom_call" | custom-call | flops 1107296256 | bytes 6000000 | tf_op jit(solution)/shard_map/attend/pallas_call | solution.py:125
  105.3 5.5 %all-to-all-start.3 = ((bf16[32,40,256]{2,1,0:T(8,128)(2,1)}), bf16[32,40,256]{2,1,0:T(8,128)(2,1)S(1)}, u32[]{:S(2)}, u32[]{:S(2)}) async-start(bf16[32,40,256]{2,1,0:T(8,128)(2,1)} %pad_maximum_fusion.2), calls=%async_computation.3 | async-start | bytes 1310720 | tf_op jit(solution)/shard_map/all_to_all | solution.py:45
  124.1 1.7 constant_dynamic-update-slice_fusion.23
  125.8 5.2 %all-to-all-done.3 = bf16[32,40,256]{2,1,0:T(8,128)(2,1)S(1)} async-done(((bf16[32,40,256]{2,1,0:T(8,128)(2,1)}), bf16[32,40,256]{2,1,0:T(8,128)(2,1)S(1)}, u32[]{:S(2)}, u32[]{:S(2)}) %all-to-all-start.3) | async-done | bytes 655392 | tf_op jit(solution)/shard_map/all_to_all | solution.py:45
  132.3 5.6 %all-to-all-start.4 = ((bf16[32,32,256]{2,1,0:T(8,128)(2,1)}), bf16[32,32,256]{2,1,0:T(8,128)(2,1)S(1)}, u32[]{:S(2)}, u32[]{:S(2)}) async-start(bf16[32,32,256]{2,1,0:T(8,128)(2,1)} %broadcast_in_dim.65), calls=%async_computation.4 | async-start | bytes 1048576 | tf_op jit(solution)/shard_map/all_to_all | solution.py:45
  137.9 1.7 constant_dynamic-update-slice_fusion.22
  139.6 1.8 constant_dynamic-update-slice_fusion.21
  143.1 1.7 constant_dynamic-update-slice_fusion.19
  144.8 1.7 constant_dynamic-update-slice_fusion.18
  146.5 1.7 constant_dynamic-update-slice_fusion.17
  148.2 1.7 constant_dynamic-update-slice_fusion.16
  151.5 4.5 %collective-permute-start = (bf16[80,128]{1,0:T(8,128)(2,1)S(1)}, bf16[80,128]{1,0:T(8,128)(2,1)S(1)}, u32[]{:S(2)}, u32[]{:S(2)}) collective-permute-start(bf16[80,128]{1,0:T(8,128)(2,1)S(1)} %pad_maximum_fusion.10), channel_id=1, source_target_pairs={{0,0},{1,8},{2,16},{3,24},{8,1},{9,9},{10,17},{11,25},{16,2},{17,1... | collective-permute-start | bytes 61448 | tf_op jit(solution)/shard_map/ppermute | solution.py:41
  159.8 1.8 collective-permute-start.10
  161.6 3.5 %collective-permute-start.7 = (bf16[64,128]{1,0:T(8,128)(2,1)S(1)}, bf16[64,128]{1,0:T(8,128)(2,1)S(1)}, u32[]{:S(2)}, u32[]{:S(2)}) collective-permute-start(bf16[64,128]{1,0:T(8,128)(2,1)S(1)} %get-tuple-element.153), channel_id=1, source_target_pairs={{0,0},{1,8},{2,16},{3,24},{8,1},{9,9},{10,17},{11,25},{16,2},{17,1... | collective-permute-start | bytes 49160 | tf_op jit(solution)/shard_map/ppermute | solution.py:41
  165.2 3.0 %collective-permute-start.8 = (bf16[64,128]{1,0:T(8,128)(2,1)S(1)}, bf16[64,128]{1,0:T(8,128)(2,1)S(1)}, u32[]{:S(2)}, u32[]{:S(2)}) collective-permute-start(bf16[64,128]{1,0:T(8,128)(2,1)S(1)} %get-tuple-element.156), channel_id=1, source_target_pairs={{0,8},{1,16},{2,24},{3,0},{8,9},{9,17},{10,25},{11,1},{16,10},{17,... | collective-permute-start | bytes 49160 | tf_op jit(solution)/shard_map/ppermute | solution.py:41
  168.6 5.1 %collective-permute-start.14 = (bf16[224,2048]{1,0:T(8,128)(2,1)}, bf16[224,2048]{1,0:T(8,128)(2,1)}, u32[]{:S(2)}, u32[]{:S(2)}) collective-permute-start(bf16[224,2048]{1,0:T(8,128)(2,1)} %get-tuple-element.18), channel_id=1, source_target_pairs={{0,2},{1,3},{2,0},{3,1},{4,6},{5,7},{6,4},{7,5},{8,10},{9,11},{10,... | collective-permute-start | bytes 2752520 | tf_op jit(solution)/shard_map/ppermute | solution.py:32
  174.9 12.3 %all-to-all-start.5 = ((bf16[32,72,128]{2,1,0:T(8,128)(2,1)}), bf16[32,72,128]{2,1,0:T(8,128)(2,1)S(1)}, u32[]{:S(2)}, u32[]{:S(2)}) async-start(bf16[32,72,128]{2,1,0:T(8,128)(2,1)} %broadcast_in_dim.66), calls=%async_computation.5 | async-start | bytes 1179648 | tf_op jit(solution)/shard_map/all_to_all | solution.py:45
  193.7 10.5 %all-to-all-done.5 = bf16[32,72,128]{2,1,0:T(8,128)(2,1)S(1)} async-done(((bf16[32,72,128]{2,1,0:T(8,128)(2,1)}), bf16[32,72,128]{2,1,0:T(8,128)(2,1)S(1)}, u32[]{:S(2)}, u32[]{:S(2)}) %all-to-all-start.5) | async-done | bytes 589856 | tf_op jit(solution)/shard_map/all_to_all | solution.py:45
  208.0 1.9 collective-permute-start.21
  224.1 1.7 collective-permute-done.13
  225.8 2.3 collective-permute-start.22
  230.9 3.2 %collective-permute-start.19 = (bf16[112,256]{1,0:T(8,128)(2,1)S(1)}, bf16[112,256]{1,0:T(8,128)(2,1)S(1)}, u32[]{:S(2)}, u32[]{:S(2)}) collective-permute-start(bf16[112,256]{1,0:T(8,128)(2,1)S(1)} %fusion.38), channel_id=1, source_target_pairs={{0,2},{1,3},{2,0},{3,1},{4,6},{5,7},{6,4},{7,5},{8,10},{9,11},{10,... | collective-permute-start | bytes 172040 | tf_op jit(solution)/shard_map/ppermute | solution.py:32
  234.4 6.3 %collective-permute-done.22 = bf16[112,2048]{1,0:T(8,128)(2,1)S(1)} collective-permute-done((bf16[112,2048]{1,0:T(8,128)(2,1)}, bf16[112,2048]{1,0:T(8,128)(2,1)S(1)}, u32[]{:S(2)}, u32[]{:S(2)}) %collective-permute-start.22) | collective-permute-done | bytes 458784 | tf_op jit(solution)/shard_map/ppermute | solution.py:32
  242.9 1.9 collective-permute-done.24
  245.4 26.8 %all_to_all.36 = bf16[32,64,128]{2,1,0:T(8,128)(2,1)S(1)} all-to-all(bf16[32,64,128]{2,1,0:T(8,128)(2,1)S(1)} %bitcast.178), channel_id=1, replica_groups=mesh['z'=8,'x'=4,'c'=2,'y'=4] {'z','x'}, dimensions={0} | all-to-all | bytes 1048576 | tf_op jit(solution)/shard_map/all_to_all | solution.py:45
  272.3 3.8 %collective-permute-start.25 = (bf16[64,128]{1,0:T(8,128)(2,1)S(1)}, bf16[64,128]{1,0:T(8,128)(2,1)S(1)}, u32[]{:S(2)}, u32[]{:S(2)}) collective-permute-start(bf16[64,128]{1,0:T(8,128)(2,1)S(1)} %add_convert_fusion), channel_id=1, source_target_pairs={{0,0},{1,8},{2,16},{3,24},{8,1},{9,9},{10,17},{11,25},{16,2},{17,1... | collective-permute-start | bytes 49160 | tf_op jit(solution)/shard_map/ppermute | solution.py:41
  277.0 4.8 %collective-permute-done.25 = bf16[64,128]{1,0:T(8,128)(2,1)S(1)} collective-permute-done((bf16[64,128]{1,0:T(8,128)(2,1)S(1)}, bf16[64,128]{1,0:T(8,128)(2,1)S(1)}, u32[]{:S(2)}, u32[]{:S(2)}) %collective-permute-start.25) | collective-permute-done | bytes 16416 | tf_op jit(solution)/shard_map/ppermute | solution.py:41
  (212 shorter events, 70.2 us)
Async XLA Ops:
  0.6 157.4 %copy-start = (bf16[2048,128]{1,0:T(8,128)(2,1)S(1)}, bf16[2048,128]{1,0:T(8,128)(2,1)}, u32[]{:S(2)}) copy-start(bf16[2048,128]{1,0:T(8,128)(2,1)} %param.18) | copy-start | bytes 1572868
  2.3 3.3 %collective-permute-start.2 = (bf16[272,128]{1,0:T(8,128)(2,1)S(1)}, bf16[272,128]{1,0:T(8,128)(2,1)S(1)}, u32[]{:S(2)}, u32[]{:S(2)}) collective-permute-start(bf16[272,128]{1,0:T(8,128)(2,1)S(1)} %pad_maximum_fusion.7), channel_id=1, source_target_pairs={{0,4},{4,0},{1,5},{5,1},{2,6},{6,2},{3,7},{7,3},{8,12},{12,8},{9,1... | collective-permute-start | bytes 208904 | tf_op jit(solution)/shard_map/ppermute | solution.py:28
  4.9 1.9 collective-permute-start.1
  42.7 24.5 %all-to-all-start.1 = ((bf16[32,40,256]{2,1,0:T(8,128)(2,1)}), bf16[32,40,256]{2,1,0:T(8,128)(2,1)S(1)}, u32[]{:S(2)}, u32[]{:S(2)}) async-start(bf16[32,40,256]{2,1,0:T(8,128)(2,1)} %broadcast_in_dim.62), calls=%async_computation.1 | async-start | bytes 1310720 | tf_op jit(solution)/shard_map/all_to_all | solution.py:45
  67.2 23.5 %all-to-all-start.2 = ((bf16[64,8,512]{2,1,0:T(8,128)(2,1)}), bf16[64,8,512]{2,1,0:T(8,128)(2,1)S(1)}, u32[]{:S(2)}, u32[]{:S(2)}) async-start(bf16[64,8,512]{2,1,0:T(8,128)(2,1)} %gather_fusion), calls=%async_computation.2 | async-start | bytes 1048576 | tf_op jit(solution)/shard_map/all_to_all | solution.py:200
  73.7 17.1 %collective-permute-start.3 = (bf16[1280,256]{1,0:T(8,128)(2,1)S(1)}, bf16[1280,256]{1,0:T(8,128)(2,1)S(1)}, u32[]{:S(2)}, u32[]{:S(2)}) collective-permute-start(bf16[1280,256]{1,0:T(8,128)(2,1)S(1)} %bitcast.149), channel_id=1, source_target_pairs={{0,4},{4,0},{1,5},{5,1},{2,6},{6,2},{3,7},{7,3},{8,12},{12,8},{9,1... | collective-permute-start | bytes 1966088 | tf_op jit(solution)/shard_map/ppermute | solution.py:28
  101.9 1.2 collective-permute-start.4
  101.9 2.3 collective-permute-start.5
  105.3 25.6 %all-to-all-start.3 = ((bf16[32,40,256]{2,1,0:T(8,128)(2,1)}), bf16[32,40,256]{2,1,0:T(8,128)(2,1)S(1)}, u32[]{:S(2)}, u32[]{:S(2)}) async-start(bf16[32,40,256]{2,1,0:T(8,128)(2,1)} %pad_maximum_fusion.2), calls=%async_computation.3 | async-start | bytes 1310720 | tf_op jit(solution)/shard_map/all_to_all | solution.py:45
  132.3 23.6 %all-to-all-start.4 = ((bf16[32,32,256]{2,1,0:T(8,128)(2,1)}), bf16[32,32,256]{2,1,0:T(8,128)(2,1)S(1)}, u32[]{:S(2)}, u32[]{:S(2)}) async-start(bf16[32,32,256]{2,1,0:T(8,128)(2,1)} %broadcast_in_dim.65), calls=%async_computation.4 | async-start | bytes 1048576 | tf_op jit(solution)/shard_map/all_to_all | solution.py:45
  149.9 62.4 %collective-permute-start.12 = (bf16[224,2048]{1,0:T(8,128)(2,1)}, bf16[224,2048]{1,0:T(8,128)(2,1)}, u32[]{:S(2)}, u32[]{:S(2)}) collective-permute-start(bf16[224,2048]{1,0:T(8,128)(2,1)} %get-tuple-element.16), channel_id=1, source_target_pairs={{0,1},{1,2},{2,3},{3,0},{4,5},{5,6},{6,7},{7,4},{8,9},{9,10},{10,1... | collective-permute-start | bytes 2752520 | tf_op jit(solution)/shard_map/ppermute | solution.py:32
  151.5 16.7 %collective-permute-start = (bf16[80,128]{1,0:T(8,128)(2,1)S(1)}, bf16[80,128]{1,0:T(8,128)(2,1)S(1)}, u32[]{:S(2)}, u32[]{:S(2)}) collective-permute-start(bf16[80,128]{1,0:T(8,128)(2,1)S(1)} %pad_maximum_fusion.10), channel_id=1, source_target_pairs={{0,0},{1,8},{2,16},{3,24},{8,1},{9,9},{10,17},{11,25},{16,2},{17,1... | collective-permute-start | bytes 61448 | tf_op jit(solution)/shard_map/ppermute | solution.py:41
  156.0 2.4 collective-permute-start.6
  159.8 8.8 %collective-permute-start.10 = (bf16[64,128]{1,0:T(8,128)(2,1)S(1)}, bf16[64,128]{1,0:T(8,128)(2,1)S(1)}, u32[]{:S(2)}, u32[]{:S(2)}) collective-permute-start(bf16[64,128]{1,0:T(8,128)(2,1)S(1)} %get-tuple-element.154), channel_id=1, source_target_pairs={{0,24},{1,0},{2,8},{3,16},{8,25},{9,1},{10,9},{11,17},{16,26},{17,... | collective-permute-start | bytes 49160 | tf_op jit(solution)/shard_map/ppermute | solution.py:41
  161.6 12.1 %collective-permute-start.7 = (bf16[64,128]{1,0:T(8,128)(2,1)S(1)}, bf16[64,128]{1,0:T(8,128)(2,1)S(1)}, u32[]{:S(2)}, u32[]{:S(2)}) collective-permute-start(bf16[64,128]{1,0:T(8,128)(2,1)S(1)} %get-tuple-element.153), channel_id=1, source_target_pairs={{0,0},{1,8},{2,16},{3,24},{8,1},{9,9},{10,17},{11,25},{16,2},{17,1... | collective-permute-start | bytes 49160 | tf_op jit(solution)/shard_map/ppermute | solution.py:41
  165.2 8.6 %collective-permute-start.8 = (bf16[64,128]{1,0:T(8,128)(2,1)S(1)}, bf16[64,128]{1,0:T(8,128)(2,1)S(1)}, u32[]{:S(2)}, u32[]{:S(2)}) collective-permute-start(bf16[64,128]{1,0:T(8,128)(2,1)S(1)} %get-tuple-element.156), channel_id=1, source_target_pairs={{0,8},{1,16},{2,24},{3,0},{8,9},{9,17},{10,25},{11,1},{16,10},{17,... | collective-permute-start | bytes 49160 | tf_op jit(solution)/shard_map/ppermute | solution.py:41
  168.1 5.6 %collective-permute-start.9 = (bf16[64,128]{1,0:T(8,128)(2,1)S(1)}, bf16[64,128]{1,0:T(8,128)(2,1)S(1)}, u32[]{:S(2)}, u32[]{:S(2)}) collective-permute-start(bf16[64,128]{1,0:T(8,128)(2,1)S(1)} %get-tuple-element.155), channel_id=1, source_target_pairs={{0,16},{1,24},{2,0},{3,8},{8,17},{9,25},{10,1},{11,9},{16,18},{17,... | collective-permute-start | bytes 49160 | tf_op jit(solution)/shard_map/ppermute | solution.py:41
  168.6 47.8 %collective-permute-start.14 = (bf16[224,2048]{1,0:T(8,128)(2,1)}, bf16[224,2048]{1,0:T(8,128)(2,1)}, u32[]{:S(2)}, u32[]{:S(2)}) collective-permute-start(bf16[224,2048]{1,0:T(8,128)(2,1)} %get-tuple-element.18), channel_id=1, source_target_pairs={{0,2},{1,3},{2,0},{3,1},{4,6},{5,7},{6,4},{7,5},{8,10},{9,11},{10,... | collective-permute-start | bytes 2752520 | tf_op jit(solution)/shard_map/ppermute | solution.py:32
  173.7 46.2 %collective-permute-start.16 = (bf16[224,2048]{1,0:T(8,128)(2,1)}, bf16[224,2048]{1,0:T(8,128)(2,1)}, u32[]{:S(2)}, u32[]{:S(2)}) collective-permute-start(bf16[224,2048]{1,0:T(8,128)(2,1)} %get-tuple-element.17), channel_id=1, source_target_pairs={{0,3},{1,0},{2,1},{3,2},{4,7},{5,4},{6,5},{7,6},{8,11},{9,8},{10,9... | collective-permute-start | bytes 2752520 | tf_op jit(solution)/shard_map/ppermute | solution.py:32
  174.9 29.3 %all-to-all-start.5 = ((bf16[32,72,128]{2,1,0:T(8,128)(2,1)}), bf16[32,72,128]{2,1,0:T(8,128)(2,1)S(1)}, u32[]{:S(2)}, u32[]{:S(2)}) async-start(bf16[32,72,128]{2,1,0:T(8,128)(2,1)} %broadcast_in_dim.66), calls=%async_computation.5 | async-start | bytes 1179648 | tf_op jit(solution)/shard_map/all_to_all | solution.py:45
  204.2 3.8 %collective-permute-start.11 = (bf16[32,72,128]{2,1,0:T(8,128)(2,1)S(1)}, bf16[32,72,128]{2,1,0:T(8,128)(2,1)}, u32[]{:S(2)}, u32[]{:S(2)}) collective-permute-start(bf16[32,72,128]{2,1,0:T(8,128)(2,1)S(1)} %all-to-all-done.5), channel_id=1, source_target_pairs={{0,4},{4,0},{1,5},{5,1},{2,6},{6,2},{3,7},{7,3},{8,12},{12,8},{9,1... | collective-permute-start | bytes 1769480 | tf_op jit(solution)/shard_map/ppermute | solution.py:28
  207.4 26.6 %collective-permute-start.23 = (bf16[112,2048]{1,0:T(8,128)(2,1)}, bf16[112,2048]{1,0:T(8,128)(2,1)}, u32[]{:S(2)}, u32[]{:S(2)}) collective-permute-start(bf16[112,2048]{1,0:T(8,128)(2,1)} %constant_dynamic-update-slice_fusion.112), channel_id=1, source_target_pairs={{0,3},{1,0},{2,1},{3,2},{4,7},{5,4},{6,5},{7,6},{8,11},{9,8},{10,9... | collective-permute-start | bytes 1376264 | tf_op jit(solution)/shard_map/ppermute | solution.py:32
  208.0 26.4 %collective-permute-start.21 = (bf16[112,2048]{1,0:T(8,128)(2,1)}, bf16[112,2048]{1,0:T(8,128)(2,1)S(1)}, u32[]{:S(2)}, u32[]{:S(2)}) collective-permute-start(bf16[112,2048]{1,0:T(8,128)(2,1)} %get-tuple-element.83), channel_id=1, source_target_pairs={{0,1},{1,2},{2,3},{3,0},{4,5},{5,6},{6,7},{7,4},{8,9},{9,10},{10,1... | collective-permute-start | bytes 1376264 | tf_op jit(solution)/shard_map/ppermute | solution.py:32
  215.0 10.8 %collective-permute-start.13 = (bf16[232,256]{1,0:T(8,128)(2,1)S(1)}, bf16[232,256]{1,0:T(8,128)(2,1)S(1)}, u32[]{:S(2)}, u32[]{:S(2)}) collective-permute-start(bf16[232,256]{1,0:T(8,128)(2,1)S(1)} %concatenate.108), channel_id=1, source_target_pairs={{0,3},{1,0},{2,1},{3,2},{4,7},{5,4},{6,5},{7,6},{8,11},{9,8},{10,9... | collective-permute-start | bytes 356360 | tf_op jit(solution)/shard_map/ppermute | solution.py:32
  219.1 9.1 %collective-permute-start.15 = (bf16[232,256]{1,0:T(8,128)(2,1)S(1)}, bf16[232,256]{1,0:T(8,128)(2,1)S(1)}, u32[]{:S(2)}, u32[]{:S(2)}) collective-permute-start(bf16[232,256]{1,0:T(8,128)(2,1)S(1)} %concatenate.110), channel_id=1, source_target_pairs={{0,2},{1,3},{2,0},{3,1},{4,6},{5,7},{6,4},{7,5},{8,10},{9,11},{10,... | collective-permute-start | bytes 356360 | tf_op jit(solution)/shard_map/ppermute | solution.py:32
  222.6 6.3 %collective-permute-start.17 = (bf16[232,256]{1,0:T(8,128)(2,1)S(1)}, bf16[232,256]{1,0:T(8,128)(2,1)S(1)}, u32[]{:S(2)}, u32[]{:S(2)}) collective-permute-start(bf16[232,256]{1,0:T(8,128)(2,1)S(1)} %concatenate.112), channel_id=1, source_target_pairs={{0,1},{1,2},{2,3},{3,0},{4,5},{5,6},{6,7},{7,4},{8,9},{9,10},{10,1... | collective-permute-start | bytes 356360 | tf_op jit(solution)/shard_map/ppermute | solution.py:32
  225.8 14.9 %collective-permute-start.22 = (bf16[112,2048]{1,0:T(8,128)(2,1)}, bf16[112,2048]{1,0:T(8,128)(2,1)S(1)}, u32[]{:S(2)}, u32[]{:S(2)}) collective-permute-start(bf16[112,2048]{1,0:T(8,128)(2,1)} %get-tuple-element.82), channel_id=1, source_target_pairs={{0,2},{1,3},{2,0},{3,1},{4,6},{5,7},{6,4},{7,5},{8,10},{9,11},{10,... | collective-permute-start | bytes 1376264 | tf_op jit(solution)/shard_map/ppermute | solution.py:32
  230.3 11.6 %collective-permute-start.18 = (bf16[112,256]{1,0:T(8,128)(2,1)S(1)}, bf16[112,256]{1,0:T(8,128)(2,1)S(1)}, u32[]{:S(2)}, u32[]{:S(2)}) collective-permute-start(bf16[112,256]{1,0:T(8,128)(2,1)S(1)} %fusion.38), channel_id=1, source_target_pairs={{0,1},{1,2},{2,3},{3,0},{4,5},{5,6},{6,7},{7,4},{8,9},{9,10},{10,1... | collective-permute-start | bytes 172040 | tf_op jit(solution)/shard_map/ppermute | solution.py:32
  230.9 11.0 %collective-permute-start.19 = (bf16[112,256]{1,0:T(8,128)(2,1)S(1)}, bf16[112,256]{1,0:T(8,128)(2,1)S(1)}, u32[]{:S(2)}, u32[]{:S(2)}) collective-permute-start(bf16[112,256]{1,0:T(8,128)(2,1)S(1)} %fusion.38), channel_id=1, source_target_pairs={{0,2},{1,3},{2,0},{3,1},{4,6},{5,7},{6,4},{7,5},{8,10},{9,11},{10,... | collective-permute-start | bytes 172040 | tf_op jit(solution)/shard_map/ppermute | solution.py:32
  234.1 8.3 %collective-permute-start.20 = (bf16[112,256]{1,0:T(8,128)(2,1)S(1)}, bf16[112,256]{1,0:T(8,128)(2,1)S(1)}, u32[]{:S(2)}, u32[]{:S(2)}) collective-permute-start(bf16[112,256]{1,0:T(8,128)(2,1)S(1)} %fusion.38), channel_id=1, source_target_pairs={{0,3},{1,0},{2,1},{3,2},{4,7},{5,4},{6,5},{7,6},{8,11},{9,8},{10,9... | collective-permute-start | bytes 172040 | tf_op jit(solution)/shard_map/ppermute | solution.py:32
  242.8 2.0 collective-permute-start.24
  272.3 9.5 %collective-permute-start.25 = (bf16[64,128]{1,0:T(8,128)(2,1)S(1)}, bf16[64,128]{1,0:T(8,128)(2,1)S(1)}, u32[]{:S(2)}, u32[]{:S(2)}) collective-permute-start(bf16[64,128]{1,0:T(8,128)(2,1)S(1)} %add_convert_fusion), channel_id=1, source_target_pairs={{0,0},{1,8},{2,16},{3,24},{8,1},{9,9},{10,17},{11,25},{16,2},{17,1... | collective-permute-start | bytes 49160 | tf_op jit(solution)/shard_map/ppermute | solution.py:41
  (10 other events, 78.2 us)

commit v2 on v1

v2 whole, which is shorter than its diff:
```python
import functools

import jax
import jax.numpy as jnp
from jax import lax
from jax.experimental import pallas as pl
from jax.experimental.pallas import tpu as pltpu
from jax.sharding import Mesh
from jax.sharding import PartitionSpec as P

D = 8192
HEAD_DIM = 128
DOC_LEN = 512
SEL_DEV = 3
EPS = 1e-05
NEG = -1e30
FLOOR = -1e29
NZ, NX, NC, NY = 8, 4, 2, 4
POOL = NZ * NX * NC
ROWS = 256

BF = jnp.bfloat16
F32 = jnp.float32


def exchange_cores(value):
    return lax.ppermute(value, "c", [(0, 1), (1, 0)])


def shift_y(value, step):
    return lax.ppermute(value, "y", [(i, (i + step) % NY) for i in range(NY)])


def permute_xy(value, target):
    pairs = []
    for x in range(NX):
        for y in range(NY):
            to_x, to_y = target(x, y)
            pairs.append((x * NY + y, (to_x % NX) * NY + to_y % NY))
    return lax.ppermute(value, ("x", "y"), pairs)


def swap_zx(value):
    return lax.all_to_all(value, ("z", "x"), 0, 0, tiled=True)


def parts_of(value):
    high = lax.reduce_precision(value, 8, 7)
    rest = value - high
    middle = lax.reduce_precision(rest, 8, 7)
    low = rest - middle
    return [high.astype(BF), middle.astype(BF), low.astype(BF)]


def shift_x(value, step):
    return lax.ppermute(value, "x", [(i, (i + step) % NX) for i in range(NX)])


def swap_z(value):
    return lax.all_to_all(value, "z", 0, 0, tiled=True)


def hold(*values):
    return lax.optimization_barrier(values)


def positions(sel_index, doc_order):
    docs = jnp.arange(POOL, dtype=jnp.int32)
    slot_of_doc = jnp.sum(jnp.where(doc_order[:, None] == docs[None, :], docs[:, None], 0), axis=0)
    sel_doc = sel_index // DOC_LEN
    sel_tok = sel_index % DOC_LEN
    sel_slot = jnp.sum(
        jnp.where(sel_doc[:, None] == docs[None, :], slot_of_doc[None, :], 0), axis=1
    )
    sel_pos = sel_slot * DOC_LEN + sel_tok
    query_pos = DOC_LEN * POOL + docs
    row_pos = jnp.concatenate(
        [sel_pos.reshape(POOL, SEL_DEV), query_pos[:, None]], axis=1
    ).reshape(ROWS)
    return slot_of_doc, row_pos


def slices_kernel(place_ref, in_ref, out_ref, *rest):
    pieces, sems = rest[:4], rest[4]
    core = place_ref[0]
    y = place_ref[1]
    for go in (True, False):
        for step in range(4):
            base = lax.rem(y + step, NY) * 256

            def body(k, carry):
                far = k // NZ
                group = jnp.where(far == 0, core, 1 - core)
                start = pl.multiple_of((k - far * NZ) * 1024 + base + group * 128, 128)
                to = pl.multiple_of(k * 128, 128)
                first = pltpu.make_async_copy(
                    in_ref.at[:, pl.ds(start, 128)],
                    pieces[step].at[0:224, pl.ds(to, 128)],
                    sems.at[step, 0, k],
                )
                second = pltpu.make_async_copy(
                    out_ref.at[:, pl.ds(start, 128)],
                    pieces[step].at[224:336, pl.ds(to, 128)],
                    sems.at[step, 1, k],
                )
                if go:
                    first.start()
                    second.start()
                else:
                    first.wait()
                    second.wait()
                return carry

            lax.fori_loop(0, 16, body, 0)


def weight_slices(place, flat_in, w_out):
    hbm = pl.BlockSpec(memory_space=pl.ANY)
    return pl.pallas_call(
        slices_kernel,
        out_shape=tuple(jax.ShapeDtypeStruct((336, 2048), BF) for _ in range(4)),
        in_specs=[pl.BlockSpec(memory_space=pltpu.SMEM), hbm, hbm],
        out_specs=tuple(hbm for _ in range(4)),
        scratch_shapes=[pltpu.SemaphoreType.DMA((4, 2, 16))],
        cost_estimate=pl.CostEstimate(flops=0, bytes_accessed=11_000_000, transcendentals=0),
        name="weight_slices",
    )(place, flat_in, w_out)


NT = (((1,), (1,)), ((), ()))
TN = (((0,), (0,)), ((), ()))


def attend_kernel(
    place_ref, bias_ref, own_ref, other_ref, c0, c1, c2, c3, acc_ref, sent_ref, stat_ref
):
    core = place_ref[0]
    blocks = (c0, c1, c2, c3)
    stat_ref[...] = jnp.zeros_like(stat_ref)
    for rel in range(2):
        query_ref = own_ref if rel == 0 else other_ref
        group = core if rel == 0 else 1 - core
        key_at = pl.ds(pl.multiple_of(group * 128, 128), 128)
        value_at = pl.ds(pl.multiple_of(256 + group * 128, 128), 128)
        for half in range(2):
            lanes = slice(half * 256, half * 256 + 256)
            query = jnp.concatenate(
                [query_ref[half * 4 + i, 0:64, :] for i in range(4)], axis=0
            )
            scores = []
            top = jnp.full((1, 256), FLOOR, F32)
            for k in range(4):
                bias = bias_ref[k * 512 : k * 512 + 512, :]
                part = lax.dot_general(
                    blocks[k][:, key_at], query, NT, preferred_element_type=F32
                ) * (HEAD_DIM**-0.5) + jnp.concatenate([bias, bias], axis=1)
                scores.append(part)
                top = jnp.maximum(top, jnp.max(part, axis=0, keepdims=True))
            total = jnp.zeros((1, 256), F32)
            acc = jnp.zeros((128, 256), F32)
            for k in range(4):
                probs = jnp.exp(scores[k] - top)
                total = total + jnp.sum(probs, axis=0, keepdims=True)
                acc = acc + lax.dot_general(
                    blocks[k][:, value_at], probs.astype(BF), TN, preferred_element_type=F32
                )
            if rel == 0:
                acc_ref[:, lanes] = acc
            else:
                sent_ref[:, lanes] = acc.astype(BF)
            stat_ref[2 * rel : 2 * rel + 1, lanes] = top
            stat_ref[2 * rel + 1 : 2 * rel + 2, lanes] = total


def attend(place, bias, own, other, blocks):
    vmem = pl.BlockSpec(memory_space=pltpu.VMEM)
    return pl.pallas_call(
        attend_kernel,
        out_shape=(
            jax.ShapeDtypeStruct((128, 512), F32),
            jax.ShapeDtypeStruct((128, 512), BF),
            jax.ShapeDtypeStruct((8, 512), F32),
        ),
        in_specs=[pl.BlockSpec(memory_space=pltpu.SMEM)] + [vmem] * 7,
        out_specs=(vmem, vmem, vmem),
        compiler_params=pltpu.CompilerParams(vmem_limit_bytes=40 * 1024 * 1024),
        cost_estimate=pl.CostEstimate(
            flops=2 * 16 * 2 * 2048 * 128 * 64, bytes_accessed=6_000_000, transcendentals=2097152
        ),
        name="attend",
    )(place, bias, own, other, *blocks)


def merge_kernel(
    acc_ref, stat_ref, far_acc_ref, far_stat_ref, own_ref, key_ref, value_ref, bias_ref, out_ref
):
    query = jnp.concatenate([own_ref[i, 0:64, :] for i in range(8)], axis=0)
    bias = bias_ref[...]
    scores = lax.dot_general(key_ref[...], query, NT, preferred_element_type=F32) * (
        HEAD_DIM**-0.5
    ) + jnp.concatenate([bias] * 4, axis=1)
    near_top = stat_ref[0:1, :]
    far_top = far_stat_ref[2:3, :]
    top = jnp.maximum(jnp.maximum(near_top, far_top), jnp.max(scores, axis=0, keepdims=True))
    near = jnp.exp(near_top - top)
    far = jnp.exp(far_top - top)
    probs = jnp.exp(scores - top)
    total = (
        stat_ref[1:2, :] * near
        + far_stat_ref[3:4, :] * far
        + jnp.sum(probs, axis=0, keepdims=True)
    )
    acc = (
        acc_ref[...] * near
        + far_acc_ref[...].astype(F32) * far
        + lax.dot_general(value_ref[...], probs.astype(BF), TN, preferred_element_type=F32)
    )
    rows = acc.T.astype(BF)
    tops = []
    for value in (top, total):
        high = value.astype(BF)
        rest = value - high.astype(F32)
        middle = rest.astype(BF)
        low = (rest - middle.astype(F32)).astype(BF)
        tops += [high.astype(F32), middle.astype(F32), low.astype(F32)]
    stats = jnp.concatenate(tops + [jnp.zeros((10, 512), F32)], axis=0).astype(BF)
    for head in range(8):
        pair = head // 2
        out_ref[head, 0:64, :] = rows[head * 64 : head * 64 + 64, :]
        out_ref[head, 64:80, :] = stats[:, pair * 128 : pair * 128 + 128]


def merge(*operands):
    vmem = pl.BlockSpec(memory_space=pltpu.VMEM)
    return pl.pallas_call(
        merge_kernel,
        out_shape=jax.ShapeDtypeStruct((8, 80, 128), BF),
        in_specs=[vmem] * 8,
        out_specs=vmem,
        cost_estimate=pl.CostEstimate(
            flops=4 * 512 * 128 * 32, bytes_accessed=1_000_000, transcendentals=20000
        ),
        name="merge",
    )(*operands)


def shards(
    hidden_rows,
    cache_kv,
    sel_index,
    doc_order,
    attn_gain,
    w_query,
    w_keyval,
    w_output,
    ffn_gain,
    w_in,
    w_out,
):
    z, x, c, y = (lax.axis_index(name) for name in ("z", "x", "c", "y"))
    mine = (z * NX + x) * NC + c
    other = 1 - c

    def half(group):
        return jnp.concatenate(
            [
                lax.dynamic_slice_in_dim(w_query, group * 1024, 1024, 1),
                lax.dynamic_slice_in_dim(w_keyval[:, 0], group * 128, 128, 1),
                lax.dynamic_slice_in_dim(w_keyval[:, 1], group * 128, 128, 1),
            ],
            axis=1,
        )

    message = jnp.concatenate(
        [hidden_rows, jnp.broadcast_to(attn_gain[None, :], (16, 128))], axis=0
    )
    theirs = exchange_cores(message)
    weight_theirs = exchange_cores(half(other))

    cache = cache_kv.reshape(DOC_LEN, 512)
    right, left = shift_x(cache, 1), shift_x(cache, -1)
    across = shift_x(right, 1)

    weight = jnp.concatenate([half(c), weight_theirs], axis=0)
    inputs = jnp.concatenate([hidden_rows, theirs[:ROWS]], axis=1).astype(F32)
    gain = jnp.concatenate([attn_gain, theirs[ROWS]], axis=0).astype(F32)
    squares = jnp.sum(inputs * inputs, axis=1)
    scaled = (inputs * gain[None, :]).astype(BF)
    partial = jnp.dot(scaled, weight, preferred_element_type=F32).astype(BF)
    query_part = jnp.transpose(partial[:, :1024].reshape(4, 64, 8, 128), (2, 0, 1, 3))
    new_part = jnp.transpose(partial[:, 1024:].reshape(4, 8, 8, 2, 128), (1, 0, 3, 2, 4))
    square_parts = jnp.stack(parts_of(squares) + [jnp.zeros((ROWS,), BF)] * 5).reshape(8, 4, 64)
    square_parts = jnp.pad(jnp.transpose(square_parts, (1, 0, 2)), ((0, 0), (0, 0), (0, 64)))
    payload = jnp.concatenate(
        [
            query_part,
            new_part.reshape(8, 4, 16, 128),
            jnp.broadcast_to(square_parts[None], (8, 4, 8, 128)),
        ],
        axis=2,
    ).reshape(32, 88, 128)
    total = jnp.sum(swap_zx(payload).astype(F32), axis=0)
    square_sum = (total[80] + (total[81] + total[82]))[:64]
    factor = lax.rsqrt(square_sum / D + EPS)
    near = lax.dynamic_slice_in_dim(factor, z * 8, 8, 0)
    piece = jnp.concatenate(
        [
            total[:64] * factor[:, None],
            (total[64:80].reshape(2, 8, 128) * near[None, :, None]).reshape(16, 128),
        ],
        axis=0,
    ).astype(BF)

    place = jnp.stack([c, y]).astype(jnp.int32)
    flat_in = jnp.transpose(w_in, (1, 2, 0)).reshape(224, D)
    pieces = weight_slices(place, flat_in, w_out)
    slices = [pieces[0], shift_y(pieces[1], 1), None, shift_y(pieces[3], 3)]

    slot_of_doc, row_pos = positions(sel_index, doc_order)
    my_pos = lax.dynamic_slice_in_dim(row_pos, x * 64, 64, 0)
    my_pos = jnp.concatenate([my_pos, my_pos])[None, :]
    token = jnp.arange(8, dtype=jnp.int32)
    docs = jnp.arange(POOL, dtype=jnp.int32)
    key_pos = []
    for step in (0, 1, 3, 2):
        base = ((z * NX + (x - step) % NX) * NC + c) * 8
        name = (docs[:, None] * DOC_LEN + base + token[None, :]).reshape(DOC_LEN)
        at = (slot_of_doc[:, None] * DOC_LEN + base + token[None, :]).reshape(DOC_LEN)
        written = jnp.any(name[:, None] == sel_index[None, :], axis=1)
        key_pos.append(jnp.where(written, DOC_LEN * POOL * 2, at))
    bias = jnp.where(jnp.concatenate(key_pos)[:, None] <= my_pos, 0.0, NEG).astype(F32)
    new_pos = lax.dynamic_slice_in_dim(row_pos, z * 32, 32, 0)
    new_bias = jnp.where(new_pos[:, None] <= my_pos, 0.0, NEG).astype(F32)

    piece, right, left, across, wo, bias = hold(piece, right, left, across, w_output, bias)
    own = swap_z(jnp.broadcast_to(piece[None], (8, 80, 128)))
    wo_right, wo_left = shift_x(wo, 1), shift_x(wo, -1)
    wo_across = shift_x(wo_right, 1)
    others = exchange_cores(own)
    new = jnp.stack([own[:, 64:], others[:, 64:]])
    acc, acc_sent, stats = attend(place, bias, own, others, (cache, right, left, across))

    new_right, new_left = shift_x(new, 1), shift_x(new, -1)
    new_all = jnp.stack([new, new_right, shift_x(new_right, 1), new_left])
    new_here = lax.dynamic_index_in_dim(new_all[:, 0], (x - z // 2) % NX, 0, keepdims=False)
    new_here = lax.dynamic_slice_in_dim(new_here, (z % 2) * 4, 4, 0).reshape(4, 2, 8, 128)

    far_acc = exchange_cores(acc_sent)
    far_stats = exchange_cores(stats)
    payload = merge(
        acc,
        stats,
        far_acc,
        far_stats,
        own,
        new_here[:, 0].reshape(32, 128),
        new_here[:, 1].reshape(32, 128),
        new_bias,
    )
    payload, slices[1], slices[3], last = hold(payload, slices[1], slices[3], pieces[2])
    slices[2] = shift_y(last, 2)
    arrived = swap_z(payload).astype(F32)
    lane = (z % 2) * 64
    tops = arrived[:, 64] + (arrived[:, 65] + arrived[:, 66])
    sums = arrived[:, 67] + (arrived[:, 68] + arrived[:, 69])
    tops = lax.dynamic_slice_in_dim(tops, lane, 64, 1)
    sums = lax.dynamic_slice_in_dim(sums, lane, 64, 1)
    by = jnp.exp(tops - jnp.max(tops, axis=0, keepdims=True))
    norm = jnp.sum(sums * by, axis=0)
    summed = jnp.sum(arrived[:, :64] * by[:, :, None], axis=0)
    piece = (summed / norm[:, None]).astype(BF)
    piece, wo_right, wo_left, wo_across = hold(piece, wo_right, wo_left, wo_across)
    attended = swap_z(jnp.broadcast_to(piece[None], (8, 64, 128)))
    attended_theirs = exchange_cores(attended)

    def flat(value):
        return jnp.transpose(value, (1, 0, 2)).reshape(64, 1024)

    wo_all = jnp.concatenate([w_output, wo_right, wo_across, wo_left], axis=1)
    wo_own = lax.dynamic_slice_in_dim(wo_all, c * 1024, 1024, 0)
    wo_theirs = lax.dynamic_slice_in_dim(wo_all, other * 1024, 1024, 0)
    projected = jnp.dot(flat(attended), wo_own, preferred_element_type=F32)
    projected = projected + jnp.dot(flat(attended_theirs), wo_theirs, preferred_element_type=F32)
    chunks = jnp.transpose(projected.reshape(64, 4, 128), (1, 0, 2))
    early = jnp.concatenate(
        [
            lax.dynamic_slice_in_dim(hidden_rows, y * 64, 64, 0),
            jnp.broadcast_to(ffn_gain[None, :], (16, 128)),
        ],
        axis=0,
    )
    early = permute_xy(early, lambda a, b: (b, a))
    chunks, slices[2] = hold(chunks, slices[2])
    mid = early[:64].astype(F32) + lax.dynamic_index_in_dim(chunks, (x - y) % NX, 0, keepdims=False)
    chunks = chunks.astype(BF)
    for step in range(1, 4):
        sent = lax.dynamic_index_in_dim(chunks, (x - y - step) % NX, 0, keepdims=False)
        mid = mid + shift_y(sent, step).astype(F32)
    feature = (mid * early[64].astype(F32)[None, :]).astype(BF)
    square_parts = jnp.stack(parts_of(jnp.sum(mid * mid, axis=1)) + [jnp.zeros((64,), BF)] * 5)
    payload = jnp.concatenate([feature, jnp.pad(square_parts, ((0, 0), (0, 64)))], axis=0)
    arrived = swap_zx(jnp.broadcast_to(payload[None], (32, 72, 128)))
    arrived_theirs = exchange_cores(arrived)

    reordered = cache.reshape(POOL, 8, 512).at[doc_order].get(mode="promise_in_bounds")
    reordered = reordered.reshape(32, 2, 8, 512)
    stay = lax.dynamic_index_in_dim(reordered, c, 1, keepdims=False)
    leave = lax.dynamic_index_in_dim(reordered, other, 1, keepdims=False)
    come = exchange_cores(leave)
    lower = jnp.where(c == 0, stay, come)
    upper = jnp.where(c == 0, come, stay)
    cache_out = jnp.concatenate([lower, upper], axis=1)
    arrived, cache_out = hold(arrived, cache_out)
    slot_cache = swap_zx(cache_out)

    def features_of(block):
        return jnp.transpose(block[:, :64].reshape(NZ, ROWS, 128), (1, 0, 2)).reshape(ROWS, 1024)

    def squares_of(block):
        parts = jnp.sum(block[:, 64:67, :64].astype(F32), axis=1)
        return jnp.sum(parts.reshape(NZ, ROWS), axis=0)

    feature_own = features_of(arrived)
    feature_theirs = features_of(arrived_theirs)
    square_sum = squares_of(arrived) + squares_of(arrived_theirs)
    square_rows = jnp.stack(parts_of(square_sum) + [jnp.zeros((ROWS,), BF)] * 5)
    hidden = []
    for step in range(4):
        term = lax.dot_general(
            slices[step][:224, :1024], feature_own, NT, preferred_element_type=F32
        ) + lax.dot_general(
            slices[step][:224, 1024:], feature_theirs, NT, preferred_element_type=F32
        )
        hidden.append(term)
    both = hidden[0]
    for step in range(1, 4):
        sent = jnp.concatenate([hidden[step].astype(BF), square_rows], axis=0)
        got = shift_y(sent, -step).astype(F32)
        both = both + got[:224]
        square_sum = square_sum + (got[224] + (got[225] + got[226]))
    both = both * lax.rsqrt(square_sum / D + EPS)[None, :]
    act = (jax.nn.silu(both[:112]) * both[112:]).astype(BF)
    acts = [act] + [shift_y(act, step) for step in range(1, 4)]
    act_all = jnp.concatenate(acts, axis=0)
    out_all = jnp.concatenate([item[224:] for item in slices], axis=0)
    term_theirs = lax.dot_general(act_all, out_all[:, 1024:], TN, preferred_element_type=F32)
    got = exchange_cores(term_theirs.astype(BF))
    term = lax.dot_general(act_all, out_all[:, :1024], TN, preferred_element_type=F32)
    term = (term + got.astype(F32)).astype(BF)
    payload = jnp.transpose(term.reshape(ROWS, NZ, 128), (1, 0, 2)).reshape(32, 64, 128)
    payload, slot_cache = hold(payload, slot_cache)
    down = jnp.sum(swap_zx(payload).astype(F32), axis=0)
    result = permute_xy((mid + down).astype(BF), lambda a, b: (b, a))

    sel_key = jnp.where(row_pos // DOC_LEN == mine, row_pos % DOC_LEN, -1)
    sel_key = jnp.concatenate(
        [lax.dynamic_slice_in_dim(sel_key, ((x - k) % NX) * 64, 64, 0) for k in range(4)]
    )
    hits = sel_key[None, :] == jnp.arange(DOC_LEN, dtype=jnp.int32)[:, None]
    covered = jnp.any(hits, axis=1)
    new_flat = new_all.reshape(4, 2, 8, 2, 8, 128)
    new_flat = jnp.where(c == 0, new_flat, new_flat[:, ::-1])
    new_flat = jnp.transpose(new_flat, (0, 2, 4, 3, 1, 5)).reshape(ROWS, 512)
    placed = jnp.dot(hits.astype(BF), new_flat, preferred_element_type=F32).astype(BF)
    joined = jnp.where(covered[:, None], placed, slot_cache.reshape(DOC_LEN, 512))
    return (result, joined.reshape(DOC_LEN, 2, 256))


def solution(mesh):
    split = Mesh(mesh.devices.reshape(NZ, NX, NC, NY), ("z", "x", "c", "y"))
    pool = ("z", "x", "c")
    return jax.shard_map(
        shards,
        mesh=split,
        in_specs=(
            P(None, pool),
            P(None, pool, None, "y"),
            P(),
            P(),
            P(pool),
            P(pool, "y"),
            P(pool, None, "y"),
            P("y", pool),
            P(pool),
            P(None, None, ("z", "x", "c", "y")),
            P(("z", "x", "c", "y"), None),
        ),
        out_specs=(P("y", pool), P(pool, None, "y")),
        check_vma=False,
    )
```

time: 285 us -> 429 us (1.51)
  Pallas kernels: 9.17 us -> 177 us
  blocking collectives: 61.1 us -> 0 us
  starting transfers between devices: 71.3 us -> 104 us
  local copies, waits for them, and re-layouts: 52.2 us -> 25.2 us
  waiting for transfers between devices: 67.3 us -> 88.7 us
  other arithmetic: 5.79 us -> 11.7 us
    pallas_call x1 -> x3, Pallas kernels: 9.17 us -> 177 us  [the longest x1 170 us: weight_slices(): pl.pallas_call(slices_kernel, out_shape=tuple((jax.ShapeDtypeStruct((336,...]
    all_to_all x2 -> x0, blocking collectives: 61.1 us -> none  [swap_zx(): return lax.all_to_all(value, ('z', 'x'), 0, 0, tiled=True)]
    unnamed x58 -> x60, local copies, waits for them, and re-layouts: 37.7 us -> 7.94 us
    all_to_all x4, waiting for transfers between devices: 32.8 us -> 49 us  [swap_zx(): return lax.all_to_all(value, ('z', 'x'), 0, 0, tiled=True)]
    ppermute x0 -> x9, waiting for transfers between devices: none -> 12.1 us  [shift_x(): return lax.ppermute(value, 'x', [(i, (i + step) % NX) for i in range(NX)])]
    all_to_all x1 -> x3, starting transfers between devices: 5.97 us -> 17.8 us  [swap_z(): return lax.all_to_all(value, 'z', 0, 0, tiled=True)]
    ppermute x0 -> x9, starting transfers between devices: none -> 11.7 us  [shift_x(): return lax.ppermute(value, 'x', [(i, (i + step) % NX) for i in range(NX)])]
    all_to_all x1 -> x3, waiting for transfers between devices: 16.3 us -> 5.68 us  [swap_z(): return lax.all_to_all(value, 'z', 0, 0, tiled=True)]
  transfers between devices with their start and end apart: 31 -> 39, of which waited for: 13 -> 20; matrix products, arithmetic and copies ran while one was open for 22% -> 9% of each run, Pallas kernels for 0% -> 42%
where the time goes in v2:
time: 429 us; the launch traced here: 423 us
  Pallas kernels  177 us (41%)
  starting transfers between devices  104 us (24%)
  waiting for transfers between devices  88.7 us (21%)
  local copies, waits for them, and re-layouts  25.2 us (6%)
  matrix products  14.8 us (3%)
  other arithmetic  11.7 us (3%)
    pallas_call x1, Pallas kernels, weight_slices(): pl.pallas_call(slices_kernel, out_shape=tuple((jax.ShapeDtypeStruct((336,...  170 us
    all_to_all x4, waiting for transfers between devices, swap_zx(): return lax.all_to_all(value, ('z', 'x'), 0, 0, tiled=True)  49 us
    all_to_all x4, starting transfers between devices, swap_zx(): return lax.all_to_all(value, ('z', 'x'), 0, 0, tiled=True)  37 us
    ppermute x12, starting transfers between devices, shift_y(): return lax.ppermute(value, 'y', [(i, (i + step) % NY) for i in range(NY)])  24.7 us
    all_to_all x3, starting transfers between devices, swap_z(): return lax.all_to_all(value, 'z', 0, 0, tiled=True)  17.8 us
    ppermute x12, waiting for transfers between devices, shift_y(): return lax.ppermute(value, 'y', [(i, (i + step) % NY) for i in range(NY)])  13.7 us
    ppermute x9, waiting for transfers between devices, shift_x(): return lax.ppermute(value, 'x', [(i, (i + step) % NX) for i in range(NX)])  12.1 us
    ppermute x9, starting transfers between devices, shift_x(): return lax.ppermute(value, 'x', [(i, (i + step) % NX) for i in range(NX)])  11.7 us
  transfers between devices with their start and end apart: 39, of which 20 were waited for; matrix products, arithmetic and copies ran while one was open for 9% of the time, Pallas kernels for 42%

profile of v2, /device:TPU:4, one launch (start us, length us, event | category | flops | bytes accessed | tf_op | source)
XLA Modules:
  0.0 423.2 jit_solution(1745655778693682605)
XLA Ops:
  10.3 11.6 %all-to-all-start = ((bf16[32,88,128]{2,1,0:T(8,128)(2,1)}), bf16[32,88,128]{2,1,0:T(8,128)(2,1)}, u32[]{:S(2)}, u32[]{:S(2)}) async-start(bf16[32,88,128]{2,1,0:T(8,128)(2,1)} %pad_maximum_fusion.1), calls=%async_computation | async-start | bytes 1441792 | tf_op jit(solution)/shard_map/all_to_all | solution.py:44
  24.2 19.1 %all-to-all-done = bf16[32,88,128]{2,1,0:T(8,128)(2,1)} async-done(((bf16[32,88,128]{2,1,0:T(8,128)(2,1)}), bf16[32,88,128]{2,1,0:T(8,128)(2,1)}, u32[]{:S(2)}, u32[]{:S(2)}) %all-to-all-start) | async-done | bytes 720928 | tf_op jit(solution)/shard_map/all_to_all | solution.py:44
  45.6 3.9 all-to-all-start.1
  50.1 169.9 %weight_slices.1 = (bf16[336,2048]{1,0:T(8,128)(2,1)}, bf16[336,2048]{1,0:T(8,128)(2,1)}, bf16[336,2048]{1,0:T(8,128)(2,1)}, bf16[336,2048]{1,0:T(8,128)(2,1)}) custom-call(s32[2]{0:T(128)} %pad_add_fusion.3.place_ref, bf16[224,8192]{1,0:T(8,128)(2,1)} %bitcast.176, bf16[112,8192]{1,0:T(8,128)(2,1)} %out_ref.1), custom_call_target="tpu_custom_call" | custom-call | bytes 11000000 | tf_op jit(solution)/shard_map/weight_slices/pallas_call | solution.py:119
  221.6 1.7 collective-permute-start.13
  227.3 2.9 collective-permute-start.14
  230.8 1.9 collective-permute-start.10
  232.7 4.8 %attend.1 = (f32[128,512]{1,0:T(8,128)S(1)}, bf16[128,512]{1,0:T(8,128)(2,1)S(1)}, f32[8,512]{1,0:T(8,128)S(1)}) custom-call(s32[2]{0:T(128)S(1)} %copy-done.3, f32[2048,128]{1,0:T(8,128)S(1)} %compare_select_fusion.bias_ref, bf16[8,80,128]{2,1,0:T(8,128)(2,1)S(1)} %all-to-all-done.1.own_ref, bf16[8,80,128]{2,1,0:T(8,128)(2,1)S(1)} %collective-permute-done.6.other_ref, ...), custom_call_target="tpu_custom_call" | custom-call | flops 1073741824 | bytes 6000000 | tf_op jit(solution)/shard_map/attend/pallas_call | solution.py:177
  238.3 4.7 %collective-permute-done.10 = bf16[2,8,16,128]{3,2,1,0:T(8,128)(2,1)S(1)} collective-permute-done((bf16[2,8,16,128]{3,2,1,0:T(8,128)(2,1)S(1)}, bf16[2,8,16,128]{3,2,1,0:T(8,128)(2,1)S(1)}, u32[]{:S(2)}, u32[]{:S(2)}) %collective-permute-start.10) | collective-permute-done | bytes 65568 | tf_op jit(solution)/shard_map/ppermute | solution.py:56
  244.9 2.2 merge.1
  247.1 5.7 %collective-permute-done.12 = bf16[336,2048]{1,0:T(8,128)(2,1)} collective-permute-done((bf16[336,2048]{1,0:T(8,128)(2,1)}, bf16[336,2048]{1,0:T(8,128)(2,1)}, u32[]{:S(2)}, u32[]{:S(2)}) %collective-permute-start.12) | collective-permute-done | bytes 1376288 | tf_op jit(solution)/shard_map/ppermute | solution.py:31
  252.8 6.9 %all-to-all-start.2 = ((bf16[8,80,128]{2,1,0:T(8,128)(2,1)}), bf16[8,80,128]{2,1,0:T(8,128)(2,1)}, u32[]{:S(2)}, u32[]{:S(2)}) async-start(bf16[8,80,128]{2,1,0:T(8,128)(2,1)} %merge.1), calls=%async_computation.2 | async-start | bytes 327680 | tf_op jit(solution)/shard_map/all_to_all | solution.py:60
  260.3 7.4 %collective-permute-start = (bf16[80,128]{1,0:T(8,128)(2,1)}, bf16[80,128]{1,0:T(8,128)(2,1)}, u32[]{:S(2)}, u32[]{:S(2)}) collective-permute-start(bf16[80,128]{1,0:T(8,128)(2,1)} %pad_maximum_fusion.12), channel_id=1, source_target_pairs={{0,0},{1,8},{2,16},{3,24},{8,1},{9,9},{10,17},{11,25},{16,2},{17,1... | collective-permute-start | bytes 61448 | tf_op jit(solution)/shard_map/ppermute | solution.py:40
  269.1 2.0 collective-permute-start.16
  273.6 7.0 %collective-permute-done.15 = bf16[2048,128]{1,0:T(8,128)(2,1)} collective-permute-done((bf16[2048,128]{1,0:T(8,128)(2,1)}, bf16[2048,128]{1,0:T(8,128)(2,1)}, u32[]{:S(2)}, u32[]{:S(2)}) %collective-permute-start.15) | collective-permute-done | bytes 524320 | tf_op jit(solution)/shard_map/ppermute | solution.py:56
  281.3 6.9 %all-to-all-start.3 = ((bf16[8,64,128]{2,1,0:T(8,128)(2,1)}), bf16[8,64,128]{2,1,0:T(8,128)(2,1)}, u32[]{:S(2)}, u32[]{:S(2)}) async-start(bf16[8,64,128]{2,1,0:T(8,128)(2,1)} %broadcast_in_dim.80), calls=%async_computation.3 | async-start | bytes 262144 | tf_op jit(solution)/shard_map/all_to_all | solution.py:60
  291.7 5.7 %all-to-all-done.3 = bf16[8,64,128]{2,1,0:T(8,128)(2,1)} async-done(((bf16[8,64,128]{2,1,0:T(8,128)(2,1)}), bf16[8,64,128]{2,1,0:T(8,128)(2,1)}, u32[]{:S(2)}, u32[]{:S(2)}) %all-to-all-start.3) | async-done | bytes 131104 | tf_op jit(solution)/shard_map/all_to_all | solution.py:60
  299.3 2.4 collective-permute-done.18
  302.2 11.7 %collective-permute-start.21 = (bf16[64,128]{1,0:T(8,128)(2,1)S(1)}, bf16[64,128]{1,0:T(8,128)(2,1)S(1)}, u32[]{:S(2)}, u32[]{:S(2)}) collective-permute-start(bf16[64,128]{1,0:T(8,128)(2,1)S(1)} %get-tuple-element.99), channel_id=1, source_target_pairs={{0,3},{1,0},{2,1},{3,2},{4,7},{5,4},{6,5},{7,6},{8,11},{9,8},{10,9... | collective-permute-start | bytes 49160 | tf_op jit(solution)/shard_map/ppermute | solution.py:31
  314.6 1.9 collective-permute-done.21
  318.3 11.6 %all-to-all-start.4 = ((bf16[32,72,128]{2,1,0:T(8,128)(2,1)}), bf16[32,72,128]{2,1,0:T(8,128)(2,1)S(1)}, u32[]{:S(2)}, u32[]{:S(2)}) async-start(bf16[32,72,128]{2,1,0:T(8,128)(2,1)} %broadcast_in_dim.81), calls=%async_computation.4 | async-start | bytes 1179648 | tf_op jit(solution)/shard_map/all_to_all | solution.py:44
  331.0 12.2 %all-to-all-done.4 = bf16[32,72,128]{2,1,0:T(8,128)(2,1)S(1)} async-done(((bf16[32,72,128]{2,1,0:T(8,128)(2,1)}), bf16[32,72,128]{2,1,0:T(8,128)(2,1)S(1)}, u32[]{:S(2)}, u32[]{:S(2)}) %all-to-all-start.4) | async-done | bytes 589856 | tf_op jit(solution)/shard_map/all_to_all | solution.py:44
  355.3 2.5 collective-permute-start.24
  359.1 1.8 collective-permute-start.25
  364.8 5.4 %all-to-all-start.5 = ((bf16[32,16,512]{2,1,0:T(8,128)(2,1)}), bf16[32,16,512]{2,1,0:T(8,128)(2,1)S(1)}, u32[]{:S(2)}, u32[]{:S(2)}) async-start(bf16[32,16,512]{2,1,0:T(8,128)(2,1)} %pad_maximum_fusion.2), calls=%async_computation.5 | async-start | bytes 1048576 | tf_op jit(solution)/shard_map/all_to_all | solution.py:44
  371.8 2.0 collective-permute-start.27
  373.8 2.7 collective-permute-start.28
  381.3 1.9 collective-permute-done.30
  387.2 8.4 %all-to-all-start.6 = ((bf16[32,64,128]{2,1,0:T(8,128)(2,1)}), bf16[32,64,128]{2,1,0:T(8,128)(2,1)S(1)}, u32[]{:S(2)}, u32[]{:S(2)}) async-start(bf16[32,64,128]{2,1,0:T(8,128)(2,1)} %bitcast.50), calls=%async_computation.6 | async-start | bytes 1048576 | tf_op jit(solution)/shard_map/all_to_all | solution.py:44
  396.3 16.4 %all-to-all-done.6 = bf16[32,64,128]{2,1,0:T(8,128)(2,1)S(1)} async-done(((bf16[32,64,128]{2,1,0:T(8,128)(2,1)}), bf16[32,64,128]{2,1,0:T(8,128)(2,1)S(1)}, u32[]{:S(2)}, u32[]{:S(2)}) %all-to-all-start.6) | async-done | bytes 524320 | tf_op jit(solution)/shard_map/all_to_all | solution.py:44
  412.8 4.1 collective-permute-start.31
  418.4 4.0 collective-permute-done.31
  (272 shorter events, 67.9 us)
Async XLA Ops:
  1.8 21.1 %collective-permute-start.3 = (bf16[512,512]{1,0:T(8,128)(2,1)S(1)}, bf16[512,512]{1,0:T(8,128)(2,1)S(1)}, u32[]{:S(2)}, u32[]{:S(2)}) collective-permute-start(bf16[512,512]{1,0:T(8,128)(2,1)S(1)} %bitcast.165), channel_id=1, source_target_pairs={{0,8},{8,16},{16,24},{24,0},{1,9},{9,17},{17,25},{25,1},{2,10},{10... | collective-permute-start | bytes 1572872 | tf_op jit(solution)/shard_map/ppermute | solution.py:56
  3.1 41.7 %collective-permute-start.4 = (bf16[512,512]{1,0:T(8,128)(2,1)S(1)}, bf16[512,512]{1,0:T(8,128)(2,1)S(1)}, u32[]{:S(2)}, u32[]{:S(2)}) collective-permute-start(bf16[512,512]{1,0:T(8,128)(2,1)S(1)} %bitcast.166), channel_id=1, source_target_pairs={{0,24},{8,0},{16,8},{24,16},{1,25},{9,1},{17,9},{25,17},{2,26},{10... | collective-permute-start | bytes 1572872 | tf_op jit(solution)/shard_map/ppermute | solution.py:56
  10.3 33.0 %all-to-all-start = ((bf16[32,88,128]{2,1,0:T(8,128)(2,1)}), bf16[32,88,128]{2,1,0:T(8,128)(2,1)}, u32[]{:S(2)}, u32[]{:S(2)}) async-start(bf16[32,88,128]{2,1,0:T(8,128)(2,1)} %pad_maximum_fusion.1), calls=%async_computation | async-start | bytes 1441792 | tf_op jit(solution)/shard_map/all_to_all | solution.py:44
  22.9 21.9 %collective-permute-start.5 = (bf16[512,512]{1,0:T(8,128)(2,1)S(1)}, bf16[512,512]{1,0:T(8,128)(2,1)S(1)}, u32[]{:S(2)}, u32[]{:S(2)}) collective-permute-start(bf16[512,512]{1,0:T(8,128)(2,1)S(1)} %collective-permute-done.3.c1), channel_id=1, source_target_pairs={{0,8},{8,16},{16,24},{24,0},{1,9},{9,17},{17,25},{25,1},{2,10},{10... | collective-permute-start | bytes 1572872 | tf_op jit(solution)/shard_map/ppermute | solution.py:56
  45.6 178.5 %all-to-all-start.1 = ((bf16[8,80,128]{2,1,0:T(8,128)(2,1)}), bf16[8,80,128]{2,1,0:T(8,128)(2,1)S(1)}, u32[]{:S(2)}, u32[]{:S(2)}) async-start(bf16[8,80,128]{2,1,0:T(8,128)(2,1)} %broadcast_in_dim.77), calls=%async_computation.1 | async-start | bytes 327680 | tf_op jit(solution)/shard_map/all_to_all | solution.py:60
  219.9 32.8 %collective-permute-start.12 = (bf16[336,2048]{1,0:T(8,128)(2,1)}, bf16[336,2048]{1,0:T(8,128)(2,1)}, u32[]{:S(2)}, u32[]{:S(2)}) collective-permute-start(bf16[336,2048]{1,0:T(8,128)(2,1)} %get-tuple-element.37), channel_id=1, source_target_pairs={{0,1},{1,2},{2,3},{3,0},{4,5},{5,6},{6,7},{7,4},{8,9},{9,10},{10,1... | collective-permute-start | bytes 4128776 | tf_op jit(solution)/shard_map/ppermute | solution.py:31
  221.6 31.2 %collective-permute-start.13 = (bf16[336,2048]{1,0:T(8,128)(2,1)}, bf16[336,2048]{1,0:T(8,128)(2,1)}, u32[]{:S(2)}, u32[]{:S(2)}) collective-permute-start(bf16[336,2048]{1,0:T(8,128)(2,1)} %get-tuple-element.38), channel_id=1, source_target_pairs={{0,3},{1,0},{2,1},{3,2},{4,7},{5,4},{6,5},{7,6},{8,11},{9,8},{10,9... | collective-permute-start | bytes 4128776 | tf_op jit(solution)/shard_map/ppermute | solution.py:31
  226.0 4.8 %collective-permute-start.9 = (bf16[2,8,16,128]{3,2,1,0:T(8,128)(2,1)S(1)}, bf16[2,8,16,128]{3,2,1,0:T(8,128)(2,1)S(1)}, u32[]{:S(2)}, u32[]{:S(2)}) collective-permute-start(bf16[2,8,16,128]{3,2,1,0:T(8,128)(2,1)S(1)} %get-tuple-element.102), channel_id=1, source_target_pairs={{0,8},{8,16},{16,24},{24,0},{1,9},{9,17},{17,25},{25,1},{2,10},{10... | collective-permute-start | bytes 196616 | tf_op jit(solution)/shard_map/ppermute | solution.py:56
  227.3 41.8 %collective-permute-start.14 = (bf16[2048,128]{1,0:T(8,128)(2,1)}, bf16[2048,128]{1,0:T(8,128)(2,1)}, u32[]{:S(2)}, u32[]{:S(2)}) collective-permute-start(bf16[2048,128]{1,0:T(8,128)(2,1)} %param.18), channel_id=1, source_target_pairs={{0,8},{8,16},{16,24},{24,0},{1,9},{9,17},{17,25},{25,1},{2,10},{10... | collective-permute-start | bytes 1572872 | tf_op jit(solution)/shard_map/ppermute | solution.py:56
  230.2 8.0 %collective-permute-start.11 = (bf16[2,8,16,128]{3,2,1,0:T(8,128)(2,1)S(1)}, bf16[2,8,16,128]{3,2,1,0:T(8,128)(2,1)S(1)}, u32[]{:S(2)}, u32[]{:S(2)}) collective-permute-start(bf16[2,8,16,128]{3,2,1,0:T(8,128)(2,1)S(1)} %get-tuple-element.102), channel_id=1, source_target_pairs={{0,24},{8,0},{16,8},{24,16},{1,25},{9,1},{17,9},{25,17},{2,26},{10... | collective-permute-start | bytes 196616 | tf_op jit(solution)/shard_map/ppermute | solution.py:56
  230.8 12.2 %collective-permute-start.10 = (bf16[2,8,16,128]{3,2,1,0:T(8,128)(2,1)S(1)}, bf16[2,8,16,128]{3,2,1,0:T(8,128)(2,1)S(1)}, u32[]{:S(2)}, u32[]{:S(2)}) collective-permute-start(bf16[2,8,16,128]{3,2,1,0:T(8,128)(2,1)S(1)} %collective-permute-done.9), channel_id=1, source_target_pairs={{0,8},{8,16},{16,24},{24,0},{1,9},{9,17},{17,25},{25,1},{2,10},{10... | collective-permute-start | bytes 196616 | tf_op jit(solution)/shard_map/ppermute | solution.py:56
  238.2 6.0 %collective-permute-start.7 = (bf16[128,512]{1,0:T(8,128)(2,1)S(1)}, bf16[128,512]{1,0:T(8,128)(2,1)S(1)}, u32[]{:S(2)}, u32[]{:S(2)}) collective-permute-start(bf16[128,512]{1,0:T(8,128)(2,1)S(1)} %get-tuple-element.36), channel_id=1, source_target_pairs={{0,4},{4,0},{1,5},{5,1},{2,6},{6,2},{3,7},{7,3},{8,12},{12,8},{9,1... | collective-permute-start | bytes 393224 | tf_op jit(solution)/shard_map/ppermute | solution.py:27
  252.8 18.3 %all-to-all-start.2 = ((bf16[8,80,128]{2,1,0:T(8,128)(2,1)}), bf16[8,80,128]{2,1,0:T(8,128)(2,1)}, u32[]{:S(2)}, u32[]{:S(2)}) async-start(bf16[8,80,128]{2,1,0:T(8,128)(2,1)} %merge.1), calls=%async_computation.2 | async-start | bytes 327680 | tf_op jit(solution)/shard_map/all_to_all | solution.py:60
  260.3 53.6 %collective-permute-start = (bf16[80,128]{1,0:T(8,128)(2,1)}, bf16[80,128]{1,0:T(8,128)(2,1)}, u32[]{:S(2)}, u32[]{:S(2)}) collective-permute-start(bf16[80,128]{1,0:T(8,128)(2,1)} %pad_maximum_fusion.12), channel_id=1, source_target_pairs={{0,0},{1,8},{2,16},{3,24},{8,1},{9,9},{10,17},{11,25},{16,2},{17,1... | collective-permute-start | bytes 61448 | tf_op jit(solution)/shard_map/ppermute | solution.py:40
  269.0 11.5 %collective-permute-start.15 = (bf16[2048,128]{1,0:T(8,128)(2,1)}, bf16[2048,128]{1,0:T(8,128)(2,1)}, u32[]{:S(2)}, u32[]{:S(2)}) collective-permute-start(bf16[2048,128]{1,0:T(8,128)(2,1)} %param.18), channel_id=1, source_target_pairs={{0,24},{8,0},{16,8},{24,16},{1,25},{9,1},{17,9},{25,17},{2,26},{10... | collective-permute-start | bytes 1572872 | tf_op jit(solution)/shard_map/ppermute | solution.py:56
  269.1 11.5 %collective-permute-start.16 = (bf16[2048,128]{1,0:T(8,128)(2,1)}, bf16[2048,128]{1,0:T(8,128)(2,1)}, u32[]{:S(2)}, u32[]{:S(2)}) collective-permute-start(bf16[2048,128]{1,0:T(8,128)(2,1)} %collective-permute-done.14), channel_id=1, source_target_pairs={{0,8},{8,16},{16,24},{24,0},{1,9},{9,17},{17,25},{25,1},{2,10},{10... | collective-permute-start | bytes 1572872 | tf_op jit(solution)/shard_map/ppermute | solution.py:56
  271.1 30.6 %collective-permute-start.18 = (bf16[336,2048]{1,0:T(8,128)(2,1)}, bf16[336,2048]{1,0:T(8,128)(2,1)S(1)}, u32[]{:S(2)}, u32[]{:S(2)}) collective-permute-start(bf16[336,2048]{1,0:T(8,128)(2,1)} %get-tuple-element.46), channel_id=1, source_target_pairs={{0,2},{1,3},{2,0},{3,1},{4,6},{5,7},{6,4},{7,5},{8,10},{9,11},{10,... | collective-permute-start | bytes 4128776 | tf_op jit(solution)/shard_map/ppermute | solution.py:31
  281.3 16.1 %all-to-all-start.3 = ((bf16[8,64,128]{2,1,0:T(8,128)(2,1)}), bf16[8,64,128]{2,1,0:T(8,128)(2,1)}, u32[]{:S(2)}, u32[]{:S(2)}) async-start(bf16[8,64,128]{2,1,0:T(8,128)(2,1)} %broadcast_in_dim.80), calls=%async_computation.3 | async-start | bytes 262144 | tf_op jit(solution)/shard_map/all_to_all | solution.py:60
  301.7 12.9 %collective-permute-start.19 = (bf16[64,128]{1,0:T(8,128)(2,1)S(1)}, bf16[64,128]{1,0:T(8,128)(2,1)S(1)}, u32[]{:S(2)}, u32[]{:S(2)}) collective-permute-start(bf16[64,128]{1,0:T(8,128)(2,1)S(1)} %get-tuple-element.98), channel_id=1, source_target_pairs={{0,1},{1,2},{2,3},{3,0},{4,5},{5,6},{6,7},{7,4},{8,9},{9,10},{10,1... | collective-permute-start | bytes 49160 | tf_op jit(solution)/shard_map/ppermute | solution.py:31
  301.8 12.8 %collective-permute-start.20 = (bf16[64,128]{1,0:T(8,128)(2,1)S(1)}, bf16[64,128]{1,0:T(8,128)(2,1)S(1)}, u32[]{:S(2)}, u32[]{:S(2)}) collective-permute-start(bf16[64,128]{1,0:T(8,128)(2,1)S(1)} %get-tuple-element.100), channel_id=1, source_target_pairs={{0,2},{1,3},{2,0},{3,1},{4,6},{5,7},{6,4},{7,5},{8,10},{9,11},{10,... | collective-permute-start | bytes 49160 | tf_op jit(solution)/shard_map/ppermute | solution.py:31
  302.2 14.3 %collective-permute-start.21 = (bf16[64,128]{1,0:T(8,128)(2,1)S(1)}, bf16[64,128]{1,0:T(8,128)(2,1)S(1)}, u32[]{:S(2)}, u32[]{:S(2)}) collective-permute-start(bf16[64,128]{1,0:T(8,128)(2,1)S(1)} %get-tuple-element.99), channel_id=1, source_target_pairs={{0,3},{1,0},{2,1},{3,2},{4,7},{5,4},{6,5},{7,6},{8,11},{9,8},{10,9... | collective-permute-start | bytes 49160 | tf_op jit(solution)/shard_map/ppermute | solution.py:31
  318.3 24.9 %all-to-all-start.4 = ((bf16[32,72,128]{2,1,0:T(8,128)(2,1)}), bf16[32,72,128]{2,1,0:T(8,128)(2,1)S(1)}, u32[]{:S(2)}, u32[]{:S(2)}) async-start(bf16[32,72,128]{2,1,0:T(8,128)(2,1)} %broadcast_in_dim.81), calls=%async_computation.4 | async-start | bytes 1179648 | tf_op jit(solution)/shard_map/all_to_all | solution.py:44
  330.9 13.4 %collective-permute-start.22 = (bf16[32,8,512]{2,1,0:T(8,128)(2,1)S(1)}, bf16[32,8,512]{2,1,0:T(8,128)(2,1)S(1)}, u32[]{:S(2)}, u32[]{:S(2)}) collective-permute-start(bf16[32,8,512]{2,1,0:T(8,128)(2,1)S(1)} %dynamic-slice_bitcast_fusion), channel_id=1, source_target_pairs={{0,4},{4,0},{1,5},{5,1},{2,6},{6,2},{3,7},{7,3},{8,12},{12,8},{9,1... | collective-permute-start | bytes 786440 | tf_op jit(solution)/shard_map/ppermute | solution.py:27
  343.2 4.5 %collective-permute-start.23 = (bf16[32,72,128]{2,1,0:T(8,128)(2,1)S(1)}, bf16[32,72,128]{2,1,0:T(8,128)(2,1)}, u32[]{:S(2)}, u32[]{:S(2)}) collective-permute-start(bf16[32,72,128]{2,1,0:T(8,128)(2,1)S(1)} %all-to-all-done.4), channel_id=1, source_target_pairs={{0,4},{4,0},{1,5},{5,1},{2,6},{6,2},{3,7},{7,3},{8,12},{12,8},{9,1... | collective-permute-start | bytes 1769480 | tf_op jit(solution)/shard_map/ppermute | solution.py:27
  355.3 14.9 %collective-permute-start.24 = (bf16[232,256]{1,0:T(8,128)(2,1)S(1)}, bf16[232,256]{1,0:T(8,128)(2,1)S(1)}, u32[]{:S(2)}, u32[]{:S(2)}) collective-permute-start(bf16[232,256]{1,0:T(8,128)(2,1)S(1)} %concatenate.102), channel_id=1, source_target_pairs={{0,3},{1,0},{2,1},{3,2},{4,7},{5,4},{6,5},{7,6},{8,11},{9,8},{10,9... | collective-permute-start | bytes 356360 | tf_op jit(solution)/shard_map/ppermute | solution.py:31
  359.1 11.1 %collective-permute-start.25 = (bf16[232,256]{1,0:T(8,128)(2,1)S(1)}, bf16[232,256]{1,0:T(8,128)(2,1)S(1)}, u32[]{:S(2)}, u32[]{:S(2)}) collective-permute-start(bf16[232,256]{1,0:T(8,128)(2,1)S(1)} %concatenate.103), channel_id=1, source_target_pairs={{0,2},{1,3},{2,0},{3,1},{4,6},{5,7},{6,4},{7,5},{8,10},{9,11},{10,... | collective-permute-start | bytes 356360 | tf_op jit(solution)/shard_map/ppermute | solution.py:31
  363.5 6.8 %collective-permute-start.26 = (bf16[232,256]{1,0:T(8,128)(2,1)}, bf16[232,256]{1,0:T(8,128)(2,1)S(1)}, u32[]{:S(2)}, u32[]{:S(2)}) collective-permute-start(bf16[232,256]{1,0:T(8,128)(2,1)} %concatenate.104), channel_id=1, source_target_pairs={{0,1},{1,2},{2,3},{3,0},{4,5},{5,6},{6,7},{7,4},{8,9},{9,10},{10,1... | collective-permute-start | bytes 356360 | tf_op jit(solution)/shard_map/ppermute | solution.py:31
  364.8 22.3 %all-to-all-start.5 = ((bf16[32,16,512]{2,1,0:T(8,128)(2,1)}), bf16[32,16,512]{2,1,0:T(8,128)(2,1)S(1)}, u32[]{:S(2)}, u32[]{:S(2)}) async-start(bf16[32,16,512]{2,1,0:T(8,128)(2,1)} %pad_maximum_fusion.2), calls=%async_computation.5 | async-start | bytes 1048576 | tf_op jit(solution)/shard_map/all_to_all | solution.py:44
  371.8 6.1 %collective-permute-start.27 = (bf16[112,256]{1,0:T(8,128)(2,1)S(1)}, bf16[112,256]{1,0:T(8,128)(2,1)S(1)}, u32[]{:S(2)}, u32[]{:S(2)}) collective-permute-start(bf16[112,256]{1,0:T(8,128)(2,1)S(1)} %fusion.46), channel_id=1, source_target_pairs={{0,1},{1,2},{2,3},{3,0},{4,5},{5,6},{6,7},{7,4},{8,9},{9,10},{10,1... | collective-permute-start | bytes 172040 | tf_op jit(solution)/shard_map/ppermute | solution.py:31
  373.8 5.7 %collective-permute-start.28 = (bf16[112,256]{1,0:T(8,128)(2,1)S(1)}, bf16[112,256]{1,0:T(8,128)(2,1)S(1)}, u32[]{:S(2)}, u32[]{:S(2)}) collective-permute-start(bf16[112,256]{1,0:T(8,128)(2,1)S(1)} %fusion.46), channel_id=1, source_target_pairs={{0,2},{1,3},{2,0},{3,1},{4,6},{5,7},{6,4},{7,5},{8,10},{9,11},{10,... | collective-permute-start | bytes 172040 | tf_op jit(solution)/shard_map/ppermute | solution.py:31
  387.2 25.6 %all-to-all-start.6 = ((bf16[32,64,128]{2,1,0:T(8,128)(2,1)}), bf16[32,64,128]{2,1,0:T(8,128)(2,1)S(1)}, u32[]{:S(2)}, u32[]{:S(2)}) async-start(bf16[32,64,128]{2,1,0:T(8,128)(2,1)} %bitcast.50), calls=%async_computation.6 | async-start | bytes 1048576 | tf_op jit(solution)/shard_map/all_to_all | solution.py:44
  412.8 9.5 %collective-permute-start.31 = (bf16[64,128]{1,0:T(8,128)(2,1)S(1)}, bf16[64,128]{1,0:T(8,128)(2,1)S(1)}, u32[]{:S(2)}, u32[]{:S(2)}) collective-permute-start(bf16[64,128]{1,0:T(8,128)(2,1)S(1)} %add_convert_fusion), channel_id=1, source_target_pairs={{0,0},{1,8},{2,16},{3,24},{8,1},{9,9},{10,17},{11,25},{16,2},{17,1... | collective-permute-start | bytes 49160 | tf_op jit(solution)/shard_map/ppermute | solution.py:40
  (32 other events, 586.1 us)

commit v3 on v2

--- a/solution.py
+++ b/solution.py
@@ -80,48 +80,29 @@
     return slot_of_doc, row_pos
 
 
-def slices_kernel(place_ref, in_ref, out_ref, *rest):
-    pieces, sems = rest[:4], rest[4]
+def slices_kernel(place_ref, in_ref, out_ref, *pieces):
     core = place_ref[0]
     y = place_ref[1]
-    for go in (True, False):
-        for step in range(4):
-            base = lax.rem(y + step, NY) * 256
-
-            def body(k, carry):
-                far = k // NZ
-                group = jnp.where(far == 0, core, 1 - core)
-                start = pl.multiple_of((k - far * NZ) * 1024 + base + group * 128, 128)
-                to = pl.multiple_of(k * 128, 128)
-                first = pltpu.make_async_copy(
-                    in_ref.at[:, pl.ds(start, 128)],
-                    pieces[step].at[0:224, pl.ds(to, 128)],
-                    sems.at[step, 0, k],
-                )
-                second = pltpu.make_async_copy(
-                    out_ref.at[:, pl.ds(start, 128)],
-                    pieces[step].at[224:336, pl.ds(to, 128)],
-                    sems.at[step, 1, k],
-                )
-                if go:
-                    first.start()
-                    second.start()
-                else:
-                    first.wait()
-                    second.wait()
-                return carry
-
-            lax.fori_loop(0, 16, body, 0)
+    for step in range(4):
+        base = lax.rem(y + step, NY) * 256
+        for rel in range(2):
+            group = core if rel == 0 else 1 - core
+            lanes = pl.ds(pl.multiple_of(base + group * 128, 128), 128)
+            pieces[step][rel, 0:224, :] = in_ref[:, lanes]
+            pieces[step][rel, 224:336, :] = out_ref[:, lanes]
 
 
 def weight_slices(place, flat_in, w_out):
-    hbm = pl.BlockSpec(memory_space=pl.ANY)
     return pl.pallas_call(
         slices_kernel,
-        out_shape=tuple(jax.ShapeDtypeStruct((336, 2048), BF) for _ in range(4)),
-        in_specs=[pl.BlockSpec(memory_space=pltpu.SMEM), hbm, hbm],
-        out_specs=tuple(hbm for _ in range(4)),
-        scratch_shapes=[pltpu.SemaphoreType.DMA((4, 2, 16))],
+        grid=(NZ,),
+        out_shape=tuple(jax.ShapeDtypeStruct((2, 336, 1024), BF) for _ in range(4)),
+        in_specs=[
+            pl.BlockSpec(memory_space=pltpu.SMEM),
+            pl.BlockSpec((224, 1024), lambda k: (0, k)),
+            pl.BlockSpec((112, 1024), lambda k: (0, k)),
+        ],
+        out_specs=tuple(pl.BlockSpec((2, 336, 128), lambda k: (0, 0, k)) for _ in range(4)),
         cost_estimate=pl.CostEstimate(flops=0, bytes_accessed=11_000_000, transcendentals=0),
         name="weight_slices",
     )(place, flat_in, w_out)
@@ -191,56 +172,166 @@
     )(place, bias, own, other, *blocks)
 
 
-def merge_kernel(
-    acc_ref, stat_ref, far_acc_ref, far_stat_ref, own_ref, key_ref, value_ref, bias_ref, out_ref
-):
-    query = jnp.concatenate([own_ref[i, 0:64, :] for i in range(8)], axis=0)
-    bias = bias_ref[...]
-    scores = lax.dot_general(key_ref[...], query, NT, preferred_element_type=F32) * (
-        HEAD_DIM**-0.5
-    ) + jnp.concatenate([bias] * 4, axis=1)
+def split_rows(value):
+    high = value.astype(BF).astype(F32)
+    rest = value - high
+    middle = rest.astype(BF).astype(F32)
+    return [high, middle, rest - middle]
+
+
+def merge_kernel(acc_ref, stat_ref, far_acc_ref, far_stat_ref, out_ref):
     near_top = stat_ref[0:1, :]
     far_top = far_stat_ref[2:3, :]
-    top = jnp.maximum(jnp.maximum(near_top, far_top), jnp.max(scores, axis=0, keepdims=True))
+    top = jnp.maximum(near_top, far_top)
     near = jnp.exp(near_top - top)
     far = jnp.exp(far_top - top)
-    probs = jnp.exp(scores - top)
-    total = (
-        stat_ref[1:2, :] * near
-        + far_stat_ref[3:4, :] * far
-        + jnp.sum(probs, axis=0, keepdims=True)
-    )
-    acc = (
-        acc_ref[...] * near
-        + far_acc_ref[...].astype(F32) * far
-        + lax.dot_general(value_ref[...], probs.astype(BF), TN, preferred_element_type=F32)
-    )
+    total = stat_ref[1:2, :] * near + far_stat_ref[3:4, :] * far
+    acc = acc_ref[...] * near + far_acc_ref[...].astype(F32) * far
     rows = acc.T.astype(BF)
-    tops = []
-    for value in (top, total):
-        high = value.astype(BF)
-        rest = value - high.astype(F32)
-        middle = rest.astype(BF)
-        low = (rest - middle.astype(F32)).astype(BF)
-        tops += [high.astype(F32), middle.astype(F32), low.astype(F32)]
-    stats = jnp.concatenate(tops + [jnp.zeros((10, 512), F32)], axis=0).astype(BF)
+    stats = split_rows(top) + split_rows(total) + [jnp.zeros((10, 512), F32)]
+    stats = jnp.concatenate(stats, axis=0).astype(BF)
     for head in range(8):
         pair = head // 2
         out_ref[head, 0:64, :] = rows[head * 64 : head * 64 + 64, :]
         out_ref[head, 64:80, :] = stats[:, pair * 128 : pair * 128 + 128]
 
 
+VMEM = pl.BlockSpec(memory_space=pltpu.VMEM)
+SMEM = pl.BlockSpec(memory_space=pltpu.SMEM)
+
+
 def merge(*operands):
-    vmem = pl.BlockSpec(memory_space=pltpu.VMEM)
     return pl.pallas_call(
         merge_kernel,
         out_shape=jax.ShapeDtypeStruct((8, 80, 128), BF),
-        in_specs=[vmem] * 8,
-        out_specs=vmem,
+        in_specs=[VMEM] * 4,
+        out_specs=VMEM,
+        cost_estimate=pl.CostEstimate(flops=500_000, bytes_accessed=1_000_000, transcendentals=0),
+        name="merge",
+    )(*operands)
+
+
+def finish_kernel(
+    place_ref, arrived_ref, own_ref, key_ref, value_ref, bias_ref, out_ref, column_ref, new_ref
+):
+    z = place_ref[0]
+    query = own_ref[z, 0:64, :]
+    query = jnp.concatenate([query, query], axis=0)
+    scores = lax.dot_general(key_ref[...], query, NT, preferred_element_type=F32)
+    scores = scores * (HEAD_DIM**-0.5) + bias_ref[...]
+    tops = []
+    sums = []
+    for k in range(8):
+        stat = arrived_ref[k, 64:80, :].astype(F32)
+        tops.append(stat[0:1] + (stat[1:2] + stat[2:3]))
+        sums.append(stat[3:4] + (stat[4:5] + stat[5:6]))
+    tops = jnp.concatenate(tops, axis=0)
+    sums = jnp.concatenate(sums, axis=0)
+    top = jnp.maximum(
+        jnp.max(tops, axis=0, keepdims=True), jnp.max(scores, axis=0, keepdims=True)
+    )
+    by = jnp.exp(tops - top)
+    probs = jnp.exp(scores - top)
+    norm = jnp.sum(sums * by, axis=0, keepdims=True) + jnp.sum(probs, axis=0, keepdims=True)
+    column_ref[...] = jnp.concatenate([by, jnp.broadcast_to(norm, (8, 128))], axis=0).T
+    new_ref[...] = lax.dot_general(
+        probs.astype(BF), value_ref[...], TN, preferred_element_type=F32
+    )
+    mine = pl.ds(pl.multiple_of(lax.rem(z, 2) * 64, 64), 64)
+    column = column_ref[mine, :]
+    acc = new_ref[mine, :]
+    for k in range(8):
+        acc = acc + arrived_ref[k, 0:64, :].astype(F32) * column[:, k : k + 1]
+    result = (acc / column[:, 8:9]).astype(BF)
+    for k in range(8):
+        out_ref[k] = result
+
+
+def finish(*operands):
+    return pl.pallas_call(
+        finish_kernel,
+        out_shape=jax.ShapeDtypeStruct((8, 64, 128), BF),
+        in_specs=[SMEM] + [VMEM] * 5,
+        out_specs=VMEM,
+        scratch_shapes=[pltpu.VMEM((128, 16), F32), pltpu.VMEM((128, 128), F32)],
+        cost_estimate=pl.CostEstimate(flops=20_000_000, bytes_accessed=800_000, transcendentals=0),
+        name="finish",
+    )(*operands)
+
+
+def ffn_in_kernel(p0, p1, p2, p3, own_ref, far_ref, keep_ref, square_ref, s1, s2, s3, feature):
+    pairs = [jnp.zeros((1, 128), F32), jnp.zeros((1, 128), F32)]
+    for rel, ref in enumerate((own_ref, far_ref)):
+        for z in range(NZ):
+            for k in range(4):
+                feature[rel, k * 64 : k * 64 + 64, z * 128 : z * 128 + 128] = ref[
+                    z * 4 + k, 0:64, :
+                ]
+                stat = ref[z * 4 + k, 64:80, :].astype(F32)
+                pairs[k // 2] = pairs[k // 2] + (stat[0:1] + (stat[1:2] + stat[2:3]))
+    squares = jnp.concatenate(pairs, axis=1)
+    square_ref[...] = jnp.broadcast_to(squares, (8, ROWS))
+    rows = jnp.concatenate(split_rows(squares) + [jnp.zeros((13, ROWS), F32)], axis=0).astype(BF)
+    for step, (piece, to) in enumerate(((p1, s1), (p2, s2), (p3, s3), (p0, keep_ref))):
+        value = lax.dot_general(
+            piece[0, 0:224, :], feature[0], NT, preferred_element_type=F32
+        ) + lax.dot_general(piece[1, 0:224, :], feature[1], NT, preferred_element_type=F32)
+        if step < 3:
+            to[0:224, :] = value.astype(BF)
+            to[224:240, :] = rows
+        else:
+            to[...] = value
+
+
+def ffn_in(*operands):
+    sent = jax.ShapeDtypeStruct((240, ROWS), BF)
+    return pl.pallas_call(
+        ffn_in_kernel,
+        out_shape=(
+            jax.ShapeDtypeStruct((224, ROWS), F32),
+            jax.ShapeDtypeStruct((8, ROWS), F32),
+            sent,
+            sent,
+            sent,
+        ),
+        in_specs=[VMEM] * 6,
+        out_specs=(VMEM,) * 5,
+        scratch_shapes=[pltpu.VMEM((2, ROWS, 1024), BF)],
+        compiler_params=pltpu.CompilerParams(vmem_limit_bytes=40 * 1024 * 1024),
         cost_estimate=pl.CostEstimate(
-            flops=4 * 512 * 128 * 32, bytes_accessed=1_000_000, transcendentals=20000
-        ),
-        name="merge",
+            flops=2 * 896 * 2048 * 256, bytes_accessed=7_500_000, transcendentals=0
+        ),
+        name="ffn_in",
+    )(*operands)
+
+
+def ffn_out_kernel(p0, p1, p2, p3, a0, a1, a2, a3, sent_ref, keep_ref):
+    act = jnp.concatenate([a0[...], a1[...], a2[...], a3[...]], axis=0)
+    for rel in (1, 0):
+        weight = jnp.concatenate([p[rel, 224:336, :] for p in (p0, p1, p2, p3)], axis=0)
+        term = lax.dot_general(act, weight, TN, preferred_element_type=F32)
+        for z in range(NZ):
+            block = term[:, z * 128 : z * 128 + 128]
+            if rel == 1:
+                sent_ref[z] = block.astype(BF)
+            else:
+                keep_ref[z] = block
+
+
+def ffn_out(*operands):
+    return pl.pallas_call(
+        ffn_out_kernel,
+        out_shape=(
+            jax.ShapeDtypeStruct((NZ, ROWS, 128), BF),
+            jax.ShapeDtypeStruct((NZ, ROWS, 128), F32),
+        ),
+        in_specs=[VMEM] * 8,
+        out_specs=(VMEM, VMEM),
+        compiler_params=pltpu.CompilerParams(vmem_limit_bytes=40 * 1024 * 1024),
+        cost_estimate=pl.CostEstimate(
+            flops=2 * 448 * 2048 * 256, bytes_accessed=7_500_000, transcendentals=0
+        ),
+        name="ffn_out",
     )(*operands)
 
 
@@ -276,10 +367,6 @@
     )
     theirs = exchange_cores(message)
     weight_theirs = exchange_cores(half(other))
-
-    cache = cache_kv.reshape(DOC_LEN, 512)
-    right, left = shift_x(cache, 1), shift_x(cache, -1)
-    across = shift_x(right, 1)
 
     weight = jnp.concatenate([half(c), weight_theirs], axis=0)
     inputs = jnp.concatenate([hidden_rows, theirs[:ROWS]], axis=1).astype(F32)
@@ -299,6 +386,10 @@
         ],
         axis=2,
     ).reshape(32, 88, 128)
+
+    payload, cache = hold(payload, cache_kv.reshape(DOC_LEN, 512))
+    right, left = shift_x(cache, 1), shift_x(cache, -1)
+    across = shift_x(right, 1)
     total = jnp.sum(swap_zx(payload).astype(F32), axis=0)
     square_sum = (total[80] + (total[81] + total[82]))[:64]
     factor = lax.rsqrt(square_sum / D + EPS)
@@ -311,7 +402,7 @@
         axis=0,
     ).astype(BF)
 
-    place = jnp.stack([c, y]).astype(jnp.int32)
+    place = jnp.stack([c, y, z]).astype(jnp.int32)
     flat_in = jnp.transpose(w_in, (1, 2, 0)).reshape(224, D)
     pieces = weight_slices(place, flat_in, w_out)
     slices = [pieces[0], shift_y(pieces[1], 1), None, shift_y(pieces[3], 3)]
@@ -329,10 +420,14 @@
         written = jnp.any(name[:, None] == sel_index[None, :], axis=1)
         key_pos.append(jnp.where(written, DOC_LEN * POOL * 2, at))
     bias = jnp.where(jnp.concatenate(key_pos)[:, None] <= my_pos, 0.0, NEG).astype(F32)
-    new_pos = lax.dynamic_slice_in_dim(row_pos, z * 32, 32, 0)
-    new_bias = jnp.where(new_pos[:, None] <= my_pos, 0.0, NEG).astype(F32)
-
-    piece, right, left, across, wo, bias = hold(piece, right, left, across, w_output, bias)
+    rel_pos = jnp.concatenate(
+        [lax.dynamic_slice_in_dim(row_pos, ((x - k) % NX) * 64, 64, 0) for k in range(4)]
+    )
+    new_bias = jnp.where(rel_pos[:, None] <= my_pos, 0.0, NEG).astype(F32)
+
+    piece, right, left, across, wo, bias, pieces = hold(
+        piece, right, left, across, w_output, bias, pieces
+    )
     own = swap_z(jnp.broadcast_to(piece[None], (8, 80, 128)))
     wo_right, wo_left = shift_x(wo, 1), shift_x(wo, -1)
     wo_across = shift_x(wo_right, 1)
@@ -342,35 +437,18 @@
 
     new_right, new_left = shift_x(new, 1), shift_x(new, -1)
     new_all = jnp.stack([new, new_right, shift_x(new_right, 1), new_left])
-    new_here = lax.dynamic_index_in_dim(new_all[:, 0], (x - z // 2) % NX, 0, keepdims=False)
-    new_here = lax.dynamic_slice_in_dim(new_here, (z % 2) * 4, 4, 0).reshape(4, 2, 8, 128)
+    new_own = jnp.transpose(new_all[:, 0].reshape(4, 8, 2, 8, 128), (2, 0, 1, 3, 4))
+    new_own = new_own.reshape(2, ROWS, 128)
 
     far_acc = exchange_cores(acc_sent)
     far_stats = exchange_cores(stats)
-    payload = merge(
-        acc,
-        stats,
-        far_acc,
-        far_stats,
-        own,
-        new_here[:, 0].reshape(32, 128),
-        new_here[:, 1].reshape(32, 128),
-        new_bias,
-    )
+    payload = merge(acc, stats, far_acc, far_stats)
     payload, slices[1], slices[3], last = hold(payload, slices[1], slices[3], pieces[2])
     slices[2] = shift_y(last, 2)
-    arrived = swap_z(payload).astype(F32)
-    lane = (z % 2) * 64
-    tops = arrived[:, 64] + (arrived[:, 65] + arrived[:, 66])
-    sums = arrived[:, 67] + (arrived[:, 68] + arrived[:, 69])
-    tops = lax.dynamic_slice_in_dim(tops, lane, 64, 1)
-    sums = lax.dynamic_slice_in_dim(sums, lane, 64, 1)
-    by = jnp.exp(tops - jnp.max(tops, axis=0, keepdims=True))
-    norm = jnp.sum(sums * by, axis=0)
-    summed = jnp.sum(arrived[:, :64] * by[:, :, None], axis=0)
-    piece = (summed / norm[:, None]).astype(BF)
+    arrived = swap_z(payload)
+    piece = finish(place[2:], arrived, own, new_own[0], new_own[1], new_bias)
     piece, wo_right, wo_left, wo_across = hold(piece, wo_right, wo_left, wo_across)
-    attended = swap_z(jnp.broadcast_to(piece[None], (8, 64, 128)))
+    attended = swap_z(piece)
     attended_theirs = exchange_cores(attended)
 
     def flat(value):
@@ -397,9 +475,15 @@
         sent = lax.dynamic_index_in_dim(chunks, (x - y - step) % NX, 0, keepdims=False)
         mid = mid + shift_y(sent, step).astype(F32)
     feature = (mid * early[64].astype(F32)[None, :]).astype(BF)
-    square_parts = jnp.stack(parts_of(jnp.sum(mid * mid, axis=1)) + [jnp.zeros((64,), BF)] * 5)
-    payload = jnp.concatenate([feature, jnp.pad(square_parts, ((0, 0), (0, 64)))], axis=0)
-    arrived = swap_zx(jnp.broadcast_to(payload[None], (32, 72, 128)))
+    square_parts = jnp.stack(parts_of(jnp.sum(mid * mid, axis=1)) + [jnp.zeros((64,), BF)] * 13)
+    empty = jnp.zeros_like(square_parts)
+    square_parts = jnp.where(
+        x % 2 == 0,
+        jnp.concatenate([square_parts, empty], axis=1),
+        jnp.concatenate([empty, square_parts], axis=1),
+    )
+    payload = jnp.concatenate([feature, square_parts], axis=0)
+    arrived = swap_zx(jnp.broadcast_to(payload[None], (32, 80, 128)))
     arrived_theirs = exchange_cores(arrived)
 
     reordered = cache.reshape(POOL, 8, 512).at[doc_order].get(mode="promise_in_bounds")
@@ -413,44 +497,19 @@
     arrived, cache_out = hold(arrived, cache_out)
     slot_cache = swap_zx(cache_out)
 
-    def features_of(block):
-        return jnp.transpose(block[:, :64].reshape(NZ, ROWS, 128), (1, 0, 2)).reshape(ROWS, 1024)
-
-    def squares_of(block):
-        parts = jnp.sum(block[:, 64:67, :64].astype(F32), axis=1)
-        return jnp.sum(parts.reshape(NZ, ROWS), axis=0)
-
-    feature_own = features_of(arrived)
-    feature_theirs = features_of(arrived_theirs)
-    square_sum = squares_of(arrived) + squares_of(arrived_theirs)
-    square_rows = jnp.stack(parts_of(square_sum) + [jnp.zeros((ROWS,), BF)] * 5)
-    hidden = []
-    for step in range(4):
-        term = lax.dot_general(
-            slices[step][:224, :1024], feature_own, NT, preferred_element_type=F32
-        ) + lax.dot_general(
-            slices[step][:224, 1024:], feature_theirs, NT, preferred_element_type=F32
-        )
-        hidden.append(term)
-    both = hidden[0]
+    both, squares, *sent = ffn_in(*slices, arrived, arrived_theirs)
+    square_sum = squares[0]
     for step in range(1, 4):
-        sent = jnp.concatenate([hidden[step].astype(BF), square_rows], axis=0)
-        got = shift_y(sent, -step).astype(F32)
+        got = shift_y(sent[step - 1], -step).astype(F32)
         both = both + got[:224]
         square_sum = square_sum + (got[224] + (got[225] + got[226]))
     both = both * lax.rsqrt(square_sum / D + EPS)[None, :]
     act = (jax.nn.silu(both[:112]) * both[112:]).astype(BF)
     acts = [act] + [shift_y(act, step) for step in range(1, 4)]
-    act_all = jnp.concatenate(acts, axis=0)
-    out_all = jnp.concatenate([item[224:] for item in slices], axis=0)
-    term_theirs = lax.dot_general(act_all, out_all[:, 1024:], TN, preferred_element_type=F32)
-    got = exchange_cores(term_theirs.astype(BF))
-    term = lax.dot_general(act_all, out_all[:, :1024], TN, preferred_element_type=F32)
-    term = (term + got.astype(F32)).astype(BF)
-    payload = jnp.transpose(term.reshape(ROWS, NZ, 128), (1, 0, 2)).reshape(32, 64, 128)
+    sent, keep = ffn_out(*slices, *acts)
+    payload = (keep + exchange_cores(sent).astype(F32)).astype(BF).reshape(32, 64, 128)
     payload, slot_cache = hold(payload, slot_cache)
     down = jnp.sum(swap_zx(payload).astype(F32), axis=0)
-    result = permute_xy((mid + down).astype(BF), lambda a, b: (b, a))
 
     sel_key = jnp.where(row_pos // DOC_LEN == mine, row_pos % DOC_LEN, -1)
     sel_key = jnp.concatenate(
@@ -463,7 +522,10 @@
     new_flat = jnp.transpose(new_flat, (0, 2, 4, 3, 1, 5)).reshape(ROWS, 512)
     placed = jnp.dot(hits.astype(BF), new_flat, preferred_element_type=F32).astype(BF)
     joined = jnp.where(covered[:, None], placed, slot_cache.reshape(DOC_LEN, 512))
-    return (result, joined.reshape(DOC_LEN, 2, 256))
+    joined = joined.reshape(DOC_LEN, 2, 256)
+    down, joined = hold(down, joined)
+    result = permute_xy((mid + down).astype(BF), lambda a, b: (b, a))
+    return (result, joined)
 
 
 def solution(mesh):

time: 429 us -> 264 us (0.62)
  Pallas kernels: 177 us -> 23.3 us
  starting transfers between devices: 104 us -> 90.9 us
  matrix products: 14.8 us -> 4.84 us
  other arithmetic: 11.7 us -> 19.7 us
  local copies, waits for them, and re-layouts: 25.2 us -> 30 us
    pallas_call x1 -> x4, Pallas kernels: 170 us -> 15.9 us  [the longest x1 7.85 us: weight_slices(): pl.pallas_call(slices_kernel, grid=(NZ,), out_shape=tuple((jax.ShapeDtype...]
    all_to_all x4, waiting for transfers between devices: 49 us -> 27.2 us  [swap_zx(): return lax.all_to_all(value, ('z', 'x'), 0, 0, tiled=True)]
    ppermute x9, waiting for transfers between devices: 12.1 us -> 28.8 us  [shift_x(): return lax.ppermute(value, 'x', [(i, (i + step) % NX) for i in range(NX)])]
    dot_general x10 -> x0, matrix products: 12.6 us -> none  [the longest x4 5.28 us: shards(): lax.dot_general(slices[step][:224, 1024:], feature_theirs, NT, preferred_...]
    all_to_all x3, waiting for transfers between devices: 5.68 us -> 17.2 us  [swap_z(): return lax.all_to_all(value, 'z', 0, 0, tiled=True)]
    ppermute x12, starting transfers between devices: 24.7 us -> 14.6 us  [shift_y(): return lax.ppermute(value, 'y', [(i, (i + step) % NY) for i in range(NY)])]
    unnamed x60 -> x86, local copies, waits for them, and re-layouts: 7.94 us -> 15 us
    slice x8 -> x1, local copies, waits for them, and re-layouts: 5.33 us -> 0.67 us  [shards(): piece = finish(place[2:], arrived, own, new_own[0], new_own[1], new_bias)]
  transfers between devices with their start and end apart: 39 -> 39, of which waited for: 20 -> 21; matrix products, arithmetic and copies ran while one was open for 9% -> 17% of each run, Pallas kernels for 42% -> 8%
where the time goes in v3:
time: 264 us; the launch traced here: 262 us
  waiting for transfers between devices  92 us (35%)
  starting transfers between devices  90.9 us (34%)
  local copies, waits for them, and re-layouts  30 us (11%)
  Pallas kernels  23.3 us (9%)
  other arithmetic  19.7 us (7%)
  matrix products  4.84 us (2%)
    all_to_all x4, starting transfers between devices, swap_zx(): return lax.all_to_all(value, ('z', 'x'), 0, 0, tiled=True)  38 us
    ppermute x9, waiting for transfers between devices, shift_x(): return lax.ppermute(value, 'x', [(i, (i + step) % NX) for i in range(NX)])  28.8 us
    all_to_all x4, waiting for transfers between devices, swap_zx(): return lax.all_to_all(value, ('z', 'x'), 0, 0, tiled=True)  27.2 us
    all_to_all x3, waiting for transfers between devices, swap_z(): return lax.all_to_all(value, 'z', 0, 0, tiled=True)  17.2 us
    unnamed x86, local copies, waits for them, and re-layouts  15 us
    ppermute x12, starting transfers between devices, shift_y(): return lax.ppermute(value, 'y', [(i, (i + step) % NY) for i in range(NY)])  14.6 us
    all_to_all x3, starting transfers between devices, swap_z(): return lax.all_to_all(value, 'z', 0, 0, tiled=True)  14.4 us
    ppermute x9, starting transfers between devices, shift_x(): return lax.ppermute(value, 'x', [(i, (i + step) % NX) for i in range(NX)])  12.7 us
  transfers between devices with their start and end apart: 39, of which 21 were waited for; matrix products, arithmetic and copies ran while one was open for 17% of the time, Pallas kernels for 8%

profile of v3, /device:TPU:4, one launch (start us, length us, event | category | flops | bytes accessed | tf_op | source)
XLA Modules:
  0.0 262.4 jit_solution(5675992419172084531)
XLA Ops:
  5.6 7.9 %weight_slices.1 = (bf16[2,336,1024]{2,1,0:T(8,128)(2,1)}, bf16[2,336,1024]{2,1,0:T(8,128)(2,1)}, bf16[2,336,1024]{2,1,0:T(8,128)(2,1)}, bf16[2,336,1024]{2,1,0:T(8,128)(2,1)}) custom-call(s32[3]{0:T(128)} %pad_add_fusion.4.place_ref, bf16[224,8192]{1,0:T(8,128)(2,1)} %bitcast.150, bf16[112,8192]{1,0:T(8,128)(2,1)} %out_ref.1), custom_call_target="tpu_custom_call" | custom-call | bytes 11000000 | tf_op jit(solution)/shard_map/weight_slices/pallas_call | solution.py:96
  13.4 3.1 %collective-permute-start.10 = (bf16[2,336,1024]{2,1,0:T(8,128)(2,1)}, bf16[2,336,1024]{2,1,0:T(8,128)(2,1)S(1)}, u32[]{:S(2)}, u32[]{:S(2)}) collective-permute-start(bf16[2,336,1024]{2,1,0:T(8,128)(2,1)} %get-tuple-element.46), channel_id=1, source_target_pairs={{0,3},{1,0},{2,1},{3,2},{4,7},{5,4},{6,5},{7,6},{8,11},{9,8},{10,9... | collective-permute-start | bytes 4128776 | tf_op jit(solution)/shard_map/ppermute | solution.py:31
  28.1 11.8 %all-to-all-start = ((bf16[32,88,128]{2,1,0:T(8,128)(2,1)}), bf16[32,88,128]{2,1,0:T(8,128)(2,1)}, u32[]{:S(2)}, u32[]{:S(2)}) async-start(bf16[32,88,128]{2,1,0:T(8,128)(2,1)} %pad_maximum_fusion), calls=%async_computation | async-start | bytes 1441792 | tf_op jit(solution)/shard_map/all_to_all | solution.py:44
  43.9 16.3 %collective-permute-done.3.c1 = bf16[512,512]{1,0:T(8,128)(2,1)} collective-permute-done((bf16[512,512]{1,0:T(8,128)(2,1)S(1)}, bf16[512,512]{1,0:T(8,128)(2,1)}, u32[]{:S(2)}, u32[]{:S(2)}) %collective-permute-start.3) | collective-permute-done | bytes 524320 | tf_op jit(solution)/shard_map/ppermute | solution.py:56
  63.3 10.0 %collective-permute-done.5.c3 = bf16[512,512]{1,0:T(8,128)(2,1)} collective-permute-done((bf16[512,512]{1,0:T(8,128)(2,1)}, bf16[512,512]{1,0:T(8,128)(2,1)}, u32[]{:S(2)}, u32[]{:S(2)}) %collective-permute-start.5) | collective-permute-done | bytes 524320 | tf_op jit(solution)/shard_map/ppermute | solution.py:56
  73.9 6.9 %all-to-all-start.1 = ((bf16[8,80,128]{2,1,0:T(8,128)(2,1)}), bf16[8,80,128]{2,1,0:T(8,128)(2,1)S(1)}, u32[]{:S(2)}, u32[]{:S(2)}) async-start(bf16[8,80,128]{2,1,0:T(8,128)(2,1)} %broadcast_in_dim.75), calls=%async_computation.1 | async-start | bytes 327680 | tf_op jit(solution)/shard_map/all_to_all | solution.py:60
  81.6 1.9 constant_dynamic-update-slice_fusion.3
  85.2 5.1 %all-to-all-done.1.own_ref = bf16[8,80,128]{2,1,0:T(8,128)(2,1)S(1)} async-done(((bf16[8,80,128]{2,1,0:T(8,128)(2,1)}), bf16[8,80,128]{2,1,0:T(8,128)(2,1)S(1)}, u32[]{:S(2)}, u32[]{:S(2)}) %all-to-all-start.1) | async-done | bytes 163872 | tf_op jit(solution)/shard_map/all_to_all | solution.py:60
  92.9 5.6 %attend.1 = (f32[128,512]{1,0:T(8,128)S(1)}, bf16[128,512]{1,0:T(8,128)(2,1)S(1)}, f32[8,512]{1,0:T(8,128)S(1)}) custom-call(s32[3]{0:T(128)S(1)} %copy-done.13, f32[2048,128]{1,0:T(8,128)S(1)} %copy-done.6, bf16[8,80,128]{2,1,0:T(8,128)(2,1)S(1)} %all-to-all-done.1.own_ref, bf16[8,80,128]{2,1,0:T(8,128)(2,1)S(1)} %collective-permute-done.6.other_ref, ...), custom_call_target="tpu_custom_call" | custom-call | flops 1073741824 | bytes 6000000 | tf_op jit(solution)/shard_map/attend/pallas_call | solution.py:158
  102.5 3.4 %collective-permute-start.16 = (bf16[2048,128]{1,0:T(8,128)(2,1)}, bf16[2048,128]{1,0:T(8,128)(2,1)}, u32[]{:S(2)}, u32[]{:S(2)}) collective-permute-start(bf16[2048,128]{1,0:T(8,128)(2,1)} %collective-permute-done.14), channel_id=1, source_target_pairs={{0,8},{8,16},{16,24},{24,0},{1,9},{9,17},{17,25},{25,1},{2,10},{10... | collective-permute-start | bytes 1572872 | tf_op jit(solution)/shard_map/ppermute | solution.py:56
  105.9 2.5 collective-permute-done.11
  108.4 2.1 collective-permute-start.13
  113.0 5.3 %collective-permute-start = (bf16[80,128]{1,0:T(8,128)(2,1)}, bf16[80,128]{1,0:T(8,128)(2,1)S(1)}, u32[]{:S(2)}, u32[]{:S(2)}) collective-permute-start(bf16[80,128]{1,0:T(8,128)(2,1)} %pad_maximum_fusion.11), channel_id=1, source_target_pairs={{0,0},{1,8},{2,16},{3,24},{8,1},{9,9},{10,17},{11,25},{16,2},{17,1... | collective-permute-start | bytes 61448 | tf_op jit(solution)/shard_map/ppermute | solution.py:40
  118.3 4.1 %all-to-all-start.2 = ((bf16[8,80,128]{2,1,0:T(8,128)(2,1)}), bf16[8,80,128]{2,1,0:T(8,128)(2,1)S(1)}, u32[]{:S(2)}, u32[]{:S(2)}) async-start(bf16[8,80,128]{2,1,0:T(8,128)(2,1)} %merge.1), calls=%async_computation.2 | async-start | bytes 327680 | tf_op jit(solution)/shard_map/all_to_all | solution.py:60
  124.0 7.8 %all-to-all-done.2.arrived_ref = bf16[8,80,128]{2,1,0:T(8,128)(2,1)S(1)} async-done(((bf16[8,80,128]{2,1,0:T(8,128)(2,1)}), bf16[8,80,128]{2,1,0:T(8,128)(2,1)S(1)}, u32[]{:S(2)}, u32[]{:S(2)}) %all-to-all-start.2) | async-done | bytes 163872 | tf_op jit(solution)/shard_map/all_to_all | solution.py:60
  132.5 2.4 finish.1
  134.9 3.4 %all-to-all-start.3 = ((bf16[8,64,128]{2,1,0:T(8,128)(2,1)}), bf16[8,64,128]{2,1,0:T(8,128)(2,1)S(1)}, u32[]{:S(2)}, u32[]{:S(2)}) async-start(bf16[8,64,128]{2,1,0:T(8,128)(2,1)} %finish.1), calls=%async_computation.3 | async-start | bytes 262144 | tf_op jit(solution)/shard_map/all_to_all | solution.py:60
  140.1 1.9 constant_dynamic-update-slice_fusion.1
  143.0 4.3 %all-to-all-done.3 = bf16[8,64,128]{2,1,0:T(8,128)(2,1)S(1)} async-done(((bf16[8,64,128]{2,1,0:T(8,128)(2,1)}), bf16[8,64,128]{2,1,0:T(8,128)(2,1)S(1)}, u32[]{:S(2)}, u32[]{:S(2)}) %all-to-all-start.3) | async-done | bytes 131104 | tf_op jit(solution)/shard_map/all_to_all | solution.py:60
  150.4 3.5 %collective-permute-done.18.p2 = bf16[2,336,1024]{2,1,0:T(8,128)(2,1)} collective-permute-done((bf16[2,336,1024]{2,1,0:T(8,128)(2,1)}, bf16[2,336,1024]{2,1,0:T(8,128)(2,1)}, u32[]{:S(2)}, u32[]{:S(2)}) %collective-permute-start.18) | collective-permute-done | bytes 1376288 | tf_op jit(solution)/shard_map/ppermute | solution.py:31
  161.2 10.7 %all-to-all-start.4 = ((bf16[32,80,128]{2,1,0:T(8,128)(2,1)}), bf16[32,80,128]{2,1,0:T(8,128)(2,1)S(1)}, u32[]{:S(2)}, u32[]{:S(2)}) async-start(bf16[32,80,128]{2,1,0:T(8,128)(2,1)} %broadcast_in_dim.78), calls=%async_computation.4 | async-start | bytes 1310720 | tf_op jit(solution)/shard_map/all_to_all | solution.py:44
  173.4 13.1 %all-to-all-done.4.own_ref = bf16[32,80,128]{2,1,0:T(8,128)(2,1)S(1)} async-done(((bf16[32,80,128]{2,1,0:T(8,128)(2,1)}), bf16[32,80,128]{2,1,0:T(8,128)(2,1)S(1)}, u32[]{:S(2)}, u32[]{:S(2)}) %all-to-all-start.4) | async-done | bytes 655392 | tf_op jit(solution)/shard_map/all_to_all | solution.py:44
  193.4 3.6 %ffn_in.1 = (f32[224,256]{1,0:T(8,128)S(1)}, f32[8,256]{1,0:T(8,128)S(1)}, bf16[240,256]{1,0:T(8,128)(2,1)}, bf16[240,256]{1,0:T(8,128)(2,1)}, bf16[240,256]{1,0:T(8,128)(2,1)S(1)}) custom-call(bf16[2,336,1024]{2,1,0:T(8,128)(2,1)S(1)} %copy-done, bf16[2,336,1024]{2,1,0:T(8,128)(2,1)S(1)} %copy-done.2, bf16[2,336,1024]{2,1,0:T(8,128)(2,1)} %collective-permute-done.18.p2, ...), custom_call_target="tpu_custom_call" | custom-call | flops 939524096 | bytes 7500000 | tf_op jit(solution)/shard_map/ffn_in/pallas_call | solution.py:288
  197.7 2.7 %collective-permute-start.24 = (bf16[240,256]{1,0:T(8,128)(2,1)}, bf16[240,256]{1,0:T(8,128)(2,1)}, u32[]{:S(2)}, u32[]{:S(2)}) collective-permute-start(bf16[240,256]{1,0:T(8,128)(2,1)} %get-tuple-element.69), channel_id=1, source_target_pairs={{0,3},{1,0},{2,1},{3,2},{4,7},{5,4},{6,5},{7,6},{8,11},{9,8},{10,9... | collective-permute-start | bytes 368648 | tf_op jit(solution)/shard_map/ppermute | solution.py:31
  201.3 5.8 %all-to-all-start.5 = ((bf16[32,16,512]{2,1,0:T(8,128)(2,1)}), bf16[32,16,512]{2,1,0:T(8,128)(2,1)}, u32[]{:S(2)}, u32[]{:S(2)}) async-start(bf16[32,16,512]{2,1,0:T(8,128)(2,1)} %pad_maximum_fusion.1), calls=%async_computation.5 | async-start | bytes 1048576 | tf_op jit(solution)/shard_map/all_to_all | solution.py:44
  212.0 1.9 collective-permute-start.28
  218.1 2.1 ffn_out.1
  223.1 2.2 add_convert_fusion
  225.3 9.7 %all-to-all-start.6 = ((bf16[32,64,128]{2,1,0:T(8,128)(2,1)}), bf16[32,64,128]{2,1,0:T(8,128)(2,1)S(1)}, u32[]{:S(2)}, u32[]{:S(2)}) async-start(bf16[32,64,128]{2,1,0:T(8,128)(2,1)} %bitcast.43), calls=%async_computation.6 | async-start | bytes 1048576 | tf_op jit(solution)/shard_map/all_to_all | solution.py:44
  238.0 14.1 %all-to-all-done.6 = bf16[32,64,128]{2,1,0:T(8,128)(2,1)S(1)} async-done(((bf16[32,64,128]{2,1,0:T(8,128)(2,1)}), bf16[32,64,128]{2,1,0:T(8,128)(2,1)S(1)}, u32[]{:S(2)}, u32[]{:S(2)}) %all-to-all-start.6) | async-done | bytes 524320 | tf_op jit(solution)/shard_map/all_to_all | solution.py:44
  252.2 4.3 %collective-permute-start.31 = (bf16[64,128]{1,0:T(8,128)(2,1)S(1)}, bf16[64,128]{1,0:T(8,128)(2,1)S(1)}, u32[]{:S(2)}, u32[]{:S(2)}) collective-permute-start(bf16[64,128]{1,0:T(8,128)(2,1)S(1)} %add_convert_fusion.1), channel_id=1, source_target_pairs={{0,0},{1,8},{2,16},{3,24},{8,1},{9,9},{10,17},{11,25},{16,2},{17,1... | collective-permute-start | bytes 49160 | tf_op jit(solution)/shard_map/ppermute | solution.py:40
  257.7 4.1 %collective-permute-done.31 = bf16[64,128]{1,0:T(8,128)(2,1)S(1)} collective-permute-done((bf16[64,128]{1,0:T(8,128)(2,1)S(1)}, bf16[64,128]{1,0:T(8,128)(2,1)S(1)}, u32[]{:S(2)}, u32[]{:S(2)}) %collective-permute-start.31) | collective-permute-done | bytes 16416 | tf_op jit(solution)/shard_map/ppermute | solution.py:40
  (262 shorter events, 77.3 us)
Async XLA Ops:
  3.8 21.5 %collective-permute-start.2 = (bf16[128,1280]{1,0:T(8,128)(2,1)}, bf16[128,1280]{1,0:T(8,128)(2,1)}, u32[]{:S(2)}, u32[]{:S(2)}) collective-permute-start(bf16[128,1280]{1,0:T(8,128)(2,1)} %pad_maximum_fusion.2), channel_id=1, source_target_pairs={{0,4},{4,0},{1,5},{5,1},{2,6},{6,2},{3,7},{7,3},{8,12},{12,8},{9,1... | collective-permute-start | bytes 983048 | tf_op jit(solution)/shard_map/ppermute | solution.py:27
  4.4 18.4 %collective-permute-start.1 = (bf16[272,128]{1,0:T(8,128)(2,1)}, bf16[272,128]{1,0:T(8,128)(2,1)}, u32[]{:S(2)}, u32[]{:S(2)}) collective-permute-start(bf16[272,128]{1,0:T(8,128)(2,1)} %pad_maximum_fusion.9), channel_id=1, source_target_pairs={{0,4},{4,0},{1,5},{5,1},{2,6},{6,2},{3,7},{7,3},{8,12},{12,8},{9,1... | collective-permute-start | bytes 208904 | tf_op jit(solution)/shard_map/ppermute | solution.py:27
  13.4 87.0 %collective-permute-start.10 = (bf16[2,336,1024]{2,1,0:T(8,128)(2,1)}, bf16[2,336,1024]{2,1,0:T(8,128)(2,1)S(1)}, u32[]{:S(2)}, u32[]{:S(2)}) collective-permute-start(bf16[2,336,1024]{2,1,0:T(8,128)(2,1)} %get-tuple-element.46), channel_id=1, source_target_pairs={{0,3},{1,0},{2,1},{3,2},{4,7},{5,4},{6,5},{7,6},{8,11},{9,8},{10,9... | collective-permute-start | bytes 4128776 | tf_op jit(solution)/shard_map/ppermute | solution.py:31
  16.5 96.4 %collective-permute-start.9 = (bf16[2,336,1024]{2,1,0:T(8,128)(2,1)}, bf16[2,336,1024]{2,1,0:T(8,128)(2,1)S(1)}, u32[]{:S(2)}, u32[]{:S(2)}) collective-permute-start(bf16[2,336,1024]{2,1,0:T(8,128)(2,1)} %get-tuple-element.44), channel_id=1, source_target_pairs={{0,1},{1,2},{2,3},{3,0},{4,5},{5,6},{6,7},{7,4},{8,9},{9,10},{10,1... | collective-permute-start | bytes 4128776 | tf_op jit(solution)/shard_map/ppermute | solution.py:31
  28.1 33.6 %all-to-all-start = ((bf16[32,88,128]{2,1,0:T(8,128)(2,1)}), bf16[32,88,128]{2,1,0:T(8,128)(2,1)}, u32[]{:S(2)}, u32[]{:S(2)}) async-start(bf16[32,88,128]{2,1,0:T(8,128)(2,1)} %pad_maximum_fusion), calls=%async_computation | async-start | bytes 1441792 | tf_op jit(solution)/shard_map/all_to_all | solution.py:44
  40.3 19.9 %collective-permute-start.3 = (bf16[512,512]{1,0:T(8,128)(2,1)S(1)}, bf16[512,512]{1,0:T(8,128)(2,1)}, u32[]{:S(2)}, u32[]{:S(2)}) collective-permute-start(bf16[512,512]{1,0:T(8,128)(2,1)S(1)} %bitcast.146), channel_id=1, source_target_pairs={{0,8},{8,16},{16,24},{24,0},{1,9},{9,17},{17,25},{25,1},{2,10},{10... | collective-permute-start | bytes 1572872 | tf_op jit(solution)/shard_map/ppermute | solution.py:56
  43.0 20.2 %collective-permute-start.4 = (bf16[512,512]{1,0:T(8,128)(2,1)S(1)}, bf16[512,512]{1,0:T(8,128)(2,1)}, u32[]{:S(2)}, u32[]{:S(2)}) collective-permute-start(bf16[512,512]{1,0:T(8,128)(2,1)S(1)} %bitcast.147), channel_id=1, source_target_pairs={{0,24},{8,0},{16,8},{24,16},{1,25},{9,1},{17,9},{25,17},{2,26},{10... | collective-permute-start | bytes 1572872 | tf_op jit(solution)/shard_map/ppermute | solution.py:56
  60.2 13.0 %collective-permute-start.5 = (bf16[512,512]{1,0:T(8,128)(2,1)}, bf16[512,512]{1,0:T(8,128)(2,1)}, u32[]{:S(2)}, u32[]{:S(2)}) collective-permute-start(bf16[512,512]{1,0:T(8,128)(2,1)} %collective-permute-done.3.c1), channel_id=1, source_target_pairs={{0,8},{8,16},{16,24},{24,0},{1,9},{9,17},{17,25},{25,1},{2,10},{10... | collective-permute-start | bytes 1572872 | tf_op jit(solution)/shard_map/ppermute | solution.py:56
  73.9 16.4 %all-to-all-start.1 = ((bf16[8,80,128]{2,1,0:T(8,128)(2,1)}), bf16[8,80,128]{2,1,0:T(8,128)(2,1)S(1)}, u32[]{:S(2)}, u32[]{:S(2)}) async-start(bf16[8,80,128]{2,1,0:T(8,128)(2,1)} %broadcast_in_dim.75), calls=%async_computation.1 | async-start | bytes 327680 | tf_op jit(solution)/shard_map/all_to_all | solution.py:60
  83.5 19.0 %collective-permute-start.14 = (bf16[2048,128]{1,0:T(8,128)(2,1)}, bf16[2048,128]{1,0:T(8,128)(2,1)}, u32[]{:S(2)}, u32[]{:S(2)}) collective-permute-start(bf16[2048,128]{1,0:T(8,128)(2,1)} %param.18), channel_id=1, source_target_pairs={{0,8},{8,16},{16,24},{24,0},{1,9},{9,17},{17,25},{25,1},{2,10},{10... | collective-permute-start | bytes 1572872 | tf_op jit(solution)/shard_map/ppermute | solution.py:56
  98.6 11.9 %collective-permute-start.7 = (bf16[128,512]{1,0:T(8,128)(2,1)S(1)}, bf16[128,512]{1,0:T(8,128)(2,1)S(1)}, u32[]{:S(2)}, u32[]{:S(2)}) collective-permute-start(bf16[128,512]{1,0:T(8,128)(2,1)S(1)} %get-tuple-element.54), channel_id=1, source_target_pairs={{0,4},{4,0},{1,5},{5,1},{2,6},{6,2},{3,7},{7,3},{8,12},{12,8},{9,1... | collective-permute-start | bytes 393224 | tf_op jit(solution)/shard_map/ppermute | solution.py:27
  100.5 34.4 %collective-permute-start.15 = (bf16[2048,128]{1,0:T(8,128)(2,1)}, bf16[2048,128]{1,0:T(8,128)(2,1)S(1)}, u32[]{:S(2)}, u32[]{:S(2)}) collective-permute-start(bf16[2048,128]{1,0:T(8,128)(2,1)} %param.18), channel_id=1, source_target_pairs={{0,24},{8,0},{16,8},{24,16},{1,25},{9,1},{17,9},{25,17},{2,26},{10... | collective-permute-start | bytes 1572872 | tf_op jit(solution)/shard_map/ppermute | solution.py:56
  102.3 6.2 %collective-permute-start.11 = (bf16[2,8,16,128]{3,2,1,0:T(8,128)(2,1)}, bf16[2,8,16,128]{3,2,1,0:T(8,128)(2,1)}, u32[]{:S(2)}, u32[]{:S(2)}) collective-permute-start(bf16[2,8,16,128]{3,2,1,0:T(8,128)(2,1)} %get-tuple-element.116), channel_id=1, source_target_pairs={{0,8},{8,16},{16,24},{24,0},{1,9},{9,17},{17,25},{25,1},{2,10},{10... | collective-permute-start | bytes 196616 | tf_op jit(solution)/shard_map/ppermute | solution.py:56
  102.5 32.4 %collective-permute-start.16 = (bf16[2048,128]{1,0:T(8,128)(2,1)}, bf16[2048,128]{1,0:T(8,128)(2,1)}, u32[]{:S(2)}, u32[]{:S(2)}) collective-permute-start(bf16[2048,128]{1,0:T(8,128)(2,1)} %collective-permute-done.14), channel_id=1, source_target_pairs={{0,8},{8,16},{16,24},{24,0},{1,9},{9,17},{17,25},{25,1},{2,10},{10... | collective-permute-start | bytes 1572872 | tf_op jit(solution)/shard_map/ppermute | solution.py:56
  108.4 14.0 %collective-permute-start.13 = (bf16[2,8,16,128]{3,2,1,0:T(8,128)(2,1)}, bf16[2,8,16,128]{3,2,1,0:T(8,128)(2,1)S(1)}, u32[]{:S(2)}, u32[]{:S(2)}) collective-permute-start(bf16[2,8,16,128]{3,2,1,0:T(8,128)(2,1)} %get-tuple-element.116), channel_id=1, source_target_pairs={{0,24},{8,0},{16,8},{24,16},{1,25},{9,1},{17,9},{25,17},{2,26},{10... | collective-permute-start | bytes 196616 | tf_op jit(solution)/shard_map/ppermute | solution.py:56
  110.5 12.0 %collective-permute-start.12 = (bf16[2,8,16,128]{3,2,1,0:T(8,128)(2,1)}, bf16[2,8,16,128]{3,2,1,0:T(8,128)(2,1)}, u32[]{:S(2)}, u32[]{:S(2)}) collective-permute-start(bf16[2,8,16,128]{3,2,1,0:T(8,128)(2,1)} %collective-permute-done.11), channel_id=1, source_target_pairs={{0,8},{8,16},{16,24},{24,0},{1,9},{9,17},{17,25},{25,1},{2,10},{10... | collective-permute-start | bytes 196616 | tf_op jit(solution)/shard_map/ppermute | solution.py:56
  113.0 44.2 %collective-permute-start = (bf16[80,128]{1,0:T(8,128)(2,1)}, bf16[80,128]{1,0:T(8,128)(2,1)S(1)}, u32[]{:S(2)}, u32[]{:S(2)}) collective-permute-start(bf16[80,128]{1,0:T(8,128)(2,1)} %pad_maximum_fusion.11), channel_id=1, source_target_pairs={{0,0},{1,8},{2,16},{3,24},{8,1},{9,9},{10,17},{11,25},{16,2},{17,1... | collective-permute-start | bytes 61448 | tf_op jit(solution)/shard_map/ppermute | solution.py:40
  118.3 13.5 %all-to-all-start.2 = ((bf16[8,80,128]{2,1,0:T(8,128)(2,1)}), bf16[8,80,128]{2,1,0:T(8,128)(2,1)S(1)}, u32[]{:S(2)}, u32[]{:S(2)}) async-start(bf16[8,80,128]{2,1,0:T(8,128)(2,1)} %merge.1), calls=%async_computation.2 | async-start | bytes 327680 | tf_op jit(solution)/shard_map/all_to_all | solution.py:60
  122.4 31.4 %collective-permute-start.18 = (bf16[2,336,1024]{2,1,0:T(8,128)(2,1)}, bf16[2,336,1024]{2,1,0:T(8,128)(2,1)}, u32[]{:S(2)}, u32[]{:S(2)}) collective-permute-start(bf16[2,336,1024]{2,1,0:T(8,128)(2,1)} %get-tuple-element.62), channel_id=1, source_target_pairs={{0,2},{1,3},{2,0},{3,1},{4,6},{5,7},{6,4},{7,5},{8,10},{9,11},{10,... | collective-permute-start | bytes 4128776 | tf_op jit(solution)/shard_map/ppermute | solution.py:31
  134.9 12.4 %all-to-all-start.3 = ((bf16[8,64,128]{2,1,0:T(8,128)(2,1)}), bf16[8,64,128]{2,1,0:T(8,128)(2,1)S(1)}, u32[]{:S(2)}, u32[]{:S(2)}) async-start(bf16[8,64,128]{2,1,0:T(8,128)(2,1)} %finish.1), calls=%async_computation.3 | async-start | bytes 262144 | tf_op jit(solution)/shard_map/all_to_all | solution.py:60
  153.9 5.0 %collective-permute-start.19 = (bf16[64,128]{1,0:T(8,128)(2,1)S(1)}, bf16[64,128]{1,0:T(8,128)(2,1)S(1)}, u32[]{:S(2)}, u32[]{:S(2)}) collective-permute-start(bf16[64,128]{1,0:T(8,128)(2,1)S(1)} %get-tuple-element.112), channel_id=1, source_target_pairs={{0,1},{1,2},{2,3},{3,0},{4,5},{5,6},{6,7},{7,4},{8,9},{9,10},{10,1... | collective-permute-start | bytes 49160 | tf_op jit(solution)/shard_map/ppermute | solution.py:31
  154.0 5.6 %collective-permute-start.20 = (bf16[64,128]{1,0:T(8,128)(2,1)S(1)}, bf16[64,128]{1,0:T(8,128)(2,1)S(1)}, u32[]{:S(2)}, u32[]{:S(2)}) collective-permute-start(bf16[64,128]{1,0:T(8,128)(2,1)S(1)} %get-tuple-element.114), channel_id=1, source_target_pairs={{0,2},{1,3},{2,0},{3,1},{4,6},{5,7},{6,4},{7,5},{8,10},{9,11},{10,... | collective-permute-start | bytes 49160 | tf_op jit(solution)/shard_map/ppermute | solution.py:31
  161.2 25.2 %all-to-all-start.4 = ((bf16[32,80,128]{2,1,0:T(8,128)(2,1)}), bf16[32,80,128]{2,1,0:T(8,128)(2,1)S(1)}, u32[]{:S(2)}, u32[]{:S(2)}) async-start(bf16[32,80,128]{2,1,0:T(8,128)(2,1)} %broadcast_in_dim.78), calls=%async_computation.4 | async-start | bytes 1310720 | tf_op jit(solution)/shard_map/all_to_all | solution.py:44
  186.4 5.6 %collective-permute-start.23 = (bf16[32,80,128]{2,1,0:T(8,128)(2,1)S(1)}, bf16[32,80,128]{2,1,0:T(8,128)(2,1)}, u32[]{:S(2)}, u32[]{:S(2)}) collective-permute-start(bf16[32,80,128]{2,1,0:T(8,128)(2,1)S(1)} %all-to-all-done.4.own_ref), channel_id=1, source_target_pairs={{0,4},{4,0},{1,5},{5,1},{2,6},{6,2},{3,7},{7,3},{8,12},{12,8},{9,1... | collective-permute-start | bytes 1966088 | tf_op jit(solution)/shard_map/ppermute | solution.py:27
  197.7 9.4 %collective-permute-start.24 = (bf16[240,256]{1,0:T(8,128)(2,1)}, bf16[240,256]{1,0:T(8,128)(2,1)}, u32[]{:S(2)}, u32[]{:S(2)}) collective-permute-start(bf16[240,256]{1,0:T(8,128)(2,1)} %get-tuple-element.69), channel_id=1, source_target_pairs={{0,3},{1,0},{2,1},{3,2},{4,7},{5,4},{6,5},{7,6},{8,11},{9,8},{10,9... | collective-permute-start | bytes 368648 | tf_op jit(solution)/shard_map/ppermute | solution.py:31
  200.5 8.0 %collective-permute-start.25 = (bf16[240,256]{1,0:T(8,128)(2,1)}, bf16[240,256]{1,0:T(8,128)(2,1)}, u32[]{:S(2)}, u32[]{:S(2)}) collective-permute-start(bf16[240,256]{1,0:T(8,128)(2,1)} %get-tuple-element.70), channel_id=1, source_target_pairs={{0,2},{1,3},{2,0},{3,1},{4,6},{5,7},{6,4},{7,5},{8,10},{9,11},{10,... | collective-permute-start | bytes 368648 | tf_op jit(solution)/shard_map/ppermute | solution.py:31
  201.2 8.9 %collective-permute-start.26 = (bf16[240,256]{1,0:T(8,128)(2,1)S(1)}, bf16[240,256]{1,0:T(8,128)(2,1)S(1)}, u32[]{:S(2)}, u32[]{:S(2)}) collective-permute-start(bf16[240,256]{1,0:T(8,128)(2,1)S(1)} %get-tuple-element.71), channel_id=1, source_target_pairs={{0,1},{1,2},{2,3},{3,0},{4,5},{5,6},{6,7},{7,4},{8,9},{9,10},{10,1... | collective-permute-start | bytes 368648 | tf_op jit(solution)/shard_map/ppermute | solution.py:31
  201.3 23.9 %all-to-all-start.5 = ((bf16[32,16,512]{2,1,0:T(8,128)(2,1)}), bf16[32,16,512]{2,1,0:T(8,128)(2,1)}, u32[]{:S(2)}, u32[]{:S(2)}) async-start(bf16[32,16,512]{2,1,0:T(8,128)(2,1)} %pad_maximum_fusion.1), calls=%async_computation.5 | async-start | bytes 1048576 | tf_op jit(solution)/shard_map/all_to_all | solution.py:44
  210.2 6.0 %collective-permute-start.27 = (bf16[112,256]{1,0:T(8,128)(2,1)S(1)}, bf16[112,256]{1,0:T(8,128)(2,1)S(1)}, u32[]{:S(2)}, u32[]{:S(2)}) collective-permute-start(bf16[112,256]{1,0:T(8,128)(2,1)S(1)} %fusion.24.a0), channel_id=1, source_target_pairs={{0,1},{1,2},{2,3},{3,0},{4,5},{5,6},{6,7},{7,4},{8,9},{9,10},{10,1... | collective-permute-start | bytes 172040 | tf_op jit(solution)/shard_map/ppermute | solution.py:31
  212.0 5.7 %collective-permute-start.28 = (bf16[112,256]{1,0:T(8,128)(2,1)S(1)}, bf16[112,256]{1,0:T(8,128)(2,1)S(1)}, u32[]{:S(2)}, u32[]{:S(2)}) collective-permute-start(bf16[112,256]{1,0:T(8,128)(2,1)S(1)} %fusion.24.a0), channel_id=1, source_target_pairs={{0,2},{1,3},{2,0},{3,1},{4,6},{5,7},{6,4},{7,5},{8,10},{9,11},{10,... | collective-permute-start | bytes 172040 | tf_op jit(solution)/shard_map/ppermute | solution.py:31
  225.3 26.9 %all-to-all-start.6 = ((bf16[32,64,128]{2,1,0:T(8,128)(2,1)}), bf16[32,64,128]{2,1,0:T(8,128)(2,1)S(1)}, u32[]{:S(2)}, u32[]{:S(2)}) async-start(bf16[32,64,128]{2,1,0:T(8,128)(2,1)} %bitcast.43), calls=%async_computation.6 | async-start | bytes 1048576 | tf_op jit(solution)/shard_map/all_to_all | solution.py:44
  252.2 9.5 %collective-permute-start.31 = (bf16[64,128]{1,0:T(8,128)(2,1)S(1)}, bf16[64,128]{1,0:T(8,128)(2,1)S(1)}, u32[]{:S(2)}, u32[]{:S(2)}) collective-permute-start(bf16[64,128]{1,0:T(8,128)(2,1)S(1)} %add_convert_fusion.1), channel_id=1, source_target_pairs={{0,0},{1,8},{2,16},{3,24},{8,1},{9,9},{10,17},{11,25},{16,2},{17,1... | collective-permute-start | bytes 49160 | tf_op jit(solution)/shard_map/ppermute | solution.py:40
  (44 other events, 522.6 us)

commit v4 on v3

v4 whole, which is shorter than its diff:
```python
import functools

import jax
import jax.numpy as jnp
from jax import lax
from jax.experimental import pallas as pl
from jax.experimental.pallas import tpu as pltpu
from jax.sharding import Mesh
from jax.sharding import PartitionSpec as P

D = 8192
HEAD_DIM = 128
DOC_LEN = 512
SEL_DEV = 3
EPS = 1e-05
NEG = -1e30
FLOOR = -1e29
NZ, NX, NC, NY = 8, 4, 2, 4
POOL = NZ * NX * NC
ROWS = 256

BF = jnp.bfloat16
F32 = jnp.float32


def exchange_cores(value):
    return lax.ppermute(value, "c", [(0, 1), (1, 0)])


def shift_y(value, step):
    return lax.ppermute(value, "y", [(i, (i + step) % NY) for i in range(NY)])


def permute_xy(value, target):
    pairs = []
    for x in range(NX):
        for y in range(NY):
            to_x, to_y = target(x, y)
            pairs.append((x * NY + y, (to_x % NX) * NY + to_y % NY))
    return lax.ppermute(value, ("x", "y"), pairs)


def swap_zx(value):
    return lax.all_to_all(value, ("z", "x"), 0, 0, tiled=True)


def parts_of(value):
    high = lax.reduce_precision(value, 8, 7)
    rest = value - high
    middle = lax.reduce_precision(rest, 8, 7)
    low = rest - middle
    return [high.astype(BF), middle.astype(BF), low.astype(BF)]


def shift_x(value, step):
    return lax.ppermute(value, "x", [(i, (i + step) % NX) for i in range(NX)])


def swap_z(value):
    return lax.all_to_all(value, "z", 0, 0, tiled=True)


def hold(*values):
    return lax.optimization_barrier(values)


def positions(sel_index, doc_order):
    docs = jnp.arange(POOL, dtype=jnp.int32)
    slot_of_doc = jnp.sum(jnp.where(doc_order[:, None] == docs[None, :], docs[:, None], 0), axis=0)
    sel_doc = sel_index // DOC_LEN
    sel_tok = sel_index % DOC_LEN
    sel_slot = jnp.sum(
        jnp.where(sel_doc[:, None] == docs[None, :], slot_of_doc[None, :], 0), axis=1
    )
    sel_pos = sel_slot * DOC_LEN + sel_tok
    query_pos = DOC_LEN * POOL + docs
    row_pos = jnp.concatenate(
        [sel_pos.reshape(POOL, SEL_DEV), query_pos[:, None]], axis=1
    ).reshape(ROWS)
    return slot_of_doc, row_pos


def slices_kernel(place_ref, in_ref, out_ref, *pieces):
    core = place_ref[0]
    y = place_ref[1]
    for step in range(4):
        base = lax.rem(y + step, NY) * 256
        for rel in range(2):
            group = core if rel == 0 else 1 - core
            lanes = pl.ds(pl.multiple_of(base + group * 128, 128), 128)
            pieces[step][0, rel, 0:224, :] = in_ref[:, lanes]
            pieces[step][0, rel, 224:336, :] = out_ref[:, lanes]


def weight_slices(place, flat_in, w_out):
    return pl.pallas_call(
        slices_kernel,
        grid=(NZ,),
        out_shape=tuple(jax.ShapeDtypeStruct((NZ, 2, 336, 128), BF) for _ in range(4)),
        in_specs=[
            pl.BlockSpec(memory_space=pltpu.SMEM),
            pl.BlockSpec((224, 1024), lambda k: (0, k)),
            pl.BlockSpec((112, 1024), lambda k: (0, k)),
        ],
        out_specs=tuple(pl.BlockSpec((1, 2, 336, 128), lambda k: (k, 0, 0, 0)) for _ in range(4)),
        compiler_params=pltpu.CompilerParams(vmem_limit_bytes=8 * 1024 * 1024),
        cost_estimate=pl.CostEstimate(flops=0, bytes_accessed=11_000_000, transcendentals=0),
        name="weight_slices",
    )(place, flat_in, w_out)


NT = (((1,), (1,)), ((), ()))
TN = (((0,), (0,)), ((), ()))


def split_rows(value):
    high = value.astype(BF).astype(F32)
    rest = value - high
    middle = rest.astype(BF).astype(F32)
    return [high, middle, rest - middle]


def attend_kernel(
    place_ref, bias_ref, own_ref, other_ref, c0, c1, c2, c3, acc_ref, sent_ref, stat_ref
):
    core = place_ref[0]
    blocks = (c0, c1, c2, c3)
    for rel in range(2):
        query_ref = own_ref if rel == 0 else other_ref
        group = core if rel == 0 else 1 - core
        key_at = pl.ds(pl.multiple_of(group * 128, 128), 128)
        value_at = pl.ds(pl.multiple_of(256 + group * 128, 128), 128)
        for half in range(2):
            lanes = slice(half * 256, half * 256 + 256)
            query = jnp.concatenate(
                [query_ref[half * 4 + i, 0:64, :] for i in range(4)], axis=0
            )
            scores = []
            top = jnp.full((1, 256), FLOOR, F32)
            for k in range(4):
                bias = bias_ref[k * 512 : k * 512 + 512, :].astype(F32)
                part = lax.dot_general(
                    blocks[k][:, key_at], query, NT, preferred_element_type=F32
                ) * (HEAD_DIM**-0.5) + jnp.concatenate([bias, bias], axis=1)
                scores.append(part)
                top = jnp.maximum(top, jnp.max(part, axis=0, keepdims=True))
            total = jnp.zeros((1, 256), F32)
            acc = jnp.zeros((128, 256), F32)
            for k in range(4):
                probs = jnp.exp(scores[k] - top)
                total = total + jnp.sum(probs, axis=0, keepdims=True)
                acc = acc + lax.dot_general(
                    blocks[k][:, value_at], probs.astype(BF), TN, preferred_element_type=F32
                )
            if rel == 0:
                acc_ref[:, lanes] = acc
                stat_ref[0:1, lanes] = top
                stat_ref[1:2, lanes] = total
            else:
                stats = split_rows(top) + split_rows(total) + [jnp.zeros((10, 256), F32)]
                sent_ref[0:128, lanes] = acc.astype(BF)
                sent_ref[128:144, lanes] = jnp.concatenate(stats, axis=0).astype(BF)


def attend(place, bias, own, other, blocks):
    vmem = pl.BlockSpec(memory_space=pltpu.VMEM)
    return pl.pallas_call(
        attend_kernel,
        out_shape=(
            jax.ShapeDtypeStruct((128, 512), F32),
            jax.ShapeDtypeStruct((144, 512), BF),
            jax.ShapeDtypeStruct((8, 512), F32),
        ),
        in_specs=[pl.BlockSpec(memory_space=pltpu.SMEM)] + [vmem] * 7,
        out_specs=(vmem, vmem, vmem),
        compiler_params=pltpu.CompilerParams(vmem_limit_bytes=16 * 1024 * 1024),
        cost_estimate=pl.CostEstimate(
            flops=2 * 16 * 2 * 2048 * 128 * 64, bytes_accessed=6_000_000, transcendentals=2097152
        ),
        name="attend",
    )(place, bias, own, other, *blocks)


def merge_kernel(acc_ref, stat_ref, far_ref, out_ref):
    near_top = stat_ref[0:1, :]
    stat = far_ref[128:144, :].astype(F32)
    far_top = stat[0:1] + (stat[1:2] + stat[2:3])
    far_total = stat[3:4] + (stat[4:5] + stat[5:6])
    top = jnp.maximum(near_top, far_top)
    near = jnp.exp(near_top - top)
    far = jnp.exp(far_top - top)
    total = stat_ref[1:2, :] * near + far_total * far
    acc = acc_ref[...] * near + far_ref[0:128, :].astype(F32) * far
    rows = acc.T.astype(BF)
    stats = split_rows(top) + split_rows(total) + [jnp.zeros((10, 512), F32)]
    stats = jnp.concatenate(stats, axis=0).astype(BF)
    for head in range(8):
        pair = head // 2
        out_ref[head, 0:64, :] = rows[head * 64 : head * 64 + 64, :]
        out_ref[head, 64:80, :] = stats[:, pair * 128 : pair * 128 + 128]


VMEM = pl.BlockSpec(memory_space=pltpu.VMEM)
SMEM = pl.BlockSpec(memory_space=pltpu.SMEM)


def merge(*operands):
    return pl.pallas_call(
        merge_kernel,
        out_shape=jax.ShapeDtypeStruct((8, 80, 128), BF),
        in_specs=[VMEM] * 3,
        out_specs=VMEM,
        cost_estimate=pl.CostEstimate(flops=500_000, bytes_accessed=1_000_000, transcendentals=0),
        compiler_params=pltpu.CompilerParams(vmem_limit_bytes=6 * 1024 * 1024),
        name="merge",
    )(*operands)


def finish_kernel(
    place_ref, arrived_ref, own_ref, bias_ref, out_ref, column_ref, new_ref
):
    z = place_ref[0]
    keys = jnp.concatenate([own_ref[k, 64:96, :] for k in range(8)], axis=0)
    values = jnp.concatenate([own_ref[k, 96:128, :] for k in range(8)], axis=0)
    query = own_ref[z, 0:64, :]
    query = jnp.concatenate([query, query], axis=0)
    scores = lax.dot_general(keys, query, NT, preferred_element_type=F32)
    scores = scores * (HEAD_DIM**-0.5) + bias_ref[...].astype(F32)
    tops = []
    sums = []
    for k in range(8):
        stat = arrived_ref[k, 64:80, :].astype(F32)
        tops.append(stat[0:1] + (stat[1:2] + stat[2:3]))
        sums.append(stat[3:4] + (stat[4:5] + stat[5:6]))
    tops = jnp.concatenate(tops, axis=0)
    sums = jnp.concatenate(sums, axis=0)
    top = jnp.maximum(
        jnp.max(tops, axis=0, keepdims=True), jnp.max(scores, axis=0, keepdims=True)
    )
    by = jnp.exp(tops - top)
    probs = jnp.exp(scores - top)
    norm = jnp.sum(sums * by, axis=0, keepdims=True) + jnp.sum(probs, axis=0, keepdims=True)
    column_ref[...] = jnp.concatenate([by, jnp.broadcast_to(norm, (8, 128))], axis=0).T
    new_ref[...] = lax.dot_general(
        probs.astype(BF), values, TN, preferred_element_type=F32
    )
    mine = pl.ds(pl.multiple_of(lax.rem(z, 2) * 64, 64), 64)
    column = column_ref[mine, :]
    acc = new_ref[mine, :]
    for k in range(8):
        acc = acc + arrived_ref[k, 0:64, :].astype(F32) * column[:, k : k + 1]
    result = (acc / column[:, 8:9]).astype(BF)
    for k in range(8):
        out_ref[k] = result


def finish(*operands):
    return pl.pallas_call(
        finish_kernel,
        out_shape=jax.ShapeDtypeStruct((8, 64, 128), BF),
        in_specs=[SMEM] + [VMEM] * 3,
        out_specs=VMEM,
        scratch_shapes=[pltpu.VMEM((128, 16), F32), pltpu.VMEM((128, 128), F32)],
        cost_estimate=pl.CostEstimate(flops=20_000_000, bytes_accessed=800_000, transcendentals=0),
        compiler_params=pltpu.CompilerParams(vmem_limit_bytes=6 * 1024 * 1024),
        name="finish",
    )(*operands)


def project_kernel(place_ref, own_ref, far_ref, w0, w1, w2, w3, out_ref):
    core = place_ref[0]
    for k, weight_ref in enumerate((w0, w1, w2, w3)):
        value = jnp.zeros((64, 128), F32)
        for rel, ref in enumerate((own_ref, far_ref)):
            group = core if rel == 0 else 1 - core
            at = pl.ds(pl.multiple_of(group * 1024, 1024), 1024)
            rows = jnp.concatenate([ref[i] for i in range(8)], axis=1)
            value = value + jnp.dot(rows, weight_ref[at, :], preferred_element_type=F32)
        out_ref[k] = value


def project(*operands):
    return pl.pallas_call(
        project_kernel,
        out_shape=jax.ShapeDtypeStruct((NX, 64, 128), F32),
        in_specs=[SMEM] + [VMEM] * 6,
        out_specs=VMEM,
        compiler_params=pltpu.CompilerParams(vmem_limit_bytes=8 * 1024 * 1024),
        cost_estimate=pl.CostEstimate(
            flops=2 * 64 * 2048 * 512, bytes_accessed=2_500_000, transcendentals=0
        ),
        name="project",
    )(*operands)


def ffn_in_kernel(p0, p1, p2, p3, own_ref, far_ref, keep_ref, square_ref, s1, s2, s3, feature):
    pairs = [jnp.zeros((1, 128), F32), jnp.zeros((1, 128), F32)]
    for rel, ref in enumerate((own_ref, far_ref)):
        for z in range(NZ):
            for k in range(4):
                feature[rel, k * 64 : k * 64 + 64, z * 128 : z * 128 + 128] = ref[
                    z * 4 + k, 0:64, :
                ]
                stat = ref[z * 4 + k, 64:80, :].astype(F32)
                pairs[k // 2] = pairs[k // 2] + (stat[0:1] + (stat[1:2] + stat[2:3]))
    squares = jnp.concatenate(pairs, axis=1)
    square_ref[...] = jnp.broadcast_to(squares, (8, ROWS))
    rows = jnp.concatenate(split_rows(squares) + [jnp.zeros((13, ROWS), F32)], axis=0).astype(BF)
    for step, (piece, to) in enumerate(((p1, s1), (p2, s2), (p3, s3), (p0, keep_ref))):
        value = jnp.zeros((224, ROWS), F32)
        for rel in range(2):
            weight = jnp.concatenate([piece[z, rel, 0:224, :] for z in range(NZ)], axis=1)
            value = value + lax.dot_general(weight, feature[rel], NT, preferred_element_type=F32)
        if step < 3:
            to[0:224, :] = value.astype(BF)
            to[224:240, :] = rows
        else:
            to[...] = value


def ffn_in(*operands):
    sent = jax.ShapeDtypeStruct((240, ROWS), BF)
    return pl.pallas_call(
        ffn_in_kernel,
        out_shape=(
            jax.ShapeDtypeStruct((224, ROWS), F32),
            jax.ShapeDtypeStruct((8, ROWS), F32),
            sent,
            sent,
            sent,
        ),
        in_specs=[VMEM] * 6,
        out_specs=(VMEM,) * 5,
        scratch_shapes=[pltpu.VMEM((2, ROWS, 1024), BF)],
        compiler_params=pltpu.CompilerParams(vmem_limit_bytes=16 * 1024 * 1024),
        cost_estimate=pl.CostEstimate(
            flops=2 * 896 * 2048 * 256, bytes_accessed=7_500_000, transcendentals=0
        ),
        name="ffn_in",
    )(*operands)


def act_kernel(both_ref, square_ref, r1, r2, r3, out_ref):
    both = both_ref[...]
    squares = square_ref[0:1, :]
    for ref in (r1, r2, r3):
        both = both + ref[0:224, :].astype(F32)
        stat = ref[224:240, :].astype(F32)
        squares = squares + (stat[0:1] + (stat[1:2] + stat[2:3]))
    both = both * lax.rsqrt(squares / D + EPS)
    gate = both[0:112]
    out_ref[...] = (gate / (1.0 + jnp.exp(-gate)) * both[112:224]).astype(BF)


def act_of(*operands):
    return pl.pallas_call(
        act_kernel,
        out_shape=jax.ShapeDtypeStruct((112, ROWS), BF),
        in_specs=[VMEM] * 5,
        out_specs=VMEM,
        cost_estimate=pl.CostEstimate(flops=500_000, bytes_accessed=700_000, transcendentals=0),
        compiler_params=pltpu.CompilerParams(vmem_limit_bytes=6 * 1024 * 1024),
        name="act",
    )(*operands)


def down_kernel(rel, p0, p1, p2, p3, a0, a1, a2, a3, *refs):
    act = jnp.concatenate([a0[...], a1[...], a2[...], a3[...]], axis=0)
    weight = jnp.concatenate(
        [
            jnp.concatenate([p[z, rel, 224:336, :] for z in range(NZ)], axis=1)
            for p in (p0, p1, p2, p3)
        ],
        axis=0,
    )
    term = lax.dot_general(act, weight, TN, preferred_element_type=F32)
    for z in range(NZ):
        block = term[:, z * 128 : z * 128 + 128]
        if rel == 1:
            refs[-1][z] = block.astype(BF)
        else:
            block = (block + refs[0][z].astype(F32)).astype(BF)
            for k in range(NX):
                refs[-1][z * NX + k, 0:64, :] = block[k * 64 : k * 64 + 64, :]
                refs[-1][z * NX + k, 64:128, :] = refs[1][z * NX + k]


def down(rel, *operands):
    return pl.pallas_call(
        functools.partial(down_kernel, rel),
        out_shape=jax.ShapeDtypeStruct((NZ, ROWS, 128) if rel else (32, 128, 128), BF),
        in_specs=[VMEM] * len(operands),
        out_specs=VMEM,
        compiler_params=pltpu.CompilerParams(vmem_limit_bytes=16 * 1024 * 1024),
        cost_estimate=pl.CostEstimate(
            flops=448 * 2048 * 256, bytes_accessed=4_000_000, transcendentals=0
        ),
        name="down",
    )(*operands)


def shards(
    hidden_rows,
    cache_kv,
    sel_index,
    doc_order,
    attn_gain,
    w_query,
    w_keyval,
    w_output,
    ffn_gain,
    w_in,
    w_out,
):
    z, x, c, y = (lax.axis_index(name) for name in ("z", "x", "c", "y"))
    mine = (z * NX + x) * NC + c
    other = 1 - c

    def half(group):
        return jnp.concatenate(
            [
                lax.dynamic_slice_in_dim(w_query, group * 1024, 1024, 1),
                lax.dynamic_slice_in_dim(w_keyval[:, 0], group * 128, 128, 1),
                lax.dynamic_slice_in_dim(w_keyval[:, 1], group * 128, 128, 1),
            ],
            axis=1,
        )

    message = jnp.concatenate(
        [hidden_rows, jnp.broadcast_to(attn_gain[None, :], (16, 128))], axis=0
    )
    theirs = exchange_cores(message)
    weight_theirs = exchange_cores(half(other))

    theirs, raw = hold(theirs, cache_kv)
    cache = raw.reshape(DOC_LEN, 512)

    weight = jnp.concatenate([half(c), weight_theirs], axis=0)
    inputs = jnp.concatenate([hidden_rows, theirs[:ROWS]], axis=1).astype(F32)
    gain = jnp.concatenate([attn_gain, theirs[ROWS]], axis=0).astype(F32)
    squares = jnp.sum(inputs * inputs, axis=1)
    scaled = (inputs * gain[None, :]).astype(BF)
    partial = jnp.dot(scaled, weight, preferred_element_type=F32).astype(BF)
    query_part = jnp.transpose(partial[:, :1024].reshape(4, 64, 8, 128), (2, 0, 1, 3))
    new_part = jnp.transpose(partial[:, 1024:].reshape(8, 32, 2, 128), (0, 2, 1, 3))
    square_parts = jnp.stack(parts_of(squares) + [jnp.zeros((ROWS,), BF)] * 5)
    by_x = jnp.transpose(square_parts.reshape(8, 4, 64), (1, 0, 2))
    by_z = jnp.transpose(square_parts.reshape(8, 8, 32), (1, 0, 2))
    square_parts = jnp.concatenate(
        [
            jnp.broadcast_to(by_x[None], (8, 4, 8, 64)),
            jnp.broadcast_to(by_z[:, None], (8, 4, 8, 32)),
            jnp.zeros((8, 4, 8, 32), BF),
        ],
        axis=3,
    )
    new_part = jnp.broadcast_to(new_part.reshape(8, 1, 64, 128), (8, 4, 64, 128))
    payload = jnp.concatenate([query_part, new_part, square_parts], axis=2).reshape(32, 136, 128)

    early = jnp.concatenate(
        [
            lax.dynamic_slice_in_dim(hidden_rows, y * 64, 64, 0),
            jnp.broadcast_to(ffn_gain[None, :], (16, 128)),
        ],
        axis=0,
    )
    payload, cache, sel_index, doc_order, early = hold(
        payload, cache, sel_index, doc_order, early
    )
    reordered = cache.reshape(POOL, 8, 512).at[doc_order].get(mode="promise_in_bounds")
    reordered = reordered.reshape(32, 2, 8, 512)
    stay = lax.dynamic_index_in_dim(reordered, c, 1, keepdims=False)
    leave = lax.dynamic_index_in_dim(reordered, other, 1, keepdims=False)
    come, w_in, w_out, early = hold(exchange_cores(leave), w_in, w_out, early)
    early = permute_xy(early, lambda a, b: (b, a))
    right, left, across = shift_x(cache, 1), shift_x(cache, -1), shift_x(cache, 2)
    arrived, right, left, across = hold(swap_zx(payload), right, left, across)
    total = jnp.sum(arrived.astype(F32), axis=0)
    square_sum = total[128] + (total[129] + total[130])
    factor = lax.rsqrt(square_sum / D + EPS)
    new = total[64:128].reshape(2, 32, 128) * factor[None, 64:96, None]
    piece = jnp.concatenate(
        [total[:64] * factor[:64, None], new.reshape(64, 128)], axis=0
    ).astype(BF)

    place = jnp.stack([c, y, z]).astype(jnp.int32)
    flat_in = jnp.transpose(w_in, (1, 2, 0)).reshape(224, D)
    pieces = weight_slices(place, flat_in, w_out)
    slices = [pieces[0], shift_y(pieces[1], 1), None, shift_y(pieces[3], 3)]

    slot_of_doc, row_pos = positions(sel_index, doc_order)
    my_pos = lax.dynamic_slice_in_dim(row_pos, x * 64, 64, 0)
    my_pos = jnp.concatenate([my_pos, my_pos])[None, :]
    token = jnp.arange(8, dtype=jnp.int32)
    docs = jnp.arange(POOL, dtype=jnp.int32)
    key_pos = []
    for step in (0, 1, 3, 2):
        base = ((z * NX + (x - step) % NX) * NC + c) * 8
        name = (docs[:, None] * DOC_LEN + base + token[None, :]).reshape(DOC_LEN)
        at = (slot_of_doc[:, None] * DOC_LEN + base + token[None, :]).reshape(DOC_LEN)
        written = jnp.any(name[:, None] == sel_index[None, :], axis=1)
        key_pos.append(jnp.where(written, DOC_LEN * POOL * 2, at))
    bias = jnp.where(jnp.concatenate(key_pos)[:, None] <= my_pos, 0.0, NEG).astype(BF)
    new_bias = jnp.where(row_pos[:, None] <= my_pos, 0.0, NEG).astype(BF)

    piece, bias, new_bias, pieces, w_output = hold(piece, bias, new_bias, pieces, w_output)
    own = swap_z(jnp.broadcast_to(piece[None], (8, 128, 128)))
    wo_right, wo_left = shift_x(w_output, 1), shift_x(w_output, -1)
    others = exchange_cores(own)
    acc, acc_sent, stats = attend(place, bias, own, others, (cache, right, left, across))

    payload = merge(acc, stats, exchange_cores(acc_sent))
    payload, w_output, wo_right, wo_left, stay, come, slices[1], slices[3], last = hold(
        payload, w_output, wo_right, wo_left, stay, come, slices[1], slices[3], pieces[2]
    )
    wo_all = [w_output, wo_right, shift_x(w_output, 2), wo_left]
    slices[2] = shift_y(last, 2)

    arrived = swap_z(payload)

    lower = jnp.where(c == 0, stay, come)
    upper = jnp.where(c == 0, come, stay)
    cache_out = jnp.concatenate([lower, upper], axis=1).reshape(32, 16, 4, 128)
    cache_out = jnp.transpose(cache_out, (0, 2, 1, 3)).reshape(32, 64, 128)
    arrived, cache_out = hold(arrived, cache_out)
    piece = finish(place[2:], arrived, own, new_bias)
    attended = swap_z(piece)
    attended_theirs = exchange_cores(attended)

    chunks = project(place, attended, attended_theirs, *wo_all)
    chunks, slices[2] = hold(chunks, slices[2])
    mid = early[:64].astype(F32) + lax.dynamic_index_in_dim(chunks, (x - y) % NX, 0, keepdims=False)
    chunks = chunks.astype(BF)
    for step in range(1, 4):
        sent = lax.dynamic_index_in_dim(chunks, (x - y - step) % NX, 0, keepdims=False)
        mid = mid + shift_y(sent, step).astype(F32)
    feature = (mid * early[64].astype(F32)[None, :]).astype(BF)
    square_parts = jnp.stack(parts_of(jnp.sum(mid * mid, axis=1)) + [jnp.zeros((64,), BF)] * 13)
    empty = jnp.zeros_like(square_parts)
    square_parts = jnp.where(
        x % 2 == 0,
        jnp.concatenate([square_parts, empty], axis=1),
        jnp.concatenate([empty, square_parts], axis=1),
    )
    payload = jnp.concatenate([feature, square_parts], axis=0)
    arrived = swap_zx(jnp.broadcast_to(payload[None], (32, 80, 128)))
    arrived_theirs = exchange_cores(arrived)

    both, squares, *sent = ffn_in(*slices, arrived, arrived_theirs)
    got = [shift_y(sent[step - 1], -step) for step in range(1, 4)]
    act = act_of(both, squares, *got)
    acts = [act] + [shift_y(act, step) for step in range(1, 4)]
    got = exchange_cores(down(1, *slices, *acts))
    arrived = swap_zx(down(0, *slices, *acts, got, cache_out))
    summed = jnp.sum(arrived[:, :64].astype(F32), axis=0)
    slot_cache = jnp.transpose(arrived[:, 64:].reshape(32, 4, 16, 128), (0, 2, 1, 3))

    sel_key = jnp.where(row_pos // DOC_LEN == mine, row_pos % DOC_LEN, -1)
    hits = sel_key[None, :] == jnp.arange(DOC_LEN, dtype=jnp.int32)[:, None]
    covered = jnp.any(hits, axis=1)
    new_own, new_others = own[:, 64:], others[:, 64:]
    new_flat = jnp.stack(
        [jnp.where(c == 0, new_own, new_others), jnp.where(c == 0, new_others, new_own)]
    ).reshape(2, 8, 2, 32, 128)
    new_flat = jnp.transpose(new_flat, (1, 3, 2, 0, 4)).reshape(ROWS, 512)
    placed = jnp.dot(hits.astype(BF), new_flat, preferred_element_type=F32).astype(BF)
    joined = jnp.where(covered[:, None], placed, slot_cache.reshape(DOC_LEN, 512))
    joined = joined.reshape(DOC_LEN, 2, 256)
    result = permute_xy((mid + summed).astype(BF), lambda a, b: (b, a))
    return (result, joined)


def solution(mesh):
    split = Mesh(mesh.devices.reshape(NZ, NX, NC, NY), ("z", "x", "c", "y"))
    pool = ("z", "x", "c")
    return jax.shard_map(
        shards,
        mesh=split,
        in_specs=(
            P(None, pool),
            P(None, pool, None, "y"),
            P(),
            P(),
            P(pool),
            P(pool, "y"),
            P(pool, None, "y"),
            P("y", pool),
            P(pool),
            P(None, None, ("z", "x", "c", "y")),
            P(("z", "x", "c", "y"), None),
        ),
        out_specs=(P("y", pool), P(pool, None, "y")),
        check_vma=False,
    )
```

time: 264 us -> 235 us (0.89)
  starting transfers between devices: 90.9 us -> 53.3 us
  blocking collectives: 0 us -> 37.6 us
  waiting for transfers between devices: 92 us -> 83.4 us
  local copies, waits for them, and re-layouts: 30 us -> 22.2 us
  other arithmetic: 19.7 us -> 11.9 us
  matrix products: 4.84 us -> 0.72 us
    all_to_all x0 -> x2, blocking collectives: none -> 37.6 us  [the longest x1 25.5 us: swap_zx(): return lax.all_to_all(value, ('z', 'x'), 0, 0, tiled=True)]
    ppermute x9 -> x6, waiting for transfers between devices: 28.8 us -> 0.02 us  [shift_x(): return lax.ppermute(value, 'x', [(i, (i + step) % NX) for i in range(NX)])]
    all_to_all x4 -> x2, starting transfers between devices: 38 us -> 15.7 us  [swap_zx(): return lax.all_to_all(value, ('z', 'x'), 0, 0, tiled=True)]
    all_to_all x4 -> x2, waiting for transfers between devices: 27.2 us -> 41.2 us  [swap_zx(): return lax.all_to_all(value, ('z', 'x'), 0, 0, tiled=True)]
    all_to_all x3 -> x2, starting transfers between devices: 14.4 us -> 7.42 us  [swap_z(): return lax.all_to_all(value, 'z', 0, 0, tiled=True)]
    ppermute x9 -> x6, starting transfers between devices: 12.7 us -> 7.68 us  [shift_x(): return lax.ppermute(value, 'x', [(i, (i + step) % NX) for i in range(NX)])]
    pallas_call x1 -> x4, Pallas kernels: 2.07 us -> 6.59 us  [the longest x2 4.47 us: down(): pl.pallas_call(functools.partial(down_kernel, rel), out_shape=jax.ShapeDt...]
    ppermute x2, starting transfers between devices: 9.68 us -> 5.24 us  [permute_xy(): return lax.ppermute(value, ('x', 'y'), pairs)]
  transfers between devices with their start and end apart: 39 -> 32, of which waited for: 21 -> 17; matrix products, arithmetic and copies ran while one was open for 17% -> 8% of each run, Pallas kernels for 8% -> 6%
where the time goes in v4:
time: 235 us; the launch traced here: 233 us
  waiting for transfers between devices  83.4 us (35%)
  starting transfers between devices  53.3 us (23%)
  blocking collectives  37.6 us (16%)
  Pallas kernels  22.5 us (10%)
  local copies, waits for them, and re-layouts  22.2 us (9%)
  other arithmetic  11.9 us (5%)
    all_to_all x2, waiting for transfers between devices, swap_zx(): return lax.all_to_all(value, ('z', 'x'), 0, 0, tiled=True)  41.2 us
    all_to_all x1, blocking collectives, swap_zx(): return lax.all_to_all(value, ('z', 'x'), 0, 0, tiled=True)  25.5 us
    ppermute x12, starting transfers between devices, shift_y(): return lax.ppermute(value, 'y', [(i, (i + step) % NY) for i in range(NY)])  16.3 us
    all_to_all x2, waiting for transfers between devices, swap_z(): return lax.all_to_all(value, 'z', 0, 0, tiled=True)  16.3 us
    all_to_all x2, starting transfers between devices, swap_zx(): return lax.all_to_all(value, ('z', 'x'), 0, 0, tiled=True)  15.7 us
    ppermute x12, waiting for transfers between devices, shift_y(): return lax.ppermute(value, 'y', [(i, (i + step) % NY) for i in range(NY)])  12.7 us
    all_to_all x1, blocking collectives, swap_z(): return lax.all_to_all(value, 'z', 0, 0, tiled=True)  12.1 us
    unnamed x46, local copies, waits for them, and re-layouts  10.8 us
  transfers between devices with their start and end apart: 32, of which 17 were waited for; matrix products, arithmetic and copies ran while one was open for 8% of the time, Pallas kernels for 6%

profile of v4, /device:TPU:4, one launch (start us, length us, event | category | flops | bytes accessed | tf_op | source)
XLA Modules:
  0.0 233.3 jit_solution(702889520295825241)
XLA Ops:
  11.1 3.5 %collective-permute-start.6 = (bf16[512,512]{1,0:T(8,128)(2,1)S(1)}, bf16[512,512]{1,0:T(8,128)(2,1)}, u32[]{:S(2)}, u32[]{:S(2)}) collective-permute-start(bf16[512,512]{1,0:T(8,128)(2,1)S(1)} %bitcast.95), channel_id=1, source_target_pairs={{0,16},{8,24},{16,0},{24,8},{1,17},{9,25},{17,1},{25,9},{2,18},{10... | collective-permute-start | bytes 1572872 | tf_op jit(solution)/shard_map/ppermute | solution.py:56
  16.0 10.0 %all-to-all-start = ((bf16[32,136,128]{2,1,0:T(8,128)(2,1)}), bf16[32,136,128]{2,1,0:T(8,128)(2,1)}, u32[]{:S(2)}, u32[]{:S(2)}) async-start(bf16[32,136,128]{2,1,0:T(8,128)(2,1)} %bitcast.10), calls=%async_computation | async-start | bytes 2228224 | tf_op jit(solution)/shard_map/all_to_all | solution.py:44
  30.3 2.0 copy-done.1
  33.8 4.7 %weight_slices.1 = (bf16[8,2,336,128]{3,2,1,0:T(8,128)(2,1)S(1)}, bf16[8,2,336,128]{3,2,1,0:T(8,128)(2,1)}, bf16[8,2,336,128]{3,2,1,0:T(8,128)(2,1)}, bf16[8,2,336,128]{3,2,1,0:T(8,128)(2,1)}) custom-call(s32[3]{0:T(128)S(1)} %pad_add_fusion.2.place_ref, bf16[224,8192]{1,0:T(8,128)(2,1)S(1)} %bitcast.92, bf16[112,8192]{1,0:T(8,128)(2,1)S(1)} %copy-done.2), custom_call_target="tpu_custom_call" | custom-call | bytes 11000000 | tf_op jit(solution)/shard_map/weight_slices/pallas_call | solution.py:96
  40.1 1.7 collective-permute-start.12
  41.8 14.3 %all-to-all-done = bf16[32,136,128]{2,1,0:T(8,128)(2,1)} async-done(((bf16[32,136,128]{2,1,0:T(8,128)(2,1)}), bf16[32,136,128]{2,1,0:T(8,128)(2,1)}, u32[]{:S(2)}, u32[]{:S(2)}) %all-to-all-start) | async-done | bytes 1114144 | tf_op jit(solution)/shard_map/all_to_all | solution.py:44
  58.5 3.4 %all-to-all-start.1 = ((bf16[8,128,128]{2,1,0:T(8,128)(2,1)}), bf16[8,128,128]{2,1,0:T(8,128)(2,1)S(1)}, u32[]{:S(2)}, u32[]{:S(2)}) async-start(bf16[8,128,128]{2,1,0:T(8,128)(2,1)} %broadcast_in_dim.91), calls=%async_computation.1 | async-start | bytes 524288 | tf_op jit(solution)/shard_map/all_to_all | solution.py:60
  64.1 9.5 %all-to-all-done.1.own_ref = bf16[8,128,128]{2,1,0:T(8,128)(2,1)S(1)} async-done(((bf16[8,128,128]{2,1,0:T(8,128)(2,1)}), bf16[8,128,128]{2,1,0:T(8,128)(2,1)S(1)}, u32[]{:S(2)}, u32[]{:S(2)}) %all-to-all-start.1) | async-done | bytes 262176 | tf_op jit(solution)/shard_map/all_to_all | solution.py:60
  76.2 5.7 %attend.1 = (f32[128,512]{1,0:T(8,128)S(1)}, bf16[144,512]{1,0:T(8,128)(2,1)S(1)}, f32[8,512]{1,0:T(8,128)S(1)}) custom-call(s32[3]{0:T(128)S(1)} %pad_add_fusion.2.place_ref, bf16[2048,128]{1,0:T(8,128)(2,1)S(1)} %copy-done.3, bf16[8,128,128]{2,1,0:T(8,128)(2,1)S(1)} %all-to-all-done.1.own_ref, bf16[8,128,128]{2,1,0:T(8,128)(2,1)S(1)} %collective-permute-done.7.other_ref, ...), custom_call_target="tpu_custom_call" | custom-call | flops 1073741824 | bytes 6000000 | tf_op jit(solution)/shard_map/attend/pallas_call | solution.py:167
  84.2 3.3 %collective-permute-start.15 = (bf16[8,2,336,128]{3,2,1,0:T(8,128)(2,1)}, bf16[8,2,336,128]{3,2,1,0:T(8,128)(2,1)}, u32[]{:S(2)}, u32[]{:S(2)}) collective-permute-start(bf16[8,2,336,128]{3,2,1,0:T(8,128)(2,1)} %get-tuple-element.81), channel_id=1, source_target_pairs={{0,2},{1,3},{2,0},{3,1},{4,6},{5,7},{6,4},{7,5},{8,10},{9,11},{10,... | collective-permute-start | bytes 4128776 | tf_op jit(solution)/shard_map/ppermute | solution.py:31
  87.5 4.0 %all-to-all-start.2 = ((bf16[8,80,128]{2,1,0:T(8,128)(2,1)}), bf16[8,80,128]{2,1,0:T(8,128)(2,1)}, u32[]{:S(2)}, u32[]{:S(2)}) async-start(bf16[8,80,128]{2,1,0:T(8,128)(2,1)} %merge.1), calls=%async_computation.2 | async-start | bytes 327680 | tf_op jit(solution)/shard_map/all_to_all | solution.py:60
  94.8 6.8 %all-to-all-done.2.arrived_ref = bf16[8,80,128]{2,1,0:T(8,128)(2,1)} async-done(((bf16[8,80,128]{2,1,0:T(8,128)(2,1)}), bf16[8,80,128]{2,1,0:T(8,128)(2,1)}, u32[]{:S(2)}, u32[]{:S(2)}) %all-to-all-start.2) | async-done | bytes 163872 | tf_op jit(solution)/shard_map/all_to_all | solution.py:60
  103.9 12.1 %all_to_all.30.own_ref = bf16[8,64,128]{2,1,0:T(8,128)(2,1)} all-to-all(bf16[8,64,128]{2,1,0:T(8,128)(2,1)S(1)} %finish.1), channel_id=1, replica_groups=mesh['z'=8,'x'=4,'c'=2,'y'=4] {'z'}, dimensions={0} | all-to-all | bytes 262144 | tf_op jit(solution)/shard_map/all_to_all | solution.py:60
  116.0 2.3 collective-permute-start.3
  119.4 2.0 project.1
  123.9 1.9 collective-permute-done.3
  125.8 2.2 collective-permute-done.17
  133.6 25.5 %all_to_all.31.own_ref = bf16[32,80,128]{2,1,0:T(8,128)(2,1)S(1)} all-to-all(bf16[32,80,128]{2,1,0:T(8,128)(2,1)S(1)} %broadcast_in_dim.92), channel_id=1, replica_groups=mesh['z'=8,'x'=4,'c'=2,'y'=4] {'z','x'}, dimensions={0} | all-to-all | bytes 1310720 | tf_op jit(solution)/shard_map/all_to_all | solution.py:44
  159.1 2.1 collective-permute-done.19.far_ref
  161.2 3.2 %ffn_in.1 = (f32[224,256]{1,0:T(8,128)S(1)}, f32[8,256]{1,0:T(8,128)S(1)}, bf16[240,256]{1,0:T(8,128)(2,1)S(1)}, bf16[240,256]{1,0:T(8,128)(2,1)S(1)}, bf16[240,256]{1,0:T(8,128)(2,1)S(1)}) custom-call(bf16[8,2,336,128]{3,2,1,0:T(8,128)(2,1)S(1)} %get-tuple-element.58.p0, bf16[8,2,336,128]{3,2,1,0:T(8,128)(2,1)S(1)} %collective-permute-done.11.p1, ...), custom_call_target="tpu_custom_call" | custom-call | flops 939524096 | bytes 7500000 | tf_op jit(solution)/shard_map/ffn_in/pallas_call | solution.py:323
  167.7 3.0 %collective-permute-done.20.r1 = bf16[240,256]{1,0:T(8,128)(2,1)S(1)} collective-permute-done((bf16[240,256]{1,0:T(8,128)(2,1)S(1)}, bf16[240,256]{1,0:T(8,128)(2,1)S(1)}, u32[]{:S(2)}, u32[]{:S(2)}) %collective-permute-start.20) | collective-permute-done | bytes 122912 | tf_op jit(solution)/shard_map/ppermute | solution.py:31
  170.6 2.2 collective-permute-done.21.r2
  174.6 2.1 collective-permute-start.24
  176.8 1.9 collective-permute-start.25
  178.7 2.1 collective-permute-done.23.a1
  181.5 2.2 down.2
  183.8 1.9 collective-permute-done.26.refs_0_
  185.7 2.3 down.3
  188.9 5.7 %all-to-all-start.5 = ((bf16[32,128,128]{2,1,0:T(8,128)(2,1)}), bf16[32,128,128]{2,1,0:T(8,128)(2,1)S(1)}, u32[]{:S(2)}, u32[]{:S(2)}) async-start(bf16[32,128,128]{2,1,0:T(8,128)(2,1)} %copy-done), calls=%async_computation.5 | async-start | bytes 2097152 | tf_op jit(solution)/shard_map/all_to_all | solution.py:44
  196.1 27.0 %all-to-all-done.5 = bf16[32,128,128]{2,1,0:T(8,128)(2,1)S(1)} async-done(((bf16[32,128,128]{2,1,0:T(8,128)(2,1)}), bf16[32,128,128]{2,1,0:T(8,128)(2,1)S(1)}, u32[]{:S(2)}, u32[]{:S(2)}) %all-to-all-start.5) | async-done | bytes 1048608 | tf_op jit(solution)/shard_map/all_to_all | solution.py:44
  223.1 3.0 %collective-permute-start.27 = (bf16[64,128]{1,0:T(8,128)(2,1)S(1)}, bf16[64,128]{1,0:T(8,128)(2,1)S(1)}, u32[]{:S(2)}, u32[]{:S(2)}) collective-permute-start(bf16[64,128]{1,0:T(8,128)(2,1)S(1)} %add_convert_fusion), channel_id=1, source_target_pairs={{0,0},{1,8},{2,16},{3,24},{8,1},{9,9},{10,17},{11,25},{16,2},{17,1... | collective-permute-start | bytes 49160 | tf_op jit(solution)/shard_map/ppermute | solution.py:40
  228.2 4.5 %collective-permute-done.27 = bf16[64,128]{1,0:T(8,128)(2,1)S(1)} collective-permute-done((bf16[64,128]{1,0:T(8,128)(2,1)S(1)}, bf16[64,128]{1,0:T(8,128)(2,1)S(1)}, u32[]{:S(2)}, u32[]{:S(2)}) %collective-permute-start.27) | collective-permute-done | bytes 16416 | tf_op jit(solution)/shard_map/ppermute | solution.py:40
  (212 shorter events, 53.7 us)
Async XLA Ops:
  2.2 3.9 %collective-permute-start = (bf16[272,128]{1,0:T(8,128)(2,1)S(1)}, bf16[272,128]{1,0:T(8,128)(2,1)S(1)}, u32[]{:S(2)}, u32[]{:S(2)}) collective-permute-start(bf16[272,128]{1,0:T(8,128)(2,1)S(1)} %pad_maximum_fusion.4), channel_id=1, source_target_pairs={{0,4},{4,0},{1,5},{5,1},{2,6},{6,2},{3,7},{7,3},{8,12},{12,8},{9,1... | collective-permute-start | bytes 208904 | tf_op jit(solution)/shard_map/ppermute | solution.py:27
  3.9 2.9 %collective-permute-start.1 = (bf16[128,1280]{1,0:T(8,128)(2,1)S(1)}, bf16[128,1280]{1,0:T(8,128)(2,1)S(1)}, u32[]{:S(2)}, u32[]{:S(2)}) collective-permute-start(bf16[128,1280]{1,0:T(8,128)(2,1)S(1)} %pad_maximum_fusion.1), channel_id=1, source_target_pairs={{0,4},{4,0},{1,5},{5,1},{2,6},{6,2},{3,7},{7,3},{8,12},{12,8},{9,1... | collective-permute-start | bytes 983048 | tf_op jit(solution)/shard_map/ppermute | solution.py:27
  9.0 32.8 %collective-permute-start.4 = (bf16[512,512]{1,0:T(8,128)(2,1)S(1)}, bf16[512,512]{1,0:T(8,128)(2,1)}, u32[]{:S(2)}, u32[]{:S(2)}) collective-permute-start(bf16[512,512]{1,0:T(8,128)(2,1)S(1)} %bitcast.93), channel_id=1, source_target_pairs={{0,8},{8,16},{16,24},{24,0},{1,9},{9,17},{17,25},{25,1},{2,10},{10... | collective-permute-start | bytes 1572872 | tf_op jit(solution)/shard_map/ppermute | solution.py:56
  10.2 31.6 %collective-permute-start.5 = (bf16[512,512]{1,0:T(8,128)(2,1)S(1)}, bf16[512,512]{1,0:T(8,128)(2,1)}, u32[]{:S(2)}, u32[]{:S(2)}) collective-permute-start(bf16[512,512]{1,0:T(8,128)(2,1)S(1)} %bitcast.94), channel_id=1, source_target_pairs={{0,24},{8,0},{16,8},{24,16},{1,25},{9,1},{17,9},{25,17},{2,26},{10... | collective-permute-start | bytes 1572872 | tf_op jit(solution)/shard_map/ppermute | solution.py:56
  11.1 30.7 %collective-permute-start.6 = (bf16[512,512]{1,0:T(8,128)(2,1)S(1)}, bf16[512,512]{1,0:T(8,128)(2,1)}, u32[]{:S(2)}, u32[]{:S(2)}) collective-permute-start(bf16[512,512]{1,0:T(8,128)(2,1)S(1)} %bitcast.95), channel_id=1, source_target_pairs={{0,16},{8,24},{16,0},{24,8},{1,17},{9,25},{17,1},{25,9},{2,18},{10... | collective-permute-start | bytes 1572872 | tf_op jit(solution)/shard_map/ppermute | solution.py:56
  16.0 13.6 %collective-permute-start.2 = (bf16[32,8,512]{2,1,0:T(8,128)(2,1)S(1)}, bf16[32,8,512]{2,1,0:T(8,128)(2,1)S(1)}, u32[]{:S(2)}, u32[]{:S(2)}) collective-permute-start(bf16[32,8,512]{2,1,0:T(8,128)(2,1)S(1)} %get-tuple-element.113), channel_id=1, source_target_pairs={{0,4},{4,0},{1,5},{5,1},{2,6},{6,2},{3,7},{7,3},{8,12},{12,8},{9,1... | collective-permute-start | bytes 786440 | tf_op jit(solution)/shard_map/ppermute | solution.py:27
  16.0 40.1 %all-to-all-start = ((bf16[32,136,128]{2,1,0:T(8,128)(2,1)}), bf16[32,136,128]{2,1,0:T(8,128)(2,1)}, u32[]{:S(2)}, u32[]{:S(2)}) async-start(bf16[32,136,128]{2,1,0:T(8,128)(2,1)} %bitcast.10), calls=%async_computation | async-start | bytes 2228224 | tf_op jit(solution)/shard_map/all_to_all | solution.py:44
  38.6 45.6 %collective-permute-start.11 = (bf16[8,2,336,128]{3,2,1,0:T(8,128)(2,1)}, bf16[8,2,336,128]{3,2,1,0:T(8,128)(2,1)S(1)}, u32[]{:S(2)}, u32[]{:S(2)}) collective-permute-start(bf16[8,2,336,128]{3,2,1,0:T(8,128)(2,1)} %get-tuple-element.59), channel_id=1, source_target_pairs={{0,1},{1,2},{2,3},{3,0},{4,5},{5,6},{6,7},{7,4},{8,9},{9,10},{10,1... | collective-permute-start | bytes 4128776 | tf_op jit(solution)/shard_map/ppermute | solution.py:31
  40.1 44.1 %collective-permute-start.12 = (bf16[8,2,336,128]{3,2,1,0:T(8,128)(2,1)}, bf16[8,2,336,128]{3,2,1,0:T(8,128)(2,1)}, u32[]{:S(2)}, u32[]{:S(2)}) collective-permute-start(bf16[8,2,336,128]{3,2,1,0:T(8,128)(2,1)} %get-tuple-element.61), channel_id=1, source_target_pairs={{0,3},{1,0},{2,1},{3,2},{4,7},{5,4},{6,5},{7,6},{8,11},{9,8},{10,9... | collective-permute-start | bytes 4128776 | tf_op jit(solution)/shard_map/ppermute | solution.py:31
  58.5 15.1 %all-to-all-start.1 = ((bf16[8,128,128]{2,1,0:T(8,128)(2,1)}), bf16[8,128,128]{2,1,0:T(8,128)(2,1)S(1)}, u32[]{:S(2)}, u32[]{:S(2)}) async-start(bf16[8,128,128]{2,1,0:T(8,128)(2,1)} %broadcast_in_dim.91), calls=%async_computation.1 | async-start | bytes 524288 | tf_op jit(solution)/shard_map/all_to_all | solution.py:60
  62.0 22.2 %collective-permute-start.9 = (bf16[2048,128]{1,0:T(8,128)(2,1)}, bf16[2048,128]{1,0:T(8,128)(2,1)}, u32[]{:S(2)}, u32[]{:S(2)}) collective-permute-start(bf16[2048,128]{1,0:T(8,128)(2,1)} %w0), channel_id=1, source_target_pairs={{0,8},{8,16},{16,24},{24,0},{1,9},{9,17},{17,25},{25,1},{2,10},{10... | collective-permute-start | bytes 1572872 | tf_op jit(solution)/shard_map/ppermute | solution.py:56
  63.2 21.0 %collective-permute-start.10 = (bf16[2048,128]{1,0:T(8,128)(2,1)}, bf16[2048,128]{1,0:T(8,128)(2,1)}, u32[]{:S(2)}, u32[]{:S(2)}) collective-permute-start(bf16[2048,128]{1,0:T(8,128)(2,1)} %w0), channel_id=1, source_target_pairs={{0,24},{8,0},{16,8},{24,16},{1,25},{9,1},{17,9},{25,17},{2,26},{10... | collective-permute-start | bytes 1572872 | tf_op jit(solution)/shard_map/ppermute | solution.py:56
  73.6 1.5 collective-permute-start.7
  81.9 1.5 collective-permute-start.8
  84.2 37.2 %collective-permute-start.15 = (bf16[8,2,336,128]{3,2,1,0:T(8,128)(2,1)}, bf16[8,2,336,128]{3,2,1,0:T(8,128)(2,1)}, u32[]{:S(2)}, u32[]{:S(2)}) collective-permute-start(bf16[8,2,336,128]{3,2,1,0:T(8,128)(2,1)} %get-tuple-element.81), channel_id=1, source_target_pairs={{0,2},{1,3},{2,0},{3,1},{4,6},{5,7},{6,4},{7,5},{8,10},{9,11},{10,... | collective-permute-start | bytes 4128776 | tf_op jit(solution)/shard_map/ppermute | solution.py:31
  87.5 14.1 %all-to-all-start.2 = ((bf16[8,80,128]{2,1,0:T(8,128)(2,1)}), bf16[8,80,128]{2,1,0:T(8,128)(2,1)}, u32[]{:S(2)}, u32[]{:S(2)}) async-start(bf16[8,80,128]{2,1,0:T(8,128)(2,1)} %merge.1), calls=%async_computation.2 | async-start | bytes 327680 | tf_op jit(solution)/shard_map/all_to_all | solution.py:60
  91.5 26.8 %collective-permute-start.14 = (bf16[2048,128]{1,0:T(8,128)(2,1)}, bf16[2048,128]{1,0:T(8,128)(2,1)}, u32[]{:S(2)}, u32[]{:S(2)}) collective-permute-start(bf16[2048,128]{1,0:T(8,128)(2,1)} %w0), channel_id=1, source_target_pairs={{0,16},{8,24},{16,0},{24,8},{1,17},{9,25},{17,1},{25,9},{2,18},{10... | collective-permute-start | bytes 1572872 | tf_op jit(solution)/shard_map/ppermute | solution.py:56
  116.0 2.3 collective-permute-start.13
  116.0 9.8 %collective-permute-start.3 = (bf16[80,128]{1,0:T(8,128)(2,1)}, bf16[80,128]{1,0:T(8,128)(2,1)S(1)}, u32[]{:S(2)}, u32[]{:S(2)}) collective-permute-start(bf16[80,128]{1,0:T(8,128)(2,1)} %pad_maximum_fusion.6), channel_id=1, source_target_pairs={{0,0},{1,8},{2,16},{3,24},{8,1},{9,9},{10,17},{11,25},{16,2},{17,1... | collective-permute-start | bytes 61448 | tf_op jit(solution)/shard_map/ppermute | solution.py:40
  121.5 4.4 %collective-permute-start.18 = (bf16[64,128]{1,0:T(8,128)(2,1)S(1)}, bf16[64,128]{1,0:T(8,128)(2,1)S(1)}, u32[]{:S(2)}, u32[]{:S(2)}) collective-permute-start(bf16[64,128]{1,0:T(8,128)(2,1)S(1)} %get-tuple-element.125), channel_id=1, source_target_pairs={{0,3},{1,0},{2,1},{3,2},{4,7},{5,4},{6,5},{7,6},{8,11},{9,8},{10,9... | collective-permute-start | bytes 49160 | tf_op jit(solution)/shard_map/ppermute | solution.py:31
  122.7 5.3 %collective-permute-start.17 = (bf16[64,128]{1,0:T(8,128)(2,1)S(1)}, bf16[64,128]{1,0:T(8,128)(2,1)S(1)}, u32[]{:S(2)}, u32[]{:S(2)}) collective-permute-start(bf16[64,128]{1,0:T(8,128)(2,1)S(1)} %get-tuple-element.126), channel_id=1, source_target_pairs={{0,2},{1,3},{2,0},{3,1},{4,6},{5,7},{6,4},{7,5},{8,10},{9,11},{10,... | collective-permute-start | bytes 49160 | tf_op jit(solution)/shard_map/ppermute | solution.py:31
  123.9 4.9 %collective-permute-start.16 = (bf16[64,128]{1,0:T(8,128)(2,1)S(1)}, bf16[64,128]{1,0:T(8,128)(2,1)S(1)}, u32[]{:S(2)}, u32[]{:S(2)}) collective-permute-start(bf16[64,128]{1,0:T(8,128)(2,1)S(1)} %get-tuple-element.124), channel_id=1, source_target_pairs={{0,1},{1,2},{2,3},{3,0},{4,5},{5,6},{6,7},{7,4},{8,9},{9,10},{10,1... | collective-permute-start | bytes 49160 | tf_op jit(solution)/shard_map/ppermute | solution.py:31
  159.1 2.1 collective-permute-start.19
  164.4 6.2 %collective-permute-start.20 = (bf16[240,256]{1,0:T(8,128)(2,1)S(1)}, bf16[240,256]{1,0:T(8,128)(2,1)S(1)}, u32[]{:S(2)}, u32[]{:S(2)}) collective-permute-start(bf16[240,256]{1,0:T(8,128)(2,1)S(1)} %get-tuple-element.88), channel_id=1, source_target_pairs={{0,3},{1,0},{2,1},{3,2},{4,7},{5,4},{6,5},{7,6},{8,11},{9,8},{10,9... | collective-permute-start | bytes 368648 | tf_op jit(solution)/shard_map/ppermute | solution.py:31
  165.2 7.6 %collective-permute-start.21 = (bf16[240,256]{1,0:T(8,128)(2,1)S(1)}, bf16[240,256]{1,0:T(8,128)(2,1)S(1)}, u32[]{:S(2)}, u32[]{:S(2)}) collective-permute-start(bf16[240,256]{1,0:T(8,128)(2,1)S(1)} %get-tuple-element.89), channel_id=1, source_target_pairs={{0,2},{1,3},{2,0},{3,1},{4,6},{5,7},{6,4},{7,5},{8,10},{9,11},{10,... | collective-permute-start | bytes 368648 | tf_op jit(solution)/shard_map/ppermute | solution.py:31
  166.5 7.9 %collective-permute-start.22 = (bf16[240,256]{1,0:T(8,128)(2,1)S(1)}, bf16[240,256]{1,0:T(8,128)(2,1)S(1)}, u32[]{:S(2)}, u32[]{:S(2)}) collective-permute-start(bf16[240,256]{1,0:T(8,128)(2,1)S(1)} %get-tuple-element.90), channel_id=1, source_target_pairs={{0,1},{1,2},{2,3},{3,0},{4,5},{5,6},{6,7},{7,4},{8,9},{9,10},{10,1... | collective-permute-start | bytes 368648 | tf_op jit(solution)/shard_map/ppermute | solution.py:31
  174.6 6.2 %collective-permute-start.23 = (bf16[112,256]{1,0:T(8,128)(2,1)S(1)}, bf16[112,256]{1,0:T(8,128)(2,1)S(1)}, u32[]{:S(2)}, u32[]{:S(2)}) collective-permute-start(bf16[112,256]{1,0:T(8,128)(2,1)S(1)} %act.1.a0), channel_id=1, source_target_pairs={{0,1},{1,2},{2,3},{3,0},{4,5},{5,6},{6,7},{7,4},{8,9},{9,10},{10,1... | collective-permute-start | bytes 172040 | tf_op jit(solution)/shard_map/ppermute | solution.py:31
  174.6 6.1 %collective-permute-start.24 = (bf16[112,256]{1,0:T(8,128)(2,1)S(1)}, bf16[112,256]{1,0:T(8,128)(2,1)S(1)}, u32[]{:S(2)}, u32[]{:S(2)}) collective-permute-start(bf16[112,256]{1,0:T(8,128)(2,1)S(1)} %act.1.a0), channel_id=1, source_target_pairs={{0,2},{1,3},{2,0},{3,1},{4,6},{5,7},{6,4},{7,5},{8,10},{9,11},{10,... | collective-permute-start | bytes 172040 | tf_op jit(solution)/shard_map/ppermute | solution.py:31
  176.8 4.7 %collective-permute-start.25 = (bf16[112,256]{1,0:T(8,128)(2,1)S(1)}, bf16[112,256]{1,0:T(8,128)(2,1)S(1)}, u32[]{:S(2)}, u32[]{:S(2)}) collective-permute-start(bf16[112,256]{1,0:T(8,128)(2,1)S(1)} %act.1.a0), channel_id=1, source_target_pairs={{0,3},{1,0},{2,1},{3,2},{4,7},{5,4},{6,5},{7,6},{8,11},{9,8},{10,9... | collective-permute-start | bytes 172040 | tf_op jit(solution)/shard_map/ppermute | solution.py:31
  183.7 2.0 collective-permute-start.26
  188.9 34.1 %all-to-all-start.5 = ((bf16[32,128,128]{2,1,0:T(8,128)(2,1)}), bf16[32,128,128]{2,1,0:T(8,128)(2,1)S(1)}, u32[]{:S(2)}, u32[]{:S(2)}) async-start(bf16[32,128,128]{2,1,0:T(8,128)(2,1)} %copy-done), calls=%async_computation.5 | async-start | bytes 2097152 | tf_op jit(solution)/shard_map/all_to_all | solution.py:44
  223.1 9.5 %collective-permute-start.27 = (bf16[64,128]{1,0:T(8,128)(2,1)S(1)}, bf16[64,128]{1,0:T(8,128)(2,1)S(1)}, u32[]{:S(2)}, u32[]{:S(2)}) collective-permute-start(bf16[64,128]{1,0:T(8,128)(2,1)S(1)} %add_convert_fusion), channel_id=1, source_target_pairs={{0,0},{1,8},{2,16},{3,24},{8,1},{9,9},{10,17},{11,25},{16,2},{17,1... | collective-permute-start | bytes 49160 | tf_op jit(solution)/shard_map/ppermute | solution.py:40
  (18 other events, 77.2 us)

commit v5 on v4

--- a/solution.py
+++ b/solution.py
@@ -118,6 +118,41 @@
     rest = value - high
     middle = rest.astype(BF).astype(F32)
     return [high, middle, rest - middle]
+
+
+VMEM = pl.BlockSpec(memory_space=pltpu.VMEM)
+SMEM = pl.BlockSpec(memory_space=pltpu.SMEM)
+
+
+def grant(mib):
+    return pltpu.CompilerParams(vmem_limit_bytes=mib * 1024 * 1024)
+
+
+def scale_kernel(in_ref, out_ref):
+    value = in_ref[0].astype(F32)
+    for k in range(1, 32):
+        value = value + in_ref[k].astype(F32)
+    squares = value[128:129] + (value[129:130] + value[130:131])
+    factor = jnp.broadcast_to(lax.rsqrt(squares / D + EPS), (8, 128)).T
+    by_x = factor[0:64, 0:1]
+    by_z = factor[64:96, 0:1]
+    result = jnp.concatenate(
+        [value[0:64] * by_x, value[64:96] * by_z, value[96:128] * by_z], axis=0
+    ).astype(BF)
+    for k in range(NZ):
+        out_ref[k] = result
+
+
+def scale(value):
+    return pl.pallas_call(
+        scale_kernel,
+        out_shape=jax.ShapeDtypeStruct((NZ, 128, 128), BF),
+        in_specs=[VMEM],
+        out_specs=VMEM,
+        compiler_params=grant(6),
+        cost_estimate=pl.CostEstimate(flops=600_000, bytes_accessed=1_500_000, transcendentals=0),
+        name="scale",
+    )(value)
 
 
 def attend_kernel(
@@ -200,10 +235,6 @@
         out_ref[head, 64:80, :] = stats[:, pair * 128 : pair * 128 + 128]
 
 
-VMEM = pl.BlockSpec(memory_space=pltpu.VMEM)
-SMEM = pl.BlockSpec(memory_space=pltpu.SMEM)
-
-
 def merge(*operands):
     return pl.pallas_call(
         merge_kernel,
@@ -219,7 +250,7 @@
 def finish_kernel(
     place_ref, arrived_ref, own_ref, bias_ref, out_ref, column_ref, new_ref
 ):
-    z = place_ref[0]
+    z = place_ref[2]
     keys = jnp.concatenate([own_ref[k, 64:96, :] for k in range(8)], axis=0)
     values = jnp.concatenate([own_ref[k, 96:128, :] for k in range(8)], axis=0)
     query = own_ref[z, 0:64, :]
@@ -267,8 +298,10 @@
     )(*operands)
 
 
-def project_kernel(place_ref, own_ref, far_ref, w0, w1, w2, w3, out_ref):
+def project_kernel(place_ref, own_ref, far_ref, w0, w1, w2, w3, keep_ref, out_ref):
     core = place_ref[0]
+    y = place_ref[1]
+    x = place_ref[3]
     for k, weight_ref in enumerate((w0, w1, w2, w3)):
         value = jnp.zeros((64, 128), F32)
         for rel, ref in enumerate((own_ref, far_ref)):
@@ -276,20 +309,61 @@
             at = pl.ds(pl.multiple_of(group * 1024, 1024), 1024)
             rows = jnp.concatenate([ref[i] for i in range(8)], axis=1)
             value = value + jnp.dot(rows, weight_ref[at, :], preferred_element_type=F32)
-        out_ref[k] = value
+        step = lax.rem(x - y - k + 2 * NX, NX)
+        out_ref[step] = value.astype(BF)
+
+        @pl.when(step == 0)
+        def _():
+            keep_ref[...] = value
 
 
 def project(*operands):
     return pl.pallas_call(
         project_kernel,
-        out_shape=jax.ShapeDtypeStruct((NX, 64, 128), F32),
+        out_shape=(
+            jax.ShapeDtypeStruct((64, 128), F32),
+            jax.ShapeDtypeStruct((NX, 64, 128), BF),
+        ),
         in_specs=[SMEM] + [VMEM] * 6,
-        out_specs=VMEM,
-        compiler_params=pltpu.CompilerParams(vmem_limit_bytes=8 * 1024 * 1024),
+        out_specs=(VMEM, VMEM),
+        compiler_params=grant(8),
         cost_estimate=pl.CostEstimate(
             flops=2 * 64 * 2048 * 512, bytes_accessed=2_500_000, transcendentals=0
         ),
         name="project",
+    )(*operands)
+
+
+def middle_kernel(place_ref, keep_ref, r1, r2, r3, early_ref, mid_ref, out_ref):
+    x = place_ref[3]
+    mid = early_ref[0:64, :].astype(F32) + keep_ref[...]
+    for ref in (r1, r2, r3):
+        mid = mid + ref[...].astype(F32)
+    mid_ref[...] = mid
+    gain = early_ref[64:80, :].astype(F32)[0:1]
+    feature = (mid * gain).astype(BF)
+    both = jnp.concatenate([mid, mid], axis=0)
+    squares = jnp.sum((both * both).T, axis=0, keepdims=True)
+    lane = lax.broadcasted_iota(jnp.int32, (1, 128), 1)
+    squares = jnp.where(lane // 64 == lax.rem(x, 2), squares, 0.0)
+    rows = jnp.concatenate(split_rows(squares) + [jnp.zeros((13, 128), F32)], axis=0).astype(BF)
+    for k in range(32):
+        out_ref[k, 0:64, :] = feature
+        out_ref[k, 64:80, :] = rows
+
+
+def middle(*operands):
+    return pl.pallas_call(
+        middle_kernel,
+        out_shape=(
+            jax.ShapeDtypeStruct((64, 128), F32),
+            jax.ShapeDtypeStruct((32, 80, 128), BF),
+        ),
+        in_specs=[SMEM] + [VMEM] * 5,
+        out_specs=(VMEM, VMEM),
+        compiler_params=grant(6),
+        cost_estimate=pl.CostEstimate(flops=100_000, bytes_accessed=800_000, transcendentals=0),
+        name="middle",
     )(*operands)
 
 
@@ -426,6 +500,17 @@
             axis=1,
         )
 
+    place = jnp.stack([c, y, z, x]).astype(jnp.int32)
+
+    early = jnp.concatenate(
+        [
+            lax.dynamic_slice_in_dim(hidden_rows, y * 64, 64, 0),
+            jnp.broadcast_to(ffn_gain[None, :], (16, 128)),
+        ],
+        axis=0,
+    )
+    early = permute_xy(early, lambda a, b: (b, a))
+
     message = jnp.concatenate(
         [hidden_rows, jnp.broadcast_to(attn_gain[None, :], (16, 128))], axis=0
     )
@@ -457,13 +542,6 @@
     new_part = jnp.broadcast_to(new_part.reshape(8, 1, 64, 128), (8, 4, 64, 128))
     payload = jnp.concatenate([query_part, new_part, square_parts], axis=2).reshape(32, 136, 128)
 
-    early = jnp.concatenate(
-        [
-            lax.dynamic_slice_in_dim(hidden_rows, y * 64, 64, 0),
-            jnp.broadcast_to(ffn_gain[None, :], (16, 128)),
-        ],
-        axis=0,
-    )
     payload, cache, sel_index, doc_order, early = hold(
         payload, cache, sel_index, doc_order, early
     )
@@ -471,19 +549,11 @@
     reordered = reordered.reshape(32, 2, 8, 512)
     stay = lax.dynamic_index_in_dim(reordered, c, 1, keepdims=False)
     leave = lax.dynamic_index_in_dim(reordered, other, 1, keepdims=False)
-    come, w_in, w_out, early = hold(exchange_cores(leave), w_in, w_out, early)
-    early = permute_xy(early, lambda a, b: (b, a))
+    come, w_in, w_out = hold(exchange_cores(leave), w_in, w_out)
     right, left, across = shift_x(cache, 1), shift_x(cache, -1), shift_x(cache, 2)
     arrived, right, left, across = hold(swap_zx(payload), right, left, across)
-    total = jnp.sum(arrived.astype(F32), axis=0)
-    square_sum = total[128] + (total[129] + total[130])
-    factor = lax.rsqrt(square_sum / D + EPS)
-    new = total[64:128].reshape(2, 32, 128) * factor[None, 64:96, None]
-    piece = jnp.concatenate(
-        [total[:64] * factor[:64, None], new.reshape(64, 128)], axis=0
-    ).astype(BF)
-
-    place = jnp.stack([c, y, z]).astype(jnp.int32)
+    piece = scale(arrived)
+
     flat_in = jnp.transpose(w_in, (1, 2, 0)).reshape(224, D)
     pieces = weight_slices(place, flat_in, w_out)
     slices = [pieces[0], shift_y(pieces[1], 1), None, shift_y(pieces[3], 3)]
@@ -504,7 +574,7 @@
     new_bias = jnp.where(row_pos[:, None] <= my_pos, 0.0, NEG).astype(BF)
 
     piece, bias, new_bias, pieces, w_output = hold(piece, bias, new_bias, pieces, w_output)
-    own = swap_z(jnp.broadcast_to(piece[None], (8, 128, 128)))
+    own = swap_z(piece)
     wo_right, wo_left = shift_x(w_output, 1), shift_x(w_output, -1)
     others = exchange_cores(own)
     acc, acc_sent, stats = attend(place, bias, own, others, (cache, right, left, across))
@@ -517,33 +587,22 @@
     slices[2] = shift_y(last, 2)
 
     arrived = swap_z(payload)
+
+    piece = finish(place, arrived, own, new_bias)
+    attended = swap_z(piece)
+    attended_theirs = exchange_cores(attended)
+
+    keep, chunks = project(place, attended, attended_theirs, *wo_all)
+    keep, chunks, slices[2] = hold(keep, chunks, slices[2])
+    got = [shift_y(chunks[step], step) for step in range(1, 4)]
+    mid, payload = middle(place, keep, *got, early)
+    payload, stay, come = hold(payload, stay, come)
 
     lower = jnp.where(c == 0, stay, come)
     upper = jnp.where(c == 0, come, stay)
     cache_out = jnp.concatenate([lower, upper], axis=1).reshape(32, 16, 4, 128)
     cache_out = jnp.transpose(cache_out, (0, 2, 1, 3)).reshape(32, 64, 128)
-    arrived, cache_out = hold(arrived, cache_out)
-    piece = finish(place[2:], arrived, own, new_bias)
-    attended = swap_z(piece)
-    attended_theirs = exchange_cores(attended)
-
-    chunks = project(place, attended, attended_theirs, *wo_all)
-    chunks, slices[2] = hold(chunks, slices[2])
-    mid = early[:64].astype(F32) + lax.dynamic_index_in_dim(chunks, (x - y) % NX, 0, keepdims=False)
-    chunks = chunks.astype(BF)
-    for step in range(1, 4):
-        sent = lax.dynamic_index_in_dim(chunks, (x - y - step) % NX, 0, keepdims=False)
-        mid = mid + shift_y(sent, step).astype(F32)
-    feature = (mid * early[64].astype(F32)[None, :]).astype(BF)
-    square_parts = jnp.stack(parts_of(jnp.sum(mid * mid, axis=1)) + [jnp.zeros((64,), BF)] * 13)
-    empty = jnp.zeros_like(square_parts)
-    square_parts = jnp.where(
-        x % 2 == 0,
-        jnp.concatenate([square_parts, empty], axis=1),
-        jnp.concatenate([empty, square_parts], axis=1),
-    )
-    payload = jnp.concatenate([feature, square_parts], axis=0)
-    arrived = swap_zx(jnp.broadcast_to(payload[None], (32, 80, 128)))
+    arrived, cache_out = hold(swap_zx(payload), cache_out)
     arrived_theirs = exchange_cores(arrived)
 
     both, squares, *sent = ffn_in(*slices, arrived, arrived_theirs)

time: 235 us -> 230 us (0.979)
  blocking collectives: 37.6 us -> 11.5 us
  waiting for transfers between devices: 83.4 us -> 98.7 us
  starting transfers between devices: 53.3 us -> 60.1 us
  other arithmetic: 11.9 us -> 8.44 us
    all_to_all x1 -> x0, blocking collectives: 25.5 us -> none  [swap_zx(): return lax.all_to_all(value, ('z', 'x'), 0, 0, tiled=True)]
    all_to_all x2 -> x3, waiting for transfers between devices: 41.2 us -> 48.7 us  [swap_zx(): return lax.all_to_all(value, ('z', 'x'), 0, 0, tiled=True)]
    all_to_all x2 -> x3, starting transfers between devices: 15.7 us -> 23.1 us  [swap_zx(): return lax.all_to_all(value, ('z', 'x'), 0, 0, tiled=True)]
    ppermute x12, waiting for transfers between devices: 12.7 us -> 17.2 us  [shift_y(): return lax.ppermute(value, 'y', [(i, (i + step) % NY) for i in range(NY)])]
    ppermute x2, starting transfers between devices: 5.24 us -> 7.73 us  [permute_xy(): return lax.ppermute(value, ('x', 'y'), pairs)]
    pallas_call x1 -> x3, Pallas kernels: 2.01 us -> 4.43 us  [the longest x1 2.26 us: project(): pl.pallas_call(project_kernel, out_shape=(jax.ShapeDtypeStruct((64, 128),...]
    unnamed x46 -> x54, local copies, waits for them, and re-layouts: 10.8 us -> 11.8 us
  transfers between devices with their start and end apart: 32 -> 33, of which waited for: 17 -> 23; matrix products, arithmetic and copies ran while one was open for 8% -> 9% of each run, Pallas kernels for 6% -> 7%
where the time goes in v5:
time: 230 us; the launch traced here: 229 us
  waiting for transfers between devices  98.7 us (43%)
  starting transfers between devices  60.1 us (26%)
  Pallas kernels  24.6 us (11%)
  local copies, waits for them, and re-layouts  23.5 us (10%)
  blocking collectives  11.5 us (5%)
  other arithmetic  8.44 us (4%)
    all_to_all x3, waiting for transfers between devices, swap_zx(): return lax.all_to_all(value, ('z', 'x'), 0, 0, tiled=True)  48.7 us
    all_to_all x3, starting transfers between devices, swap_zx(): return lax.all_to_all(value, ('z', 'x'), 0, 0, tiled=True)  23.1 us
    ppermute x12, waiting for transfers between devices, shift_y(): return lax.ppermute(value, 'y', [(i, (i + step) % NY) for i in range(NY)])  17.2 us
    all_to_all x2, waiting for transfers between devices, swap_z(): return lax.all_to_all(value, 'z', 0, 0, tiled=True)  17.1 us
    ppermute x12, starting transfers between devices, shift_y(): return lax.ppermute(value, 'y', [(i, (i + step) % NY) for i in range(NY)])  14.9 us
    unnamed x54, local copies, waits for them, and re-layouts  11.8 us
    all_to_all x1, blocking collectives, swap_z(): return lax.all_to_all(value, 'z', 0, 0, tiled=True)  11.5 us
    ppermute x8, waiting for transfers between devices, exchange_cores(): return lax.ppermute(value, 'c', [(0, 1), (1, 0)])  8.41 us
  transfers between devices with their start and end apart: 33, of which 23 were waited for; matrix products, arithmetic and copies ran while one was open for 9% of the time, Pallas kernels for 7%

profile of v5, /device:TPU:4, one launch (start us, length us, event | category | flops | bytes accessed | tf_op | source)
XLA Modules:
  0.0 229.0 jit_solution(18281556898495443765)
XLA Ops:
  2.1 5.0 %collective-permute-start.2 = (bf16[80,128]{1,0:T(8,128)(2,1)S(1)}, bf16[80,128]{1,0:T(8,128)(2,1)S(1)}, u32[]{:S(2)}, u32[]{:S(2)}) collective-permute-start(bf16[80,128]{1,0:T(8,128)(2,1)S(1)} %pad_maximum_fusion.5), channel_id=1, source_target_pairs={{0,0},{1,8},{2,16},{3,24},{8,1},{9,9},{10,17},{11,25},{16,2},{17,1... | collective-permute-start | bytes 61448 | tf_op jit(solution)/shard_map/ppermute | solution.py:40
  15.0 2.4 %collective-permute-start.4 = (bf16[512,512]{1,0:T(8,128)(2,1)S(1)}, bf16[512,512]{1,0:T(8,128)(2,1)}, u32[]{:S(2)}, u32[]{:S(2)}) collective-permute-start(bf16[512,512]{1,0:T(8,128)(2,1)S(1)} %bitcast.70), channel_id=1, source_target_pairs={{0,24},{8,0},{16,8},{24,16},{1,25},{9,1},{17,9},{25,17},{2,26},{10... | collective-permute-start | bytes 1572872 | tf_op jit(solution)/shard_map/ppermute | solution.py:56
  17.6 12.4 %all-to-all-start = ((bf16[32,136,128]{2,1,0:T(8,128)(2,1)}), bf16[32,136,128]{2,1,0:T(8,128)(2,1)}, u32[]{:S(2)}, u32[]{:S(2)}) async-start(bf16[32,136,128]{2,1,0:T(8,128)(2,1)} %bitcast.14), calls=%async_computation | async-start | bytes 2228224 | tf_op jit(solution)/shard_map/all_to_all | solution.py:44
  34.6 2.0 copy-done.1
  38.2 4.8 %weight_slices.1 = (bf16[8,2,336,128]{3,2,1,0:T(8,128)(2,1)S(1)}, bf16[8,2,336,128]{3,2,1,0:T(8,128)(2,1)}, bf16[8,2,336,128]{3,2,1,0:T(8,128)(2,1)}, bf16[8,2,336,128]{3,2,1,0:T(8,128)(2,1)}) custom-call(s32[4]{0:T(128)S(1)} %pad_add_fusion.2.place_ref, bf16[224,8192]{1,0:T(8,128)(2,1)S(1)} %bitcast.68, bf16[112,8192]{1,0:T(8,128)(2,1)S(1)} %copy-done.3), custom_call_target="tpu_custom_call" | custom-call | bytes 11000000 | tf_op jit(solution)/shard_map/weight_slices/pallas_call | solution.py:96
  44.3 2.4 %collective-permute-start.12 = (bf16[8,2,336,128]{3,2,1,0:T(8,128)(2,1)}, bf16[8,2,336,128]{3,2,1,0:T(8,128)(2,1)}, u32[]{:S(2)}, u32[]{:S(2)}) collective-permute-start(bf16[8,2,336,128]{3,2,1,0:T(8,128)(2,1)} %get-tuple-element.66), channel_id=1, source_target_pairs={{0,3},{1,0},{2,1},{3,2},{4,7},{5,4},{6,5},{7,6},{8,11},{9,8},{10,9... | collective-permute-start | bytes 4128776 | tf_op jit(solution)/shard_map/ppermute | solution.py:31
  47.9 2.0 collective-permute-done.3.c1
  49.9 9.4 %all-to-all-done.in_ref = bf16[32,136,128]{2,1,0:T(8,128)(2,1)} async-done(((bf16[32,136,128]{2,1,0:T(8,128)(2,1)}), bf16[32,136,128]{2,1,0:T(8,128)(2,1)}, u32[]{:S(2)}, u32[]{:S(2)}) %all-to-all-start) | async-done | bytes 1114144 | tf_op jit(solution)/shard_map/all_to_all | solution.py:44
  61.5 3.4 %all-to-all-start.1 = ((bf16[8,128,128]{2,1,0:T(8,128)(2,1)}), bf16[8,128,128]{2,1,0:T(8,128)(2,1)S(1)}, u32[]{:S(2)}, u32[]{:S(2)}) async-start(bf16[8,128,128]{2,1,0:T(8,128)(2,1)} %copy-done.6), calls=%async_computation.1 | async-start | bytes 524288 | tf_op jit(solution)/shard_map/all_to_all | solution.py:60
  67.0 9.1 %all-to-all-done.1.own_ref = bf16[8,128,128]{2,1,0:T(8,128)(2,1)S(1)} async-done(((bf16[8,128,128]{2,1,0:T(8,128)(2,1)}), bf16[8,128,128]{2,1,0:T(8,128)(2,1)S(1)}, u32[]{:S(2)}, u32[]{:S(2)}) %all-to-all-start.1) | async-done | bytes 262176 | tf_op jit(solution)/shard_map/all_to_all | solution.py:60
  78.7 5.7 %attend.1 = (f32[128,512]{1,0:T(8,128)S(1)}, bf16[144,512]{1,0:T(8,128)(2,1)S(1)}, f32[8,512]{1,0:T(8,128)S(1)}) custom-call(s32[4]{0:T(128)S(1)} %pad_add_fusion.2.place_ref, bf16[2048,128]{1,0:T(8,128)(2,1)S(1)} %copy-done.9, bf16[8,128,128]{2,1,0:T(8,128)(2,1)S(1)} %all-to-all-done.1.own_ref, bf16[8,128,128]{2,1,0:T(8,128)(2,1)S(1)} %collective-permute-done.7.other_ref, ...), custom_call_target="tpu_custom_call" | custom-call | flops 1073741824 | bytes 6000000 | tf_op jit(solution)/shard_map/attend/pallas_call | solution.py:202
  88.3 3.4 %all-to-all-start.2 = ((bf16[8,80,128]{2,1,0:T(8,128)(2,1)}), bf16[8,80,128]{2,1,0:T(8,128)(2,1)S(1)}, u32[]{:S(2)}, u32[]{:S(2)}) async-start(bf16[8,80,128]{2,1,0:T(8,128)(2,1)} %merge.1), calls=%async_computation.2 | async-start | bytes 327680 | tf_op jit(solution)/shard_map/all_to_all | solution.py:60
  91.7 2.0 collective-permute-start.14
  93.7 8.0 %all-to-all-done.2.arrived_ref = bf16[8,80,128]{2,1,0:T(8,128)(2,1)S(1)} async-done(((bf16[8,80,128]{2,1,0:T(8,128)(2,1)}), bf16[8,80,128]{2,1,0:T(8,128)(2,1)S(1)}, u32[]{:S(2)}, u32[]{:S(2)}) %all-to-all-start.2) | async-done | bytes 163872 | tf_op jit(solution)/shard_map/all_to_all | solution.py:60
  103.6 11.5 %all_to_all.30.own_ref = bf16[8,64,128]{2,1,0:T(8,128)(2,1)S(1)} all-to-all(bf16[8,64,128]{2,1,0:T(8,128)(2,1)S(1)} %finish.1), channel_id=1, replica_groups=mesh['z'=8,'x'=4,'c'=2,'y'=4] {'z'}, dimensions={0} | all-to-all | bytes 262144 | tf_op jit(solution)/shard_map/all_to_all | solution.py:60
  117.5 2.3 project.1
  120.9 2.7 %collective-permute-start.18 = (bf16[64,128]{1,0:T(8,128)(2,1)S(1)}, bf16[64,128]{1,0:T(8,128)(2,1)S(1)}, u32[]{:S(2)}, u32[]{:S(2)}) collective-permute-start(bf16[64,128]{1,0:T(8,128)(2,1)S(1)} %get-tuple-element.134), channel_id=1, source_target_pairs={{0,3},{1,0},{2,1},{3,2},{4,7},{5,4},{6,5},{7,6},{8,11},{9,8},{10,9... | collective-permute-start | bytes 49160 | tf_op jit(solution)/shard_map/ppermute | solution.py:31
  125.0 3.8 %collective-permute-done.17.r2 = bf16[64,128]{1,0:T(8,128)(2,1)S(1)} collective-permute-done((bf16[64,128]{1,0:T(8,128)(2,1)S(1)}, bf16[64,128]{1,0:T(8,128)(2,1)S(1)}, u32[]{:S(2)}, u32[]{:S(2)}) %collective-permute-start.17) | collective-permute-done | bytes 16416 | tf_op jit(solution)/shard_map/ppermute | solution.py:31
  130.6 5.0 %all-to-all-start.4 = ((bf16[32,80,128]{2,1,0:T(8,128)(2,1)}), bf16[32,80,128]{2,1,0:T(8,128)(2,1)S(1)}, u32[]{:S(2)}, u32[]{:S(2)}) async-start(bf16[32,80,128]{2,1,0:T(8,128)(2,1)} %copy-done.7), calls=%async_computation.4 | async-start | bytes 1310720 | tf_op jit(solution)/shard_map/all_to_all | solution.py:44
  137.5 2.0 reshape.364
  141.4 12.4 %all-to-all-done.4.own_ref = bf16[32,80,128]{2,1,0:T(8,128)(2,1)S(1)} async-done(((bf16[32,80,128]{2,1,0:T(8,128)(2,1)}), bf16[32,80,128]{2,1,0:T(8,128)(2,1)S(1)}, u32[]{:S(2)}, u32[]{:S(2)}) %all-to-all-start.4) | async-done | bytes 655392 | tf_op jit(solution)/shard_map/all_to_all | solution.py:44
  153.7 2.1 collective-permute-done.19.far_ref
  155.8 3.2 %ffn_in.1 = (f32[224,256]{1,0:T(8,128)S(1)}, f32[8,256]{1,0:T(8,128)S(1)}, bf16[240,256]{1,0:T(8,128)(2,1)S(1)}, bf16[240,256]{1,0:T(8,128)(2,1)S(1)}, bf16[240,256]{1,0:T(8,128)(2,1)S(1)}) custom-call(bf16[8,2,336,128]{3,2,1,0:T(8,128)(2,1)S(1)} %get-tuple-element.63.p0, bf16[8,2,336,128]{3,2,1,0:T(8,128)(2,1)S(1)} %collective-permute-done.11.p1, ...), custom_call_target="tpu_custom_call" | custom-call | flops 939524096 | bytes 7500000 | tf_op jit(solution)/shard_map/ffn_in/pallas_call | solution.py:397
  162.0 3.4 %collective-permute-done.20.r1 = bf16[240,256]{1,0:T(8,128)(2,1)S(1)} collective-permute-done((bf16[240,256]{1,0:T(8,128)(2,1)S(1)}, bf16[240,256]{1,0:T(8,128)(2,1)S(1)}, u32[]{:S(2)}, u32[]{:S(2)}) %collective-permute-start.20) | collective-permute-done | bytes 122912 | tf_op jit(solution)/shard_map/ppermute | solution.py:31
  166.8 2.0 collective-permute-done.22.r3
  173.4 2.9 %collective-permute-done.24.a2 = bf16[112,256]{1,0:T(8,128)(2,1)S(1)} collective-permute-done((bf16[112,256]{1,0:T(8,128)(2,1)S(1)}, bf16[112,256]{1,0:T(8,128)(2,1)S(1)}, u32[]{:S(2)}, u32[]{:S(2)}) %collective-permute-start.24) | collective-permute-done | bytes 57376 | tf_op jit(solution)/shard_map/ppermute | solution.py:31
  176.6 2.2 down.2
  180.8 2.2 down.3
  184.1 5.7 %all-to-all-start.5 = ((bf16[32,128,128]{2,1,0:T(8,128)(2,1)}), bf16[32,128,128]{2,1,0:T(8,128)(2,1)S(1)}, u32[]{:S(2)}, u32[]{:S(2)}) async-start(bf16[32,128,128]{2,1,0:T(8,128)(2,1)} %copy-done), calls=%async_computation.5 | async-start | bytes 2097152 | tf_op jit(solution)/shard_map/all_to_all | solution.py:44
  191.2 27.0 %all-to-all-done.5 = bf16[32,128,128]{2,1,0:T(8,128)(2,1)S(1)} async-done(((bf16[32,128,128]{2,1,0:T(8,128)(2,1)}), bf16[32,128,128]{2,1,0:T(8,128)(2,1)S(1)}, u32[]{:S(2)}, u32[]{:S(2)}) %all-to-all-start.5) | async-done | bytes 1048608 | tf_op jit(solution)/shard_map/all_to_all | solution.py:44
  218.8 2.7 %collective-permute-start.27 = (bf16[64,128]{1,0:T(8,128)(2,1)S(1)}, bf16[64,128]{1,0:T(8,128)(2,1)S(1)}, u32[]{:S(2)}, u32[]{:S(2)}) collective-permute-start(bf16[64,128]{1,0:T(8,128)(2,1)S(1)} %add_convert_fusion), channel_id=1, source_target_pairs={{0,0},{1,8},{2,16},{3,24},{8,1},{9,9},{10,17},{11,25},{16,2},{17,1... | collective-permute-start | bytes 49160 | tf_op jit(solution)/shard_map/ppermute | solution.py:40
  223.0 5.3 %collective-permute-done.27 = bf16[64,128]{1,0:T(8,128)(2,1)S(1)} collective-permute-done((bf16[64,128]{1,0:T(8,128)(2,1)S(1)}, bf16[64,128]{1,0:T(8,128)(2,1)S(1)}, u32[]{:S(2)}, u32[]{:S(2)}) %collective-permute-start.27) | collective-permute-done | bytes 16416 | tf_op jit(solution)/shard_map/ppermute | solution.py:40
  (202 shorter events, 57.2 us)
Async XLA Ops:
  2.1 12.7 %collective-permute-start.2 = (bf16[80,128]{1,0:T(8,128)(2,1)S(1)}, bf16[80,128]{1,0:T(8,128)(2,1)S(1)}, u32[]{:S(2)}, u32[]{:S(2)}) collective-permute-start(bf16[80,128]{1,0:T(8,128)(2,1)S(1)} %pad_maximum_fusion.5), channel_id=1, source_target_pairs={{0,0},{1,8},{2,16},{3,24},{8,1},{9,9},{10,17},{11,25},{16,2},{17,1... | collective-permute-start | bytes 61448 | tf_op jit(solution)/shard_map/ppermute | solution.py:40
  8.6 3.2 %collective-permute-start = (bf16[272,128]{1,0:T(8,128)(2,1)S(1)}, bf16[272,128]{1,0:T(8,128)(2,1)S(1)}, u32[]{:S(2)}, u32[]{:S(2)}) collective-permute-start(bf16[272,128]{1,0:T(8,128)(2,1)S(1)} %pad_maximum_fusion.4), channel_id=1, source_target_pairs={{0,4},{4,0},{1,5},{5,1},{2,6},{6,2},{3,7},{7,3},{8,12},{12,8},{9,1... | collective-permute-start | bytes 208904 | tf_op jit(solution)/shard_map/ppermute | solution.py:27
  10.3 2.2 collective-permute-start.1
  14.9 33.0 %collective-permute-start.5 = (bf16[512,512]{1,0:T(8,128)(2,1)S(1)}, bf16[512,512]{1,0:T(8,128)(2,1)}, u32[]{:S(2)}, u32[]{:S(2)}) collective-permute-start(bf16[512,512]{1,0:T(8,128)(2,1)S(1)} %bitcast.69), channel_id=1, source_target_pairs={{0,16},{8,24},{16,0},{24,8},{1,17},{9,25},{17,1},{25,9},{2,18},{10... | collective-permute-start | bytes 1572872 | tf_op jit(solution)/shard_map/ppermute | solution.py:56
  15.0 32.9 %collective-permute-start.4 = (bf16[512,512]{1,0:T(8,128)(2,1)S(1)}, bf16[512,512]{1,0:T(8,128)(2,1)}, u32[]{:S(2)}, u32[]{:S(2)}) collective-permute-start(bf16[512,512]{1,0:T(8,128)(2,1)S(1)} %bitcast.70), channel_id=1, source_target_pairs={{0,24},{8,0},{16,8},{24,16},{1,25},{9,1},{17,9},{25,17},{2,26},{10... | collective-permute-start | bytes 1572872 | tf_op jit(solution)/shard_map/ppermute | solution.py:56
  17.4 32.5 %collective-permute-start.3 = (bf16[512,512]{1,0:T(8,128)(2,1)S(1)}, bf16[512,512]{1,0:T(8,128)(2,1)}, u32[]{:S(2)}, u32[]{:S(2)}) collective-permute-start(bf16[512,512]{1,0:T(8,128)(2,1)S(1)} %bitcast.71), channel_id=1, source_target_pairs={{0,8},{8,16},{16,24},{24,0},{1,9},{9,17},{17,25},{25,1},{2,10},{10... | collective-permute-start | bytes 1572872 | tf_op jit(solution)/shard_map/ppermute | solution.py:56
  17.6 41.7 %all-to-all-start = ((bf16[32,136,128]{2,1,0:T(8,128)(2,1)}), bf16[32,136,128]{2,1,0:T(8,128)(2,1)}, u32[]{:S(2)}, u32[]{:S(2)}) async-start(bf16[32,136,128]{2,1,0:T(8,128)(2,1)} %bitcast.14), calls=%async_computation | async-start | bytes 2228224 | tf_op jit(solution)/shard_map/all_to_all | solution.py:44
  32.4 1.5 collective-permute-start.6
  42.9 43.8 %collective-permute-start.11 = (bf16[8,2,336,128]{3,2,1,0:T(8,128)(2,1)}, bf16[8,2,336,128]{3,2,1,0:T(8,128)(2,1)S(1)}, u32[]{:S(2)}, u32[]{:S(2)}) collective-permute-start(bf16[8,2,336,128]{3,2,1,0:T(8,128)(2,1)} %get-tuple-element.64), channel_id=1, source_target_pairs={{0,1},{1,2},{2,3},{3,0},{4,5},{5,6},{6,7},{7,4},{8,9},{9,10},{10,1... | collective-permute-start | bytes 4128776 | tf_op jit(solution)/shard_map/ppermute | solution.py:31
  44.3 42.4 %collective-permute-start.12 = (bf16[8,2,336,128]{3,2,1,0:T(8,128)(2,1)}, bf16[8,2,336,128]{3,2,1,0:T(8,128)(2,1)}, u32[]{:S(2)}, u32[]{:S(2)}) collective-permute-start(bf16[8,2,336,128]{3,2,1,0:T(8,128)(2,1)} %get-tuple-element.66), channel_id=1, source_target_pairs={{0,3},{1,0},{2,1},{3,2},{4,7},{5,4},{6,5},{7,6},{8,11},{9,8},{10,9... | collective-permute-start | bytes 4128776 | tf_op jit(solution)/shard_map/ppermute | solution.py:31
  61.5 14.6 %all-to-all-start.1 = ((bf16[8,128,128]{2,1,0:T(8,128)(2,1)}), bf16[8,128,128]{2,1,0:T(8,128)(2,1)S(1)}, u32[]{:S(2)}, u32[]{:S(2)}) async-start(bf16[8,128,128]{2,1,0:T(8,128)(2,1)} %copy-done.6), calls=%async_computation.1 | async-start | bytes 524288 | tf_op jit(solution)/shard_map/all_to_all | solution.py:60
  64.9 21.8 %collective-permute-start.10 = (bf16[2048,128]{1,0:T(8,128)(2,1)}, bf16[2048,128]{1,0:T(8,128)(2,1)}, u32[]{:S(2)}, u32[]{:S(2)}) collective-permute-start(bf16[2048,128]{1,0:T(8,128)(2,1)} %w0), channel_id=1, source_target_pairs={{0,24},{8,0},{16,8},{24,16},{1,25},{9,1},{17,9},{25,17},{2,26},{10... | collective-permute-start | bytes 1572872 | tf_op jit(solution)/shard_map/ppermute | solution.py:56
  65.5 21.2 %collective-permute-start.9 = (bf16[2048,128]{1,0:T(8,128)(2,1)}, bf16[2048,128]{1,0:T(8,128)(2,1)}, u32[]{:S(2)}, u32[]{:S(2)}) collective-permute-start(bf16[2048,128]{1,0:T(8,128)(2,1)} %w0), channel_id=1, source_target_pairs={{0,8},{8,16},{16,24},{24,0},{1,9},{9,17},{17,25},{25,1},{2,10},{10... | collective-permute-start | bytes 1572872 | tf_op jit(solution)/shard_map/ppermute | solution.py:56
  76.1 1.5 collective-permute-start.7
  84.4 1.5 collective-permute-start.8
  86.7 34.1 %collective-permute-start.15 = (bf16[8,2,336,128]{3,2,1,0:T(8,128)(2,1)}, bf16[8,2,336,128]{3,2,1,0:T(8,128)(2,1)}, u32[]{:S(2)}, u32[]{:S(2)}) collective-permute-start(bf16[8,2,336,128]{3,2,1,0:T(8,128)(2,1)} %get-tuple-element.85), channel_id=1, source_target_pairs={{0,2},{1,3},{2,0},{3,1},{4,6},{5,7},{6,4},{7,5},{8,10},{9,11},{10,... | collective-permute-start | bytes 4128776 | tf_op jit(solution)/shard_map/ppermute | solution.py:31
  88.3 13.4 %all-to-all-start.2 = ((bf16[8,80,128]{2,1,0:T(8,128)(2,1)}), bf16[8,80,128]{2,1,0:T(8,128)(2,1)S(1)}, u32[]{:S(2)}, u32[]{:S(2)}) async-start(bf16[8,80,128]{2,1,0:T(8,128)(2,1)} %merge.1), calls=%async_computation.2 | async-start | bytes 327680 | tf_op jit(solution)/shard_map/all_to_all | solution.py:60
  91.7 23.4 %collective-permute-start.14 = (bf16[2048,128]{1,0:T(8,128)(2,1)}, bf16[2048,128]{1,0:T(8,128)(2,1)}, u32[]{:S(2)}, u32[]{:S(2)}) collective-permute-start(bf16[2048,128]{1,0:T(8,128)(2,1)} %w0), channel_id=1, source_target_pairs={{0,16},{8,24},{16,0},{24,8},{1,17},{9,25},{17,1},{25,9},{2,18},{10... | collective-permute-start | bytes 1572872 | tf_op jit(solution)/shard_map/ppermute | solution.py:56
  120.9 4.2 %collective-permute-start.18 = (bf16[64,128]{1,0:T(8,128)(2,1)S(1)}, bf16[64,128]{1,0:T(8,128)(2,1)S(1)}, u32[]{:S(2)}, u32[]{:S(2)}) collective-permute-start(bf16[64,128]{1,0:T(8,128)(2,1)S(1)} %get-tuple-element.134), channel_id=1, source_target_pairs={{0,3},{1,0},{2,1},{3,2},{4,7},{5,4},{6,5},{7,6},{8,11},{9,8},{10,9... | collective-permute-start | bytes 49160 | tf_op jit(solution)/shard_map/ppermute | solution.py:31
  123.6 5.2 %collective-permute-start.17 = (bf16[64,128]{1,0:T(8,128)(2,1)S(1)}, bf16[64,128]{1,0:T(8,128)(2,1)S(1)}, u32[]{:S(2)}, u32[]{:S(2)}) collective-permute-start(bf16[64,128]{1,0:T(8,128)(2,1)S(1)} %get-tuple-element.135), channel_id=1, source_target_pairs={{0,2},{1,3},{2,0},{3,1},{4,6},{5,7},{6,4},{7,5},{8,10},{9,11},{10,... | collective-permute-start | bytes 49160 | tf_op jit(solution)/shard_map/ppermute | solution.py:31
  124.0 5.0 %collective-permute-start.16 = (bf16[64,128]{1,0:T(8,128)(2,1)S(1)}, bf16[64,128]{1,0:T(8,128)(2,1)S(1)}, u32[]{:S(2)}, u32[]{:S(2)}) collective-permute-start(bf16[64,128]{1,0:T(8,128)(2,1)S(1)} %get-tuple-element.136), channel_id=1, source_target_pairs={{0,1},{1,2},{2,3},{3,0},{4,5},{5,6},{6,7},{7,4},{8,9},{9,10},{10,1... | collective-permute-start | bytes 49160 | tf_op jit(solution)/shard_map/ppermute | solution.py:31
  130.6 23.2 %all-to-all-start.4 = ((bf16[32,80,128]{2,1,0:T(8,128)(2,1)}), bf16[32,80,128]{2,1,0:T(8,128)(2,1)S(1)}, u32[]{:S(2)}, u32[]{:S(2)}) async-start(bf16[32,80,128]{2,1,0:T(8,128)(2,1)} %copy-done.7), calls=%async_computation.4 | async-start | bytes 1310720 | tf_op jit(solution)/shard_map/all_to_all | solution.py:44
  153.7 2.1 collective-permute-start.19
  159.1 6.2 %collective-permute-start.20 = (bf16[240,256]{1,0:T(8,128)(2,1)S(1)}, bf16[240,256]{1,0:T(8,128)(2,1)S(1)}, u32[]{:S(2)}, u32[]{:S(2)}) collective-permute-start(bf16[240,256]{1,0:T(8,128)(2,1)S(1)} %get-tuple-element.102), channel_id=1, source_target_pairs={{0,3},{1,0},{2,1},{3,2},{4,7},{5,4},{6,5},{7,6},{8,11},{9,8},{10,9... | collective-permute-start | bytes 368648 | tf_op jit(solution)/shard_map/ppermute | solution.py:31
  159.3 7.4 %collective-permute-start.21 = (bf16[240,256]{1,0:T(8,128)(2,1)S(1)}, bf16[240,256]{1,0:T(8,128)(2,1)S(1)}, u32[]{:S(2)}, u32[]{:S(2)}) collective-permute-start(bf16[240,256]{1,0:T(8,128)(2,1)S(1)} %get-tuple-element.103), channel_id=1, source_target_pairs={{0,2},{1,3},{2,0},{3,1},{4,6},{5,7},{6,4},{7,5},{8,10},{9,11},{10,... | collective-permute-start | bytes 368648 | tf_op jit(solution)/shard_map/ppermute | solution.py:31
  160.6 8.1 %collective-permute-start.22 = (bf16[240,256]{1,0:T(8,128)(2,1)S(1)}, bf16[240,256]{1,0:T(8,128)(2,1)S(1)}, u32[]{:S(2)}, u32[]{:S(2)}) collective-permute-start(bf16[240,256]{1,0:T(8,128)(2,1)S(1)} %get-tuple-element.104), channel_id=1, source_target_pairs={{0,1},{1,2},{2,3},{3,0},{4,5},{5,6},{6,7},{7,4},{8,9},{9,10},{10,1... | collective-permute-start | bytes 368648 | tf_op jit(solution)/shard_map/ppermute | solution.py:31
  168.9 4.5 %collective-permute-start.25 = (bf16[112,256]{1,0:T(8,128)(2,1)S(1)}, bf16[112,256]{1,0:T(8,128)(2,1)S(1)}, u32[]{:S(2)}, u32[]{:S(2)}) collective-permute-start(bf16[112,256]{1,0:T(8,128)(2,1)S(1)} %act.1.a0), channel_id=1, source_target_pairs={{0,3},{1,0},{2,1},{3,2},{4,7},{5,4},{6,5},{7,6},{8,11},{9,8},{10,9... | collective-permute-start | bytes 172040 | tf_op jit(solution)/shard_map/ppermute | solution.py:31
  170.0 6.3 %collective-permute-start.24 = (bf16[112,256]{1,0:T(8,128)(2,1)S(1)}, bf16[112,256]{1,0:T(8,128)(2,1)S(1)}, u32[]{:S(2)}, u32[]{:S(2)}) collective-permute-start(bf16[112,256]{1,0:T(8,128)(2,1)S(1)} %act.1.a0), channel_id=1, source_target_pairs={{0,2},{1,3},{2,0},{3,1},{4,6},{5,7},{6,4},{7,5},{8,10},{9,11},{10,... | collective-permute-start | bytes 172040 | tf_op jit(solution)/shard_map/ppermute | solution.py:31
  170.9 5.7 %collective-permute-start.23 = (bf16[112,256]{1,0:T(8,128)(2,1)S(1)}, bf16[112,256]{1,0:T(8,128)(2,1)S(1)}, u32[]{:S(2)}, u32[]{:S(2)}) collective-permute-start(bf16[112,256]{1,0:T(8,128)(2,1)S(1)} %act.1.a0), channel_id=1, source_target_pairs={{0,1},{1,2},{2,3},{3,0},{4,5},{5,6},{6,7},{7,4},{8,9},{9,10},{10,1... | collective-permute-start | bytes 172040 | tf_op jit(solution)/shard_map/ppermute | solution.py:31
  178.8 2.0 collective-permute-start.26
  184.1 34.1 %all-to-all-start.5 = ((bf16[32,128,128]{2,1,0:T(8,128)(2,1)}), bf16[32,128,128]{2,1,0:T(8,128)(2,1)S(1)}, u32[]{:S(2)}, u32[]{:S(2)}) async-start(bf16[32,128,128]{2,1,0:T(8,128)(2,1)} %copy-done), calls=%async_computation.5 | async-start | bytes 2097152 | tf_op jit(solution)/shard_map/all_to_all | solution.py:44
  218.8 9.5 %collective-permute-start.27 = (bf16[64,128]{1,0:T(8,128)(2,1)S(1)}, bf16[64,128]{1,0:T(8,128)(2,1)S(1)}, u32[]{:S(2)}, u32[]{:S(2)}) collective-permute-start(bf16[64,128]{1,0:T(8,128)(2,1)S(1)} %add_convert_fusion), channel_id=1, source_target_pairs={{0,0},{1,8},{2,16},{3,24},{8,1},{9,9},{10,17},{11,25},{16,2},{17,1... | collective-permute-start | bytes 49160 | tf_op jit(solution)/shard_map/ppermute | solution.py:40
  (23 other events, 129.6 us)

commit v6 on v5

--- a/solution.py
+++ b/solution.py
@@ -298,7 +298,9 @@
     )(*operands)
 
 
-def project_kernel(place_ref, own_ref, far_ref, w0, w1, w2, w3, keep_ref, out_ref):
+def project_kernel(
+    place_ref, own_ref, far_ref, w0, w1, w2, w3, keep_ref, gain_ref, out_ref
+):
     core = place_ref[0]
     y = place_ref[1]
     x = place_ref[3]
@@ -314,7 +316,9 @@
 
         @pl.when(step == 0)
         def _():
-            keep_ref[...] = value
+            rows = pl.ds(pl.multiple_of(2048 + x * 64, 64), 64)
+            keep_ref[...] = value + weight_ref[rows, :].astype(F32)
+            gain_ref[...] = weight_ref[2304:2320, :]
 
 
 def project(*operands):
@@ -322,10 +326,11 @@
         project_kernel,
         out_shape=(
             jax.ShapeDtypeStruct((64, 128), F32),
+            jax.ShapeDtypeStruct((16, 128), BF),
             jax.ShapeDtypeStruct((NX, 64, 128), BF),
         ),
         in_specs=[SMEM] + [VMEM] * 6,
-        out_specs=(VMEM, VMEM),
+        out_specs=(VMEM,) * 3,
         compiler_params=grant(8),
         cost_estimate=pl.CostEstimate(
             flops=2 * 64 * 2048 * 512, bytes_accessed=2_500_000, transcendentals=0
@@ -334,13 +339,13 @@
     )(*operands)
 
 
-def middle_kernel(place_ref, keep_ref, r1, r2, r3, early_ref, mid_ref, out_ref):
+def middle_kernel(place_ref, keep_ref, r1, r2, r3, gain_ref, mid_ref, out_ref):
     x = place_ref[3]
-    mid = early_ref[0:64, :].astype(F32) + keep_ref[...]
+    mid = keep_ref[...]
     for ref in (r1, r2, r3):
         mid = mid + ref[...].astype(F32)
     mid_ref[...] = mid
-    gain = early_ref[64:80, :].astype(F32)[0:1]
+    gain = gain_ref[...].astype(F32)[0:1]
     feature = (mid * gain).astype(BF)
     both = jnp.concatenate([mid, mid], axis=0)
     squares = jnp.sum((both * both).T, axis=0, keepdims=True)
@@ -367,35 +372,59 @@
     )(*operands)
 
 
-def ffn_in_kernel(p0, p1, p2, p3, own_ref, far_ref, keep_ref, square_ref, s1, s2, s3, feature):
+def gathered(ref, feature):
     pairs = [jnp.zeros((1, 128), F32), jnp.zeros((1, 128), F32)]
-    for rel, ref in enumerate((own_ref, far_ref)):
-        for z in range(NZ):
-            for k in range(4):
-                feature[rel, k * 64 : k * 64 + 64, z * 128 : z * 128 + 128] = ref[
-                    z * 4 + k, 0:64, :
-                ]
-                stat = ref[z * 4 + k, 64:80, :].astype(F32)
-                pairs[k // 2] = pairs[k // 2] + (stat[0:1] + (stat[1:2] + stat[2:3]))
-    squares = jnp.concatenate(pairs, axis=1)
+    for z in range(NZ):
+        for k in range(4):
+            feature[k * 64 : k * 64 + 64, z * 128 : z * 128 + 128] = ref[z * 4 + k, 0:64, :]
+            stat = ref[z * 4 + k, 64:80, :].astype(F32)
+            pairs[k // 2] = pairs[k // 2] + (stat[0:1] + (stat[1:2] + stat[2:3]))
+    return jnp.concatenate(pairs, axis=1)
+
+
+def ffn_product(rel, piece, feature):
+    weight = jnp.concatenate([piece[z, rel, 0:224, :] for z in range(NZ)], axis=1)
+    return lax.dot_general(weight, feature[...], NT, preferred_element_type=F32)
+
+
+def ffn_near_kernel(p0, p1, p2, p3, own_ref, square_ref, t0, t1, t2, t3, feature):
+    square_ref[...] = jnp.broadcast_to(gathered(own_ref, feature), (8, ROWS))
+    for piece, to in ((p0, t0), (p1, t1), (p2, t2), (p3, t3)):
+        to[...] = ffn_product(0, piece, feature)
+
+
+def ffn_far_kernel(
+    p0, p1, p2, p3, far_ref, near_ref, t0, t1, t2, t3, keep_ref, square_ref, s1, s2, s3, feature
+):
+    squares = near_ref[0:1, :] + gathered(far_ref, feature)
     square_ref[...] = jnp.broadcast_to(squares, (8, ROWS))
     rows = jnp.concatenate(split_rows(squares) + [jnp.zeros((13, ROWS), F32)], axis=0).astype(BF)
-    for step, (piece, to) in enumerate(((p1, s1), (p2, s2), (p3, s3), (p0, keep_ref))):
-        value = jnp.zeros((224, ROWS), F32)
-        for rel in range(2):
-            weight = jnp.concatenate([piece[z, rel, 0:224, :] for z in range(NZ)], axis=1)
-            value = value + lax.dot_general(weight, feature[rel], NT, preferred_element_type=F32)
-        if step < 3:
-            to[0:224, :] = value.astype(BF)
-            to[224:240, :] = rows
-        else:
-            to[...] = value
-
-
-def ffn_in(*operands):
+    for piece, term, to in ((p1, t1, s1), (p2, t2, s2), (p3, t3, s3)):
+        to[0:224, :] = (term[...] + ffn_product(1, piece, feature)).astype(BF)
+        to[224:240, :] = rows
+    keep_ref[...] = t0[...] + ffn_product(1, p0, feature)
+
+
+def ffn_near(*operands):
+    term = jax.ShapeDtypeStruct((224, ROWS), F32)
+    return pl.pallas_call(
+        ffn_near_kernel,
+        out_shape=(jax.ShapeDtypeStruct((8, ROWS), F32), term, term, term, term),
+        in_specs=[VMEM] * 5,
+        out_specs=(VMEM,) * 5,
+        scratch_shapes=[pltpu.VMEM((ROWS, 1024), BF)],
+        compiler_params=grant(16),
+        cost_estimate=pl.CostEstimate(
+            flops=896 * 2048 * 256, bytes_accessed=4_000_000, transcendentals=0
+        ),
+        name="ffn_near",
+    )(*operands)
+
+
+def ffn_far(*operands):
     sent = jax.ShapeDtypeStruct((240, ROWS), BF)
     return pl.pallas_call(
-        ffn_in_kernel,
+        ffn_far_kernel,
         out_shape=(
             jax.ShapeDtypeStruct((224, ROWS), F32),
             jax.ShapeDtypeStruct((8, ROWS), F32),
@@ -403,14 +432,14 @@
             sent,
             sent,
         ),
-        in_specs=[VMEM] * 6,
+        in_specs=[VMEM] * 10,
         out_specs=(VMEM,) * 5,
-        scratch_shapes=[pltpu.VMEM((2, ROWS, 1024), BF)],
-        compiler_params=pltpu.CompilerParams(vmem_limit_bytes=16 * 1024 * 1024),
+        scratch_shapes=[pltpu.VMEM((ROWS, 1024), BF)],
+        compiler_params=grant(16),
         cost_estimate=pl.CostEstimate(
-            flops=2 * 896 * 2048 * 256, bytes_accessed=7_500_000, transcendentals=0
-        ),
-        name="ffn_in",
+            flops=896 * 2048 * 256, bytes_accessed=4_000_000, transcendentals=0
+        ),
+        name="ffn_far",
     )(*operands)
 
 
@@ -501,15 +530,6 @@
         )
 
     place = jnp.stack([c, y, z, x]).astype(jnp.int32)
-
-    early = jnp.concatenate(
-        [
-            lax.dynamic_slice_in_dim(hidden_rows, y * 64, 64, 0),
-            jnp.broadcast_to(ffn_gain[None, :], (16, 128)),
-        ],
-        axis=0,
-    )
-    early = permute_xy(early, lambda a, b: (b, a))
 
     message = jnp.concatenate(
         [hidden_rows, jnp.broadcast_to(attn_gain[None, :], (16, 128))], axis=0
@@ -542,9 +562,7 @@
     new_part = jnp.broadcast_to(new_part.reshape(8, 1, 64, 128), (8, 4, 64, 128))
     payload = jnp.concatenate([query_part, new_part, square_parts], axis=2).reshape(32, 136, 128)
 
-    payload, cache, sel_index, doc_order, early = hold(
-        payload, cache, sel_index, doc_order, early
-    )
+    payload, cache, sel_index, doc_order = hold(payload, cache, sel_index, doc_order)
     reordered = cache.reshape(POOL, 8, 512).at[doc_order].get(mode="promise_in_bounds")
     reordered = reordered.reshape(32, 2, 8, 512)
     stay = lax.dynamic_index_in_dim(reordered, c, 1, keepdims=False)
@@ -557,6 +575,10 @@
     flat_in = jnp.transpose(w_in, (1, 2, 0)).reshape(224, D)
     pieces = weight_slices(place, flat_in, w_out)
     slices = [pieces[0], shift_y(pieces[1], 1), None, shift_y(pieces[3], 3)]
+
+    w_output = jnp.concatenate(
+        [w_output, hidden_rows, jnp.broadcast_to(ffn_gain[None, :], (16, 128))], axis=0
+    )
 
     slot_of_doc, row_pos = positions(sel_index, doc_order)
     my_pos = lax.dynamic_slice_in_dim(row_pos, x * 64, 64, 0)
@@ -585,17 +607,16 @@
     )
     wo_all = [w_output, wo_right, shift_x(w_output, 2), wo_left]
     slices[2] = shift_y(last, 2)
-
     arrived = swap_z(payload)
 
     piece = finish(place, arrived, own, new_bias)
     attended = swap_z(piece)
     attended_theirs = exchange_cores(attended)
 
-    keep, chunks = project(place, attended, attended_theirs, *wo_all)
+    keep, gain, chunks = project(place, attended, attended_theirs, *wo_all)
     keep, chunks, slices[2] = hold(keep, chunks, slices[2])
     got = [shift_y(chunks[step], step) for step in range(1, 4)]
-    mid, payload = middle(place, keep, *got, early)
+    mid, payload = middle(place, keep, *got, gain)
     payload, stay, come = hold(payload, stay, come)
 
     lower = jnp.where(c == 0, stay, come)
@@ -605,7 +626,7 @@
     arrived, cache_out = hold(swap_zx(payload), cache_out)
     arrived_theirs = exchange_cores(arrived)
 
-    both, squares, *sent = ffn_in(*slices, arrived, arrived_theirs)
+    both, squares, *sent = ffn_far(*slices, arrived_theirs, *ffn_near(*slices, arrived))
     got = [shift_y(sent[step - 1], -step) for step in range(1, 4)]
     act = act_of(both, squares, *got)
     acts = [act] + [shift_y(act, step) for step in range(1, 4)]

time: 230 us -> 226 us (0.983)
  waiting for transfers between devices: 98.7 us -> 94.2 us
  starting transfers between devices: 60.1 us -> 57.4 us
  Pallas kernels: 24.6 us -> 27.3 us
    ppermute x2 -> x1, starting transfers between devices: 7.73 us -> 2.8 us  [permute_xy(): return lax.ppermute(value, ('x', 'y'), pairs)]
    pallas_call x1 -> x2, Pallas kernels: 3.22 us -> 5.19 us  [the longest x1 2.61 us: ffn_far(): pl.pallas_call(ffn_far_kernel, out_shape=(jax.ShapeDtypeStruct((224, ROWS...]
    unnamed x54 -> x48, local copies, waits for them, and re-layouts: 11.8 us -> 11.6 us
    ppermute x2 -> x1, waiting for transfers between devices: 5.35 us -> 5.24 us  [permute_xy(): return lax.ppermute(value, ('x', 'y'), pairs)]
  transfers between devices with their start and end apart: 33 -> 32, of which waited for: 23 -> 20; matrix products, arithmetic and copies ran while one was open for 9% -> 9% of each run, Pallas kernels for 7% -> 9%
where the time goes in v6:
time: 226 us; the launch traced here: 225 us
  waiting for transfers between devices  94.2 us (42%)
  starting transfers between devices  57.4 us (25%)
  Pallas kernels  27.3 us (12%)
  local copies, waits for them, and re-layouts  23 us (10%)
  blocking collectives  11.5 us (5%)
  other arithmetic  9.4 us (4%)
    all_to_all x3, waiting for transfers between devices, swap_zx(): return lax.all_to_all(value, ('z', 'x'), 0, 0, tiled=True)  47.8 us
    all_to_all x3, starting transfers between devices, swap_zx(): return lax.all_to_all(value, ('z', 'x'), 0, 0, tiled=True)  22.4 us
    all_to_all x2, waiting for transfers between devices, swap_z(): return lax.all_to_all(value, 'z', 0, 0, tiled=True)  17.9 us
    ppermute x12, starting transfers between devices, shift_y(): return lax.ppermute(value, 'y', [(i, (i + step) % NY) for i in range(NY)])  16.9 us
    ppermute x12, waiting for transfers between devices, shift_y(): return lax.ppermute(value, 'y', [(i, (i + step) % NY) for i in range(NY)])  16.1 us
    unnamed x48, local copies, waits for them, and re-layouts  11.6 us
    all_to_all x1, blocking collectives, swap_z(): return lax.all_to_all(value, 'z', 0, 0, tiled=True)  11.5 us
    all_to_all x2, starting transfers between devices, swap_z(): return lax.all_to_all(value, 'z', 0, 0, tiled=True)  7.44 us
  transfers between devices with their start and end apart: 32, of which 20 were waited for; matrix products, arithmetic and copies ran while one was open for 9% of the time, Pallas kernels for 9%

profile of v6, /device:TPU:4, one launch (start us, length us, event | category | flops | bytes accessed | tf_op | source)
XLA Modules:
  0.0 224.9 jit_solution(16333209744513724228)
XLA Ops:
  9.4 2.3 %collective-permute-start.4 = (bf16[512,512]{1,0:T(8,128)(2,1)}, bf16[512,512]{1,0:T(8,128)(2,1)}, u32[]{:S(2)}, u32[]{:S(2)}) collective-permute-start(bf16[512,512]{1,0:T(8,128)(2,1)} %bitcast.43.c0), channel_id=1, source_target_pairs={{0,16},{8,24},{16,0},{24,8},{1,17},{9,25},{17,1},{25,9},{2,18},{10... | collective-permute-start | bytes 1572872 | tf_op jit(solution)/shard_map/ppermute | solution.py:56
  13.8 11.8 %all-to-all-start = ((bf16[32,136,128]{2,1,0:T(8,128)(2,1)}), bf16[32,136,128]{2,1,0:T(8,128)(2,1)}, u32[]{:S(2)}, u32[]{:S(2)}) async-start(bf16[32,136,128]{2,1,0:T(8,128)(2,1)} %bitcast.14), calls=%async_computation | async-start | bytes 2228224 | tf_op jit(solution)/shard_map/all_to_all | solution.py:44
  31.3 2.0 copy-done.1
  34.8 4.8 %weight_slices.1 = (bf16[8,2,336,128]{3,2,1,0:T(8,128)(2,1)S(1)}, bf16[8,2,336,128]{3,2,1,0:T(8,128)(2,1)}, bf16[8,2,336,128]{3,2,1,0:T(8,128)(2,1)}, bf16[8,2,336,128]{3,2,1,0:T(8,128)(2,1)}) custom-call(s32[4]{0:T(128)S(1)} %pad_add_fusion.2.place_ref, bf16[224,8192]{1,0:T(8,128)(2,1)S(1)} %bitcast.68, bf16[112,8192]{1,0:T(8,128)(2,1)S(1)} %copy-done.3), custom_call_target="tpu_custom_call" | custom-call | bytes 11000000 | tf_op jit(solution)/shard_map/weight_slices/pallas_call | solution.py:96
  44.6 10.0 %all-to-all-done.in_ref = bf16[32,136,128]{2,1,0:T(8,128)(2,1)} async-done(((bf16[32,136,128]{2,1,0:T(8,128)(2,1)}), bf16[32,136,128]{2,1,0:T(8,128)(2,1)}, u32[]{:S(2)}, u32[]{:S(2)}) %all-to-all-start) | async-done | bytes 1114144 | tf_op jit(solution)/shard_map/all_to_all | solution.py:44
  56.8 4.1 %all-to-all-start.1 = ((bf16[8,128,128]{2,1,0:T(8,128)(2,1)}), bf16[8,128,128]{2,1,0:T(8,128)(2,1)}, u32[]{:S(2)}, u32[]{:S(2)}) async-start(bf16[8,128,128]{2,1,0:T(8,128)(2,1)} %copy-done.4), calls=%async_computation.1 | async-start | bytes 524288 | tf_op jit(solution)/shard_map/all_to_all | solution.py:60
  63.0 8.4 %all-to-all-done.1.own_ref = bf16[8,128,128]{2,1,0:T(8,128)(2,1)} async-done(((bf16[8,128,128]{2,1,0:T(8,128)(2,1)}), bf16[8,128,128]{2,1,0:T(8,128)(2,1)}, u32[]{:S(2)}, u32[]{:S(2)}) %all-to-all-start.1) | async-done | bytes 262176 | tf_op jit(solution)/shard_map/all_to_all | solution.py:60
  74.1 5.9 %attend.1 = (f32[128,512]{1,0:T(8,128)S(1)}, bf16[144,512]{1,0:T(8,128)(2,1)S(1)}, f32[8,512]{1,0:T(8,128)S(1)}) custom-call(s32[4]{0:T(128)S(1)} %pad_add_fusion.2.place_ref, bf16[2048,128]{1,0:T(8,128)(2,1)S(1)} %copy-done.6, bf16[8,128,128]{2,1,0:T(8,128)(2,1)} %all-to-all-done.1.own_ref, bf16[8,128,128]{2,1,0:T(8,128)(2,1)S(1)} %collective-permute-done.6.other_ref, ...), custom_call_target="tpu_custom_call" | custom-call | flops 1073741824 | bytes 6000000 | tf_op jit(solution)/shard_map/attend/pallas_call | solution.py:202
  82.4 3.3 %collective-permute-start.14 = (bf16[8,2,336,128]{3,2,1,0:T(8,128)(2,1)}, bf16[8,2,336,128]{3,2,1,0:T(8,128)(2,1)}, u32[]{:S(2)}, u32[]{:S(2)}) collective-permute-start(bf16[8,2,336,128]{3,2,1,0:T(8,128)(2,1)} %get-tuple-element.90), channel_id=1, source_target_pairs={{0,2},{1,3},{2,0},{3,1},{4,6},{5,7},{6,4},{7,5},{8,10},{9,11},{10,... | collective-permute-start | bytes 4128776 | tf_op jit(solution)/shard_map/ppermute | solution.py:31
  85.7 3.4 %all-to-all-start.2 = ((bf16[8,80,128]{2,1,0:T(8,128)(2,1)}), bf16[8,80,128]{2,1,0:T(8,128)(2,1)S(1)}, u32[]{:S(2)}, u32[]{:S(2)}) async-start(bf16[8,80,128]{2,1,0:T(8,128)(2,1)} %merge.1), calls=%async_computation.2 | async-start | bytes 327680 | tf_op jit(solution)/shard_map/all_to_all | solution.py:60
  89.5 9.6 %all-to-all-done.2.arrived_ref = bf16[8,80,128]{2,1,0:T(8,128)(2,1)S(1)} async-done(((bf16[8,80,128]{2,1,0:T(8,128)(2,1)}), bf16[8,80,128]{2,1,0:T(8,128)(2,1)S(1)}, u32[]{:S(2)}, u32[]{:S(2)}) %all-to-all-start.2) | async-done | bytes 163872 | tf_op jit(solution)/shard_map/all_to_all | solution.py:60
  101.4 11.5 %all_to_all.30.own_ref = bf16[8,64,128]{2,1,0:T(8,128)(2,1)S(1)} all-to-all(bf16[8,64,128]{2,1,0:T(8,128)(2,1)S(1)} %finish.1), channel_id=1, replica_groups=mesh['z'=8,'x'=4,'c'=2,'y'=4] {'z'}, dimensions={0} | all-to-all | bytes 262144 | tf_op jit(solution)/shard_map/all_to_all | solution.py:60
  114.2 2.3 %project.1 = (f32[64,128]{1,0:T(8,128)S(1)}, bf16[16,128]{1,0:T(8,128)(2,1)S(1)}, bf16[4,64,128]{2,1,0:T(8,128)(2,1)S(1)}) custom-call(s32[4]{0:T(128)S(1)} %pad_add_fusion.2.place_ref, bf16[8,64,128]{2,1,0:T(8,128)(2,1)S(1)} %all_to_all.30.own_ref, bf16[8,64,128]{2,1,0:T(8,128)(2,1)S(1)} %collective-permute-done.12.far_ref, ...), custom_call_target="tpu_custom_call" | custom-call | flops 134217728 | bytes 2500000 | tf_op jit(solution)/shard_map/project/pallas_call | solution.py:325
  116.6 2.9 %collective-permute-start.17 = (bf16[64,128]{1,0:T(8,128)(2,1)S(1)}, bf16[64,128]{1,0:T(8,128)(2,1)S(1)}, u32[]{:S(2)}, u32[]{:S(2)}) collective-permute-start(bf16[64,128]{1,0:T(8,128)(2,1)S(1)} %get-tuple-element.144), channel_id=1, source_target_pairs={{0,3},{1,0},{2,1},{3,2},{4,7},{5,4},{6,5},{7,6},{8,11},{9,8},{10,9... | collective-permute-start | bytes 49160 | tf_op jit(solution)/shard_map/ppermute | solution.py:31
  121.2 3.6 %collective-permute-done.16.r2 = bf16[64,128]{1,0:T(8,128)(2,1)S(1)} collective-permute-done((bf16[64,128]{1,0:T(8,128)(2,1)S(1)}, bf16[64,128]{1,0:T(8,128)(2,1)S(1)}, u32[]{:S(2)}, u32[]{:S(2)}) %collective-permute-start.16) | collective-permute-done | bytes 16416 | tf_op jit(solution)/shard_map/ppermute | solution.py:31
  126.7 5.0 %all-to-all-start.4 = ((bf16[32,80,128]{2,1,0:T(8,128)(2,1)}), bf16[32,80,128]{2,1,0:T(8,128)(2,1)S(1)}, u32[]{:S(2)}, u32[]{:S(2)}) async-start(bf16[32,80,128]{2,1,0:T(8,128)(2,1)} %copy-done.5), calls=%async_computation.4 | async-start | bytes 1310720 | tf_op jit(solution)/shard_map/all_to_all | solution.py:44
  133.6 2.0 reshape.364
  135.5 1.9 copy.66
  137.5 11.7 %all-to-all-done.4.own_ref = bf16[32,80,128]{2,1,0:T(8,128)(2,1)S(1)} async-done(((bf16[32,80,128]{2,1,0:T(8,128)(2,1)}), bf16[32,80,128]{2,1,0:T(8,128)(2,1)S(1)}, u32[]{:S(2)}, u32[]{:S(2)}) %all-to-all-start.4) | async-done | bytes 655392 | tf_op jit(solution)/shard_map/all_to_all | solution.py:44
  149.2 2.6 %ffn_near.1 = (f32[8,256]{1,0:T(8,128)S(1)}, f32[224,256]{1,0:T(8,128)S(1)}, f32[224,256]{1,0:T(8,128)S(1)}, f32[224,256]{1,0:T(8,128)S(1)}, f32[224,256]{1,0:T(8,128)S(1)}) custom-call(bf16[8,2,336,128]{3,2,1,0:T(8,128)(2,1)S(1)} %get-tuple-element.68.p0, bf16[8,2,336,128]{3,2,1,0:T(8,128)(2,1)S(1)} %collective-permute-done.10.p1, ...), custom_call_target="tpu_custom_call" | custom-call | flops 469762048 | bytes 4000000 | tf_op jit(solution)/shard_map/ffn_near/pallas_call | solution.py:410
  151.8 2.6 %ffn_far.1 = (f32[224,256]{1,0:T(8,128)S(1)}, f32[8,256]{1,0:T(8,128)S(1)}, bf16[240,256]{1,0:T(8,128)(2,1)S(1)}, bf16[240,256]{1,0:T(8,128)(2,1)S(1)}, bf16[240,256]{1,0:T(8,128)(2,1)S(1)}) custom-call(bf16[8,2,336,128]{3,2,1,0:T(8,128)(2,1)S(1)} %get-tuple-element.68.p0, bf16[8,2,336,128]{3,2,1,0:T(8,128)(2,1)S(1)} %collective-permute-done.10.p1, ...), custom_call_target="tpu_custom_call" | custom-call | flops 469762048 | bytes 4000000 | tf_op jit(solution)/shard_map/ffn_far/pallas_call | solution.py:426
  157.7 3.1 %collective-permute-done.19.r1 = bf16[240,256]{1,0:T(8,128)(2,1)S(1)} collective-permute-done((bf16[240,256]{1,0:T(8,128)(2,1)S(1)}, bf16[240,256]{1,0:T(8,128)(2,1)S(1)}, u32[]{:S(2)}, u32[]{:S(2)}) %collective-permute-start.19) | collective-permute-done | bytes 122912 | tf_op jit(solution)/shard_map/ppermute | solution.py:31
  160.8 2.5 %collective-permute-done.20.r2 = bf16[240,256]{1,0:T(8,128)(2,1)S(1)} collective-permute-done((bf16[240,256]{1,0:T(8,128)(2,1)S(1)}, bf16[240,256]{1,0:T(8,128)(2,1)S(1)}, u32[]{:S(2)}, u32[]{:S(2)}) %collective-permute-start.20) | collective-permute-done | bytes 122912 | tf_op jit(solution)/shard_map/ppermute | solution.py:31
  163.3 1.9 collective-permute-done.21.r3
  167.9 2.0 collective-permute-done.24.a3
  169.9 1.9 collective-permute-done.23.a2
  172.5 2.2 down.2
  176.7 2.2 %down.3 = bf16[32,128,128]{2,1,0:T(8,128)(2,1)S(1)} custom-call(bf16[8,2,336,128]{3,2,1,0:T(8,128)(2,1)S(1)} %get-tuple-element.68.p0, bf16[8,2,336,128]{3,2,1,0:T(8,128)(2,1)S(1)} %collective-permute-done.10.p1, bf16[8,2,336,128]{3,2,1,0:T(8,128)(2,1)} %collective-permute-done.14.p2, bf16[8,2,336,128]{3,2,1,0:T(8,128)(2,1)} %collective-permute-done.11.p3, ...), custom_call_target="tpu_custom_call" | custom-call | flops 234881024 | bytes 4000000 | tf_op jit(solution)/shard_map/down/pallas_call | solution.py:492
  180.0 5.7 %all-to-all-start.5 = ((bf16[32,128,128]{2,1,0:T(8,128)(2,1)}), bf16[32,128,128]{2,1,0:T(8,128)(2,1)S(1)}, u32[]{:S(2)}, u32[]{:S(2)}) async-start(bf16[32,128,128]{2,1,0:T(8,128)(2,1)} %copy-done), calls=%async_computation.5 | async-start | bytes 2097152 | tf_op jit(solution)/shard_map/all_to_all | solution.py:44
  188.0 26.1 %all-to-all-done.5 = bf16[32,128,128]{2,1,0:T(8,128)(2,1)S(1)} async-done(((bf16[32,128,128]{2,1,0:T(8,128)(2,1)}), bf16[32,128,128]{2,1,0:T(8,128)(2,1)S(1)}, u32[]{:S(2)}, u32[]{:S(2)}) %all-to-all-start.5) | async-done | bytes 1048608 | tf_op jit(solution)/shard_map/all_to_all | solution.py:44
  214.8 2.8 %collective-permute-start.26 = (bf16[64,128]{1,0:T(8,128)(2,1)S(1)}, bf16[64,128]{1,0:T(8,128)(2,1)S(1)}, u32[]{:S(2)}, u32[]{:S(2)}) collective-permute-start(bf16[64,128]{1,0:T(8,128)(2,1)S(1)} %add_convert_fusion), channel_id=1, source_target_pairs={{0,0},{1,8},{2,16},{3,24},{8,1},{9,9},{10,17},{11,25},{16,2},{17,1... | collective-permute-start | bytes 49160 | tf_op jit(solution)/shard_map/ppermute | solution.py:40
  219.1 5.2 %collective-permute-done.26 = bf16[64,128]{1,0:T(8,128)(2,1)S(1)} collective-permute-done((bf16[64,128]{1,0:T(8,128)(2,1)S(1)}, bf16[64,128]{1,0:T(8,128)(2,1)S(1)}, u32[]{:S(2)}, u32[]{:S(2)}) %collective-permute-start.26) | collective-permute-done | bytes 16416 | tf_op jit(solution)/shard_map/ppermute | solution.py:40
  (194 shorter events, 56.1 us)
Async XLA Ops:
  2.2 3.3 %collective-permute-start = (bf16[272,128]{1,0:T(8,128)(2,1)S(1)}, bf16[272,128]{1,0:T(8,128)(2,1)S(1)}, u32[]{:S(2)}, u32[]{:S(2)}) collective-permute-start(bf16[272,128]{1,0:T(8,128)(2,1)S(1)} %pad_maximum_fusion.5), channel_id=1, source_target_pairs={{0,4},{4,0},{1,5},{5,1},{2,6},{6,2},{3,7},{7,3},{8,12},{12,8},{9,1... | collective-permute-start | bytes 208904 | tf_op jit(solution)/shard_map/ppermute | solution.py:27
  3.9 3.1 %collective-permute-start.1 = (bf16[128,1280]{1,0:T(8,128)(2,1)S(1)}, bf16[128,1280]{1,0:T(8,128)(2,1)S(1)}, u32[]{:S(2)}, u32[]{:S(2)}) collective-permute-start(bf16[128,1280]{1,0:T(8,128)(2,1)S(1)} %pad_maximum_fusion.2), channel_id=1, source_target_pairs={{0,4},{4,0},{1,5},{5,1},{2,6},{6,2},{3,7},{7,3},{8,12},{12,8},{9,1... | collective-permute-start | bytes 983048 | tf_op jit(solution)/shard_map/ppermute | solution.py:27
  9.4 34.6 %collective-permute-start.4 = (bf16[512,512]{1,0:T(8,128)(2,1)}, bf16[512,512]{1,0:T(8,128)(2,1)}, u32[]{:S(2)}, u32[]{:S(2)}) collective-permute-start(bf16[512,512]{1,0:T(8,128)(2,1)} %bitcast.43.c0), channel_id=1, source_target_pairs={{0,16},{8,24},{16,0},{24,8},{1,17},{9,25},{17,1},{25,9},{2,18},{10... | collective-permute-start | bytes 1572872 | tf_op jit(solution)/shard_map/ppermute | solution.py:56
  11.7 32.3 %collective-permute-start.3 = (bf16[512,512]{1,0:T(8,128)(2,1)}, bf16[512,512]{1,0:T(8,128)(2,1)}, u32[]{:S(2)}, u32[]{:S(2)}) collective-permute-start(bf16[512,512]{1,0:T(8,128)(2,1)} %bitcast.43.c0), channel_id=1, source_target_pairs={{0,24},{8,0},{16,8},{24,16},{1,25},{9,1},{17,9},{25,17},{2,26},{10... | collective-permute-start | bytes 1572872 | tf_op jit(solution)/shard_map/ppermute | solution.py:56
  12.1 32.5 %collective-permute-start.2 = (bf16[512,512]{1,0:T(8,128)(2,1)}, bf16[512,512]{1,0:T(8,128)(2,1)}, u32[]{:S(2)}, u32[]{:S(2)}) collective-permute-start(bf16[512,512]{1,0:T(8,128)(2,1)} %bitcast.43.c0), channel_id=1, source_target_pairs={{0,8},{8,16},{16,24},{24,0},{1,9},{9,17},{17,25},{25,1},{2,10},{10... | collective-permute-start | bytes 1572872 | tf_op jit(solution)/shard_map/ppermute | solution.py:56
  13.8 40.8 %all-to-all-start = ((bf16[32,136,128]{2,1,0:T(8,128)(2,1)}), bf16[32,136,128]{2,1,0:T(8,128)(2,1)}, u32[]{:S(2)}, u32[]{:S(2)}) async-start(bf16[32,136,128]{2,1,0:T(8,128)(2,1)} %bitcast.14), calls=%async_computation | async-start | bytes 2228224 | tf_op jit(solution)/shard_map/all_to_all | solution.py:44
  29.0 1.5 collective-permute-start.5
  39.6 42.8 %collective-permute-start.10 = (bf16[8,2,336,128]{3,2,1,0:T(8,128)(2,1)}, bf16[8,2,336,128]{3,2,1,0:T(8,128)(2,1)S(1)}, u32[]{:S(2)}, u32[]{:S(2)}) collective-permute-start(bf16[8,2,336,128]{3,2,1,0:T(8,128)(2,1)} %get-tuple-element.69), channel_id=1, source_target_pairs={{0,1},{1,2},{2,3},{3,0},{4,5},{5,6},{6,7},{7,4},{8,9},{9,10},{10,1... | collective-permute-start | bytes 4128776 | tf_op jit(solution)/shard_map/ppermute | solution.py:31
  41.1 41.2 %collective-permute-start.11 = (bf16[8,2,336,128]{3,2,1,0:T(8,128)(2,1)}, bf16[8,2,336,128]{3,2,1,0:T(8,128)(2,1)}, u32[]{:S(2)}, u32[]{:S(2)}) collective-permute-start(bf16[8,2,336,128]{3,2,1,0:T(8,128)(2,1)} %get-tuple-element.71), channel_id=1, source_target_pairs={{0,3},{1,0},{2,1},{3,2},{4,7},{5,4},{6,5},{7,6},{8,11},{9,8},{10,9... | collective-permute-start | bytes 4128776 | tf_op jit(solution)/shard_map/ppermute | solution.py:31
  56.8 14.5 %all-to-all-start.1 = ((bf16[8,128,128]{2,1,0:T(8,128)(2,1)}), bf16[8,128,128]{2,1,0:T(8,128)(2,1)}, u32[]{:S(2)}, u32[]{:S(2)}) async-start(bf16[8,128,128]{2,1,0:T(8,128)(2,1)} %copy-done.4), calls=%async_computation.1 | async-start | bytes 524288 | tf_op jit(solution)/shard_map/all_to_all | solution.py:60
  60.9 21.5 %collective-permute-start.9 = (bf16[2320,128]{1,0:T(8,128)(2,1)S(1)}, bf16[2320,128]{1,0:T(8,128)(2,1)}, u32[]{:S(2)}, u32[]{:S(2)}) collective-permute-start(bf16[2320,128]{1,0:T(8,128)(2,1)S(1)} %pad_maximum_fusion.w0), channel_id=1, source_target_pairs={{0,24},{8,0},{16,8},{24,16},{1,25},{9,1},{17,9},{25,17},{2,26},{10... | collective-permute-start | bytes 1781768 | tf_op jit(solution)/shard_map/ppermute | solution.py:56
  61.5 20.9 %collective-permute-start.8 = (bf16[2320,128]{1,0:T(8,128)(2,1)S(1)}, bf16[2320,128]{1,0:T(8,128)(2,1)}, u32[]{:S(2)}, u32[]{:S(2)}) collective-permute-start(bf16[2320,128]{1,0:T(8,128)(2,1)S(1)} %pad_maximum_fusion.w0), channel_id=1, source_target_pairs={{0,8},{8,16},{16,24},{24,0},{1,9},{9,17},{17,25},{25,1},{2,10},{10... | collective-permute-start | bytes 1781768 | tf_op jit(solution)/shard_map/ppermute | solution.py:56
  71.3 1.7 collective-permute-start.6
  80.1 1.5 collective-permute-start.7
  82.4 34.2 %collective-permute-start.14 = (bf16[8,2,336,128]{3,2,1,0:T(8,128)(2,1)}, bf16[8,2,336,128]{3,2,1,0:T(8,128)(2,1)}, u32[]{:S(2)}, u32[]{:S(2)}) collective-permute-start(bf16[8,2,336,128]{3,2,1,0:T(8,128)(2,1)} %get-tuple-element.90), channel_id=1, source_target_pairs={{0,2},{1,3},{2,0},{3,1},{4,6},{5,7},{6,4},{7,5},{8,10},{9,11},{10,... | collective-permute-start | bytes 4128776 | tf_op jit(solution)/shard_map/ppermute | solution.py:31
  85.7 13.4 %all-to-all-start.2 = ((bf16[8,80,128]{2,1,0:T(8,128)(2,1)}), bf16[8,80,128]{2,1,0:T(8,128)(2,1)S(1)}, u32[]{:S(2)}, u32[]{:S(2)}) async-start(bf16[8,80,128]{2,1,0:T(8,128)(2,1)} %merge.1), calls=%async_computation.2 | async-start | bytes 327680 | tf_op jit(solution)/shard_map/all_to_all | solution.py:60
  89.1 23.8 %collective-permute-start.13 = (bf16[2320,128]{1,0:T(8,128)(2,1)S(1)}, bf16[2320,128]{1,0:T(8,128)(2,1)}, u32[]{:S(2)}, u32[]{:S(2)}) collective-permute-start(bf16[2320,128]{1,0:T(8,128)(2,1)S(1)} %pad_maximum_fusion.w0), channel_id=1, source_target_pairs={{0,16},{8,24},{16,0},{24,8},{1,17},{9,25},{17,1},{25,9},{2,18},{10... | collective-permute-start | bytes 1781768 | tf_op jit(solution)/shard_map/ppermute | solution.py:56
  112.9 1.3 collective-permute-start.12
  116.6 4.5 %collective-permute-start.17 = (bf16[64,128]{1,0:T(8,128)(2,1)S(1)}, bf16[64,128]{1,0:T(8,128)(2,1)S(1)}, u32[]{:S(2)}, u32[]{:S(2)}) collective-permute-start(bf16[64,128]{1,0:T(8,128)(2,1)S(1)} %get-tuple-element.144), channel_id=1, source_target_pairs={{0,3},{1,0},{2,1},{3,2},{4,7},{5,4},{6,5},{7,6},{8,11},{9,8},{10,9... | collective-permute-start | bytes 49160 | tf_op jit(solution)/shard_map/ppermute | solution.py:31
  119.6 5.2 %collective-permute-start.16 = (bf16[64,128]{1,0:T(8,128)(2,1)S(1)}, bf16[64,128]{1,0:T(8,128)(2,1)S(1)}, u32[]{:S(2)}, u32[]{:S(2)}) collective-permute-start(bf16[64,128]{1,0:T(8,128)(2,1)S(1)} %get-tuple-element.145), channel_id=1, source_target_pairs={{0,2},{1,3},{2,0},{3,1},{4,6},{5,7},{6,4},{7,5},{8,10},{9,11},{10,... | collective-permute-start | bytes 49160 | tf_op jit(solution)/shard_map/ppermute | solution.py:31
  120.2 4.9 %collective-permute-start.15 = (bf16[64,128]{1,0:T(8,128)(2,1)S(1)}, bf16[64,128]{1,0:T(8,128)(2,1)S(1)}, u32[]{:S(2)}, u32[]{:S(2)}) collective-permute-start(bf16[64,128]{1,0:T(8,128)(2,1)S(1)} %get-tuple-element.146), channel_id=1, source_target_pairs={{0,1},{1,2},{2,3},{3,0},{4,5},{5,6},{6,7},{7,4},{8,9},{9,10},{10,1... | collective-permute-start | bytes 49160 | tf_op jit(solution)/shard_map/ppermute | solution.py:31
  126.7 22.5 %all-to-all-start.4 = ((bf16[32,80,128]{2,1,0:T(8,128)(2,1)}), bf16[32,80,128]{2,1,0:T(8,128)(2,1)S(1)}, u32[]{:S(2)}, u32[]{:S(2)}) async-start(bf16[32,80,128]{2,1,0:T(8,128)(2,1)} %copy-done.5), calls=%async_computation.4 | async-start | bytes 1310720 | tf_op jit(solution)/shard_map/all_to_all | solution.py:44
  149.2 2.6 %collective-permute-start.18 = (bf16[32,80,128]{2,1,0:T(8,128)(2,1)S(1)}, bf16[32,80,128]{2,1,0:T(8,128)(2,1)S(1)}, u32[]{:S(2)}, u32[]{:S(2)}) collective-permute-start(bf16[32,80,128]{2,1,0:T(8,128)(2,1)S(1)} %all-to-all-done.4.own_ref), channel_id=1, source_target_pairs={{0,4},{4,0},{1,5},{5,1},{2,6},{6,2},{3,7},{7,3},{8,12},{12,8},{9,1... | collective-permute-start | bytes 1966088 | tf_op jit(solution)/shard_map/ppermute | solution.py:27
  154.4 6.4 %collective-permute-start.19 = (bf16[240,256]{1,0:T(8,128)(2,1)S(1)}, bf16[240,256]{1,0:T(8,128)(2,1)S(1)}, u32[]{:S(2)}, u32[]{:S(2)}) collective-permute-start(bf16[240,256]{1,0:T(8,128)(2,1)S(1)} %get-tuple-element.112), channel_id=1, source_target_pairs={{0,3},{1,0},{2,1},{3,2},{4,7},{5,4},{6,5},{7,6},{8,11},{9,8},{10,9... | collective-permute-start | bytes 368648 | tf_op jit(solution)/shard_map/ppermute | solution.py:31
  155.7 7.7 %collective-permute-start.20 = (bf16[240,256]{1,0:T(8,128)(2,1)S(1)}, bf16[240,256]{1,0:T(8,128)(2,1)S(1)}, u32[]{:S(2)}, u32[]{:S(2)}) collective-permute-start(bf16[240,256]{1,0:T(8,128)(2,1)S(1)} %get-tuple-element.113), channel_id=1, source_target_pairs={{0,2},{1,3},{2,0},{3,1},{4,6},{5,7},{6,4},{7,5},{8,10},{9,11},{10,... | collective-permute-start | bytes 368648 | tf_op jit(solution)/shard_map/ppermute | solution.py:31
  156.7 8.5 %collective-permute-start.21 = (bf16[240,256]{1,0:T(8,128)(2,1)S(1)}, bf16[240,256]{1,0:T(8,128)(2,1)S(1)}, u32[]{:S(2)}, u32[]{:S(2)}) collective-permute-start(bf16[240,256]{1,0:T(8,128)(2,1)S(1)} %get-tuple-element.114), channel_id=1, source_target_pairs={{0,1},{1,2},{2,3},{3,0},{4,5},{5,6},{6,7},{7,4},{8,9},{9,10},{10,1... | collective-permute-start | bytes 368648 | tf_op jit(solution)/shard_map/ppermute | solution.py:31
  165.4 4.5 %collective-permute-start.24 = (bf16[112,256]{1,0:T(8,128)(2,1)S(1)}, bf16[112,256]{1,0:T(8,128)(2,1)S(1)}, u32[]{:S(2)}, u32[]{:S(2)}) collective-permute-start(bf16[112,256]{1,0:T(8,128)(2,1)S(1)} %act.1.a0), channel_id=1, source_target_pairs={{0,3},{1,0},{2,1},{3,2},{4,7},{5,4},{6,5},{7,6},{8,11},{9,8},{10,9... | collective-permute-start | bytes 172040 | tf_op jit(solution)/shard_map/ppermute | solution.py:31
  166.0 5.8 %collective-permute-start.23 = (bf16[112,256]{1,0:T(8,128)(2,1)S(1)}, bf16[112,256]{1,0:T(8,128)(2,1)S(1)}, u32[]{:S(2)}, u32[]{:S(2)}) collective-permute-start(bf16[112,256]{1,0:T(8,128)(2,1)S(1)} %act.1.a0), channel_id=1, source_target_pairs={{0,2},{1,3},{2,0},{3,1},{4,6},{5,7},{6,4},{7,5},{8,10},{9,11},{10,... | collective-permute-start | bytes 172040 | tf_op jit(solution)/shard_map/ppermute | solution.py:31
  167.1 5.4 %collective-permute-start.22 = (bf16[112,256]{1,0:T(8,128)(2,1)S(1)}, bf16[112,256]{1,0:T(8,128)(2,1)S(1)}, u32[]{:S(2)}, u32[]{:S(2)}) collective-permute-start(bf16[112,256]{1,0:T(8,128)(2,1)S(1)} %act.1.a0), channel_id=1, source_target_pairs={{0,1},{1,2},{2,3},{3,0},{4,5},{5,6},{6,7},{7,4},{8,9},{9,10},{10,1... | collective-permute-start | bytes 172040 | tf_op jit(solution)/shard_map/ppermute | solution.py:31
  174.7 2.0 collective-permute-start.25
  180.0 34.1 %all-to-all-start.5 = ((bf16[32,128,128]{2,1,0:T(8,128)(2,1)}), bf16[32,128,128]{2,1,0:T(8,128)(2,1)S(1)}, u32[]{:S(2)}, u32[]{:S(2)}) async-start(bf16[32,128,128]{2,1,0:T(8,128)(2,1)} %copy-done), calls=%async_computation.5 | async-start | bytes 2097152 | tf_op jit(solution)/shard_map/all_to_all | solution.py:44
  214.8 9.5 %collective-permute-start.26 = (bf16[64,128]{1,0:T(8,128)(2,1)S(1)}, bf16[64,128]{1,0:T(8,128)(2,1)S(1)}, u32[]{:S(2)}, u32[]{:S(2)}) collective-permute-start(bf16[64,128]{1,0:T(8,128)(2,1)S(1)} %add_convert_fusion), channel_id=1, source_target_pairs={{0,0},{1,8},{2,16},{3,24},{8,1},{9,9},{10,17},{11,25},{16,2},{17,1... | collective-permute-start | bytes 49160 | tf_op jit(solution)/shard_map/ppermute | solution.py:40
  (19 other events, 50.7 us)

commit v7 on v6

--- a/solution.py
+++ b/solution.py
@@ -531,18 +531,16 @@
 
     place = jnp.stack([c, y, z, x]).astype(jnp.int32)
 
-    message = jnp.concatenate(
-        [hidden_rows, jnp.broadcast_to(attn_gain[None, :], (16, 128))], axis=0
-    )
-    theirs = exchange_cores(message)
+    theirs = exchange_cores(hidden_rows)
+    gain_theirs = exchange_cores(attn_gain.reshape(1, 128))
     weight_theirs = exchange_cores(half(other))
 
     theirs, raw = hold(theirs, cache_kv)
     cache = raw.reshape(DOC_LEN, 512)
 
     weight = jnp.concatenate([half(c), weight_theirs], axis=0)
-    inputs = jnp.concatenate([hidden_rows, theirs[:ROWS]], axis=1).astype(F32)
-    gain = jnp.concatenate([attn_gain, theirs[ROWS]], axis=0).astype(F32)
+    inputs = jnp.concatenate([hidden_rows, theirs], axis=1).astype(F32)
+    gain = jnp.concatenate([attn_gain, gain_theirs[0]], axis=0).astype(F32)
     squares = jnp.sum(inputs * inputs, axis=1)
     scaled = (inputs * gain[None, :]).astype(BF)
     partial = jnp.dot(scaled, weight, preferred_element_type=F32).astype(BF)

time: 226 us -> 225 us (level)
    ppermute x8 -> x9, waiting for transfers between devices: 6.51 us -> 6.53 us  [exchange_cores(): return lax.ppermute(value, 'c', [(0, 1), (1, 0)])]
  transfers between devices with their start and end apart: 32 -> 33, of which waited for: 20 -> 20; matrix products, arithmetic and copies ran while one was open for 9% -> 9% of each run, Pallas kernels for 9% -> 9%
where the time goes in v7:
time: 225 us; the launch traced here: 224 us
  waiting for transfers between devices  94.5 us (42%)
  starting transfers between devices  57.4 us (26%)
  Pallas kernels  27.3 us (12%)
  local copies, waits for them, and re-layouts  22.2 us (10%)
  blocking collectives  11.5 us (5%)
  other arithmetic  8.55 us (4%)
    all_to_all x3, waiting for transfers between devices, swap_zx(): return lax.all_to_all(value, ('z', 'x'), 0, 0, tiled=True)  48.3 us
    all_to_all x3, starting transfers between devices, swap_zx(): return lax.all_to_all(value, ('z', 'x'), 0, 0, tiled=True)  22.4 us
    all_to_all x2, waiting for transfers between devices, swap_z(): return lax.all_to_all(value, 'z', 0, 0, tiled=True)  17.9 us
    ppermute x12, starting transfers between devices, shift_y(): return lax.ppermute(value, 'y', [(i, (i + step) % NY) for i in range(NY)])  16.7 us
    ppermute x12, waiting for transfers between devices, shift_y(): return lax.ppermute(value, 'y', [(i, (i + step) % NY) for i in range(NY)])  16.1 us
    unnamed x48, local copies, waits for them, and re-layouts  11.6 us
    all_to_all x1, blocking collectives, swap_z(): return lax.all_to_all(value, 'z', 0, 0, tiled=True)  11.5 us
    all_to_all x2, starting transfers between devices, swap_z(): return lax.all_to_all(value, 'z', 0, 0, tiled=True)  7.43 us
  transfers between devices with their start and end apart: 33, of which 20 were waited for; matrix products, arithmetic and copies ran while one was open for 9% of the time, Pallas kernels for 9%

profile of v7, /device:TPU:4, one launch (start us, length us, event | category | flops | bytes accessed | tf_op | source)
XLA Modules:
  0.0 223.6 jit_solution(15429153427252968057)
XLA Ops:
  8.0 2.3 %collective-permute-start.5 = (bf16[512,512]{1,0:T(8,128)(2,1)}, bf16[512,512]{1,0:T(8,128)(2,1)}, u32[]{:S(2)}, u32[]{:S(2)}) collective-permute-start(bf16[512,512]{1,0:T(8,128)(2,1)} %bitcast.44.c0), channel_id=1, source_target_pairs={{0,16},{8,24},{16,0},{24,8},{1,17},{9,25},{17,1},{25,9},{2,18},{10... | collective-permute-start | bytes 1572872 | tf_op jit(solution)/shard_map/ppermute | solution.py:56
  12.5 11.8 %all-to-all-start = ((bf16[32,136,128]{2,1,0:T(8,128)(2,1)}), bf16[32,136,128]{2,1,0:T(8,128)(2,1)}, u32[]{:S(2)}, u32[]{:S(2)}) async-start(bf16[32,136,128]{2,1,0:T(8,128)(2,1)} %bitcast.15), calls=%async_computation | async-start | bytes 2228224 | tf_op jit(solution)/shard_map/all_to_all | solution.py:44
  29.9 2.0 copy-done.1
  33.5 4.7 %weight_slices.1 = (bf16[8,2,336,128]{3,2,1,0:T(8,128)(2,1)S(1)}, bf16[8,2,336,128]{3,2,1,0:T(8,128)(2,1)}, bf16[8,2,336,128]{3,2,1,0:T(8,128)(2,1)}, bf16[8,2,336,128]{3,2,1,0:T(8,128)(2,1)}) custom-call(s32[4]{0:T(128)S(1)} %pad_add_fusion.2.place_ref, bf16[224,8192]{1,0:T(8,128)(2,1)S(1)} %bitcast.68, bf16[112,8192]{1,0:T(8,128)(2,1)S(1)} %copy-done.3), custom_call_target="tpu_custom_call" | custom-call | bytes 11000000 | tf_op jit(solution)/shard_map/weight_slices/pallas_call | solution.py:96
  43.0 10.5 %all-to-all-done.in_ref = bf16[32,136,128]{2,1,0:T(8,128)(2,1)} async-done(((bf16[32,136,128]{2,1,0:T(8,128)(2,1)}), bf16[32,136,128]{2,1,0:T(8,128)(2,1)}, u32[]{:S(2)}, u32[]{:S(2)}) %all-to-all-start) | async-done | bytes 1114144 | tf_op jit(solution)/shard_map/all_to_all | solution.py:44
  55.7 4.0 %all-to-all-start.1 = ((bf16[8,128,128]{2,1,0:T(8,128)(2,1)}), bf16[8,128,128]{2,1,0:T(8,128)(2,1)}, u32[]{:S(2)}, u32[]{:S(2)}) async-start(bf16[8,128,128]{2,1,0:T(8,128)(2,1)} %copy-done.4), calls=%async_computation.1 | async-start | bytes 524288 | tf_op jit(solution)/shard_map/all_to_all | solution.py:60
  61.8 8.4 %all-to-all-done.1.own_ref = bf16[8,128,128]{2,1,0:T(8,128)(2,1)} async-done(((bf16[8,128,128]{2,1,0:T(8,128)(2,1)}), bf16[8,128,128]{2,1,0:T(8,128)(2,1)}, u32[]{:S(2)}, u32[]{:S(2)}) %all-to-all-start.1) | async-done | bytes 262176 | tf_op jit(solution)/shard_map/all_to_all | solution.py:60
  73.0 5.9 %attend.1 = (f32[128,512]{1,0:T(8,128)S(1)}, bf16[144,512]{1,0:T(8,128)(2,1)S(1)}, f32[8,512]{1,0:T(8,128)S(1)}) custom-call(s32[4]{0:T(128)S(1)} %pad_add_fusion.2.place_ref, bf16[2048,128]{1,0:T(8,128)(2,1)S(1)} %copy-done.6, bf16[8,128,128]{2,1,0:T(8,128)(2,1)} %all-to-all-done.1.own_ref, bf16[8,128,128]{2,1,0:T(8,128)(2,1)S(1)} %collective-permute-done.7.other_ref, ...), custom_call_target="tpu_custom_call" | custom-call | flops 1073741824 | bytes 6000000 | tf_op jit(solution)/shard_map/attend/pallas_call | solution.py:202
  81.3 3.3 %collective-permute-start.15 = (bf16[8,2,336,128]{3,2,1,0:T(8,128)(2,1)}, bf16[8,2,336,128]{3,2,1,0:T(8,128)(2,1)}, u32[]{:S(2)}, u32[]{:S(2)}) collective-permute-start(bf16[8,2,336,128]{3,2,1,0:T(8,128)(2,1)} %get-tuple-element.90), channel_id=1, source_target_pairs={{0,2},{1,3},{2,0},{3,1},{4,6},{5,7},{6,4},{7,5},{8,10},{9,11},{10,... | collective-permute-start | bytes 4128776 | tf_op jit(solution)/shard_map/ppermute | solution.py:31
  84.5 3.4 %all-to-all-start.2 = ((bf16[8,80,128]{2,1,0:T(8,128)(2,1)}), bf16[8,80,128]{2,1,0:T(8,128)(2,1)S(1)}, u32[]{:S(2)}, u32[]{:S(2)}) async-start(bf16[8,80,128]{2,1,0:T(8,128)(2,1)} %merge.1), calls=%async_computation.2 | async-start | bytes 327680 | tf_op jit(solution)/shard_map/all_to_all | solution.py:60
  88.4 9.5 %all-to-all-done.2.arrived_ref = bf16[8,80,128]{2,1,0:T(8,128)(2,1)S(1)} async-done(((bf16[8,80,128]{2,1,0:T(8,128)(2,1)}), bf16[8,80,128]{2,1,0:T(8,128)(2,1)S(1)}, u32[]{:S(2)}, u32[]{:S(2)}) %all-to-all-start.2) | async-done | bytes 163872 | tf_op jit(solution)/shard_map/all_to_all | solution.py:60
  100.3 11.5 %all_to_all.30.own_ref = bf16[8,64,128]{2,1,0:T(8,128)(2,1)S(1)} all-to-all(bf16[8,64,128]{2,1,0:T(8,128)(2,1)S(1)} %finish.1), channel_id=1, replica_groups=mesh['z'=8,'x'=4,'c'=2,'y'=4] {'z'}, dimensions={0} | all-to-all | bytes 262144 | tf_op jit(solution)/shard_map/all_to_all | solution.py:60
  113.1 2.3 %project.1 = (f32[64,128]{1,0:T(8,128)S(1)}, bf16[16,128]{1,0:T(8,128)(2,1)S(1)}, bf16[4,64,128]{2,1,0:T(8,128)(2,1)S(1)}) custom-call(s32[4]{0:T(128)S(1)} %pad_add_fusion.2.place_ref, bf16[8,64,128]{2,1,0:T(8,128)(2,1)S(1)} %all_to_all.30.own_ref, bf16[8,64,128]{2,1,0:T(8,128)(2,1)S(1)} %collective-permute-done.13.far_ref, ...), custom_call_target="tpu_custom_call" | custom-call | flops 134217728 | bytes 2500000 | tf_op jit(solution)/shard_map/project/pallas_call | solution.py:325
  115.5 2.9 %collective-permute-start.18 = (bf16[64,128]{1,0:T(8,128)(2,1)S(1)}, bf16[64,128]{1,0:T(8,128)(2,1)S(1)}, u32[]{:S(2)}, u32[]{:S(2)}) collective-permute-start(bf16[64,128]{1,0:T(8,128)(2,1)S(1)} %get-tuple-element.144), channel_id=1, source_target_pairs={{0,3},{1,0},{2,1},{3,2},{4,7},{5,4},{6,5},{7,6},{8,11},{9,8},{10,9... | collective-permute-start | bytes 49160 | tf_op jit(solution)/shard_map/ppermute | solution.py:31
  120.0 3.6 %collective-permute-done.17.r2 = bf16[64,128]{1,0:T(8,128)(2,1)S(1)} collective-permute-done((bf16[64,128]{1,0:T(8,128)(2,1)S(1)}, bf16[64,128]{1,0:T(8,128)(2,1)S(1)}, u32[]{:S(2)}, u32[]{:S(2)}) %collective-permute-start.17) | collective-permute-done | bytes 16416 | tf_op jit(solution)/shard_map/ppermute | solution.py:31
  125.5 5.0 %all-to-all-start.4 = ((bf16[32,80,128]{2,1,0:T(8,128)(2,1)}), bf16[32,80,128]{2,1,0:T(8,128)(2,1)S(1)}, u32[]{:S(2)}, u32[]{:S(2)}) async-start(bf16[32,80,128]{2,1,0:T(8,128)(2,1)} %copy-done.5), calls=%async_computation.4 | async-start | bytes 1310720 | tf_op jit(solution)/shard_map/all_to_all | solution.py:44
  132.4 2.0 reshape.364
  134.4 1.9 copy.66
  136.3 11.7 %all-to-all-done.4.own_ref = bf16[32,80,128]{2,1,0:T(8,128)(2,1)S(1)} async-done(((bf16[32,80,128]{2,1,0:T(8,128)(2,1)}), bf16[32,80,128]{2,1,0:T(8,128)(2,1)S(1)}, u32[]{:S(2)}, u32[]{:S(2)}) %all-to-all-start.4) | async-done | bytes 655392 | tf_op jit(solution)/shard_map/all_to_all | solution.py:44
  148.0 2.6 %ffn_near.1 = (f32[8,256]{1,0:T(8,128)S(1)}, f32[224,256]{1,0:T(8,128)S(1)}, f32[224,256]{1,0:T(8,128)S(1)}, f32[224,256]{1,0:T(8,128)S(1)}, f32[224,256]{1,0:T(8,128)S(1)}) custom-call(bf16[8,2,336,128]{3,2,1,0:T(8,128)(2,1)S(1)} %get-tuple-element.68.p0, bf16[8,2,336,128]{3,2,1,0:T(8,128)(2,1)S(1)} %collective-permute-done.11.p1, ...), custom_call_target="tpu_custom_call" | custom-call | flops 469762048 | bytes 4000000 | tf_op jit(solution)/shard_map/ffn_near/pallas_call | solution.py:410
  150.6 2.6 %ffn_far.1 = (f32[224,256]{1,0:T(8,128)S(1)}, f32[8,256]{1,0:T(8,128)S(1)}, bf16[240,256]{1,0:T(8,128)(2,1)S(1)}, bf16[240,256]{1,0:T(8,128)(2,1)S(1)}, bf16[240,256]{1,0:T(8,128)(2,1)S(1)}) custom-call(bf16[8,2,336,128]{3,2,1,0:T(8,128)(2,1)S(1)} %get-tuple-element.68.p0, bf16[8,2,336,128]{3,2,1,0:T(8,128)(2,1)S(1)} %collective-permute-done.11.p1, ...), custom_call_target="tpu_custom_call" | custom-call | flops 469762048 | bytes 4000000 | tf_op jit(solution)/shard_map/ffn_far/pallas_call | solution.py:426
  156.3 3.1 %collective-permute-done.20.r1 = bf16[240,256]{1,0:T(8,128)(2,1)S(1)} collective-permute-done((bf16[240,256]{1,0:T(8,128)(2,1)S(1)}, bf16[240,256]{1,0:T(8,128)(2,1)S(1)}, u32[]{:S(2)}, u32[]{:S(2)}) %collective-permute-start.20) | collective-permute-done | bytes 122912 | tf_op jit(solution)/shard_map/ppermute | solution.py:31
  159.4 2.5 %collective-permute-done.21.r2 = bf16[240,256]{1,0:T(8,128)(2,1)S(1)} collective-permute-done((bf16[240,256]{1,0:T(8,128)(2,1)S(1)}, bf16[240,256]{1,0:T(8,128)(2,1)S(1)}, u32[]{:S(2)}, u32[]{:S(2)}) %collective-permute-start.21) | collective-permute-done | bytes 122912 | tf_op jit(solution)/shard_map/ppermute | solution.py:31
  162.0 1.9 collective-permute-done.22.r3
  166.6 2.0 collective-permute-done.25.a3
  168.6 1.9 collective-permute-done.24.a2
  171.1 2.2 down.2
  175.3 2.2 %down.3 = bf16[32,128,128]{2,1,0:T(8,128)(2,1)S(1)} custom-call(bf16[8,2,336,128]{3,2,1,0:T(8,128)(2,1)S(1)} %get-tuple-element.68.p0, bf16[8,2,336,128]{3,2,1,0:T(8,128)(2,1)S(1)} %collective-permute-done.11.p1, bf16[8,2,336,128]{3,2,1,0:T(8,128)(2,1)} %collective-permute-done.15.p2, bf16[8,2,336,128]{3,2,1,0:T(8,128)(2,1)} %collective-permute-done.12.p3, ...), custom_call_target="tpu_custom_call" | custom-call | flops 234881024 | bytes 4000000 | tf_op jit(solution)/shard_map/down/pallas_call | solution.py:492
  178.6 5.7 %all-to-all-start.5 = ((bf16[32,128,128]{2,1,0:T(8,128)(2,1)}), bf16[32,128,128]{2,1,0:T(8,128)(2,1)S(1)}, u32[]{:S(2)}, u32[]{:S(2)}) async-start(bf16[32,128,128]{2,1,0:T(8,128)(2,1)} %copy-done), calls=%async_computation.5 | async-start | bytes 2097152 | tf_op jit(solution)/shard_map/all_to_all | solution.py:44
  186.6 26.1 %all-to-all-done.5 = bf16[32,128,128]{2,1,0:T(8,128)(2,1)S(1)} async-done(((bf16[32,128,128]{2,1,0:T(8,128)(2,1)}), bf16[32,128,128]{2,1,0:T(8,128)(2,1)S(1)}, u32[]{:S(2)}, u32[]{:S(2)}) %all-to-all-start.5) | async-done | bytes 1048608 | tf_op jit(solution)/shard_map/all_to_all | solution.py:44
  213.4 2.8 %collective-permute-start.27 = (bf16[64,128]{1,0:T(8,128)(2,1)S(1)}, bf16[64,128]{1,0:T(8,128)(2,1)S(1)}, u32[]{:S(2)}, u32[]{:S(2)}) collective-permute-start(bf16[64,128]{1,0:T(8,128)(2,1)S(1)} %add_convert_fusion), channel_id=1, source_target_pairs={{0,0},{1,8},{2,16},{3,24},{8,1},{9,9},{10,17},{11,25},{16,2},{17,1... | collective-permute-start | bytes 49160 | tf_op jit(solution)/shard_map/ppermute | solution.py:40
  217.7 5.2 %collective-permute-done.27 = bf16[64,128]{1,0:T(8,128)(2,1)S(1)} collective-permute-done((bf16[64,128]{1,0:T(8,128)(2,1)S(1)}, bf16[64,128]{1,0:T(8,128)(2,1)S(1)}, u32[]{:S(2)}, u32[]{:S(2)}) %collective-permute-start.27) | collective-permute-done | bytes 16416 | tf_op jit(solution)/shard_map/ppermute | solution.py:40
  (192 shorter events, 54.3 us)
Async XLA Ops:
  0.6 3.5 %collective-permute-start.1 = (bf16[1,128]{1,0:T(2,128)(2,1)}, bf16[1,128]{1,0:T(2,128)(2,1)S(1)}, u32[]{:S(2)}, u32[]{:S(2)}) collective-permute-start(bf16[1,128]{1,0:T(2,128)(2,1)} %bitcast.87), channel_id=1, source_target_pairs={{0,4},{4,0},{1,5},{5,1},{2,6},{6,2},{3,7},{7,3},{8,12},{12,8},{9,1... | collective-permute-start | bytes 776 | tf_op jit(solution)/shard_map/ppermute | solution.py:27
  0.7 3.4 %collective-permute-start = (bf16[256,128]{1,0:T(8,128)(2,1)}, bf16[256,128]{1,0:T(8,128)(2,1)S(1)}, u32[]{:S(2)}, u32[]{:S(2)}) collective-permute-start(bf16[256,128]{1,0:T(8,128)(2,1)} %param.11), channel_id=1, source_target_pairs={{0,4},{4,0},{1,5},{5,1},{2,6},{6,2},{3,7},{7,3},{8,12},{12,8},{9,1... | collective-permute-start | bytes 196616 | tf_op jit(solution)/shard_map/ppermute | solution.py:27
  2.9 2.7 %collective-permute-start.2 = (bf16[128,1280]{1,0:T(8,128)(2,1)S(1)}, bf16[128,1280]{1,0:T(8,128)(2,1)S(1)}, u32[]{:S(2)}, u32[]{:S(2)}) collective-permute-start(bf16[128,1280]{1,0:T(8,128)(2,1)S(1)} %pad_maximum_fusion.2), channel_id=1, source_target_pairs={{0,4},{4,0},{1,5},{5,1},{2,6},{6,2},{3,7},{7,3},{8,12},{12,8},{9,1... | collective-permute-start | bytes 983048 | tf_op jit(solution)/shard_map/ppermute | solution.py:27
  8.0 34.6 %collective-permute-start.5 = (bf16[512,512]{1,0:T(8,128)(2,1)}, bf16[512,512]{1,0:T(8,128)(2,1)}, u32[]{:S(2)}, u32[]{:S(2)}) collective-permute-start(bf16[512,512]{1,0:T(8,128)(2,1)} %bitcast.44.c0), channel_id=1, source_target_pairs={{0,16},{8,24},{16,0},{24,8},{1,17},{9,25},{17,1},{25,9},{2,18},{10... | collective-permute-start | bytes 1572872 | tf_op jit(solution)/shard_map/ppermute | solution.py:56
  10.3 32.2 %collective-permute-start.4 = (bf16[512,512]{1,0:T(8,128)(2,1)}, bf16[512,512]{1,0:T(8,128)(2,1)}, u32[]{:S(2)}, u32[]{:S(2)}) collective-permute-start(bf16[512,512]{1,0:T(8,128)(2,1)} %bitcast.44.c0), channel_id=1, source_target_pairs={{0,24},{8,0},{16,8},{24,16},{1,25},{9,1},{17,9},{25,17},{2,26},{10... | collective-permute-start | bytes 1572872 | tf_op jit(solution)/shard_map/ppermute | solution.py:56
  10.8 32.2 %collective-permute-start.3 = (bf16[512,512]{1,0:T(8,128)(2,1)}, bf16[512,512]{1,0:T(8,128)(2,1)}, u32[]{:S(2)}, u32[]{:S(2)}) collective-permute-start(bf16[512,512]{1,0:T(8,128)(2,1)} %bitcast.44.c0), channel_id=1, source_target_pairs={{0,8},{8,16},{16,24},{24,0},{1,9},{9,17},{17,25},{25,1},{2,10},{10... | collective-permute-start | bytes 1572872 | tf_op jit(solution)/shard_map/ppermute | solution.py:56
  12.5 41.0 %all-to-all-start = ((bf16[32,136,128]{2,1,0:T(8,128)(2,1)}), bf16[32,136,128]{2,1,0:T(8,128)(2,1)}, u32[]{:S(2)}, u32[]{:S(2)}) async-start(bf16[32,136,128]{2,1,0:T(8,128)(2,1)} %bitcast.15), calls=%async_computation | async-start | bytes 2228224 | tf_op jit(solution)/shard_map/all_to_all | solution.py:44
  27.7 1.5 collective-permute-start.6
  38.2 43.0 %collective-permute-start.11 = (bf16[8,2,336,128]{3,2,1,0:T(8,128)(2,1)}, bf16[8,2,336,128]{3,2,1,0:T(8,128)(2,1)S(1)}, u32[]{:S(2)}, u32[]{:S(2)}) collective-permute-start(bf16[8,2,336,128]{3,2,1,0:T(8,128)(2,1)} %get-tuple-element.69), channel_id=1, source_target_pairs={{0,1},{1,2},{2,3},{3,0},{4,5},{5,6},{6,7},{7,4},{8,9},{9,10},{10,1... | collective-permute-start | bytes 4128776 | tf_op jit(solution)/shard_map/ppermute | solution.py:31
  39.8 41.5 %collective-permute-start.12 = (bf16[8,2,336,128]{3,2,1,0:T(8,128)(2,1)}, bf16[8,2,336,128]{3,2,1,0:T(8,128)(2,1)}, u32[]{:S(2)}, u32[]{:S(2)}) collective-permute-start(bf16[8,2,336,128]{3,2,1,0:T(8,128)(2,1)} %get-tuple-element.71), channel_id=1, source_target_pairs={{0,3},{1,0},{2,1},{3,2},{4,7},{5,4},{6,5},{7,6},{8,11},{9,8},{10,9... | collective-permute-start | bytes 4128776 | tf_op jit(solution)/shard_map/ppermute | solution.py:31
  55.7 14.5 %all-to-all-start.1 = ((bf16[8,128,128]{2,1,0:T(8,128)(2,1)}), bf16[8,128,128]{2,1,0:T(8,128)(2,1)}, u32[]{:S(2)}, u32[]{:S(2)}) async-start(bf16[8,128,128]{2,1,0:T(8,128)(2,1)} %copy-done.4), calls=%async_computation.1 | async-start | bytes 524288 | tf_op jit(solution)/shard_map/all_to_all | solution.py:60
  59.7 21.5 %collective-permute-start.10 = (bf16[2320,128]{1,0:T(8,128)(2,1)S(1)}, bf16[2320,128]{1,0:T(8,128)(2,1)}, u32[]{:S(2)}, u32[]{:S(2)}) collective-permute-start(bf16[2320,128]{1,0:T(8,128)(2,1)S(1)} %pad_maximum_fusion.w0), channel_id=1, source_target_pairs={{0,24},{8,0},{16,8},{24,16},{1,25},{9,1},{17,9},{25,17},{2,26},{10... | collective-permute-start | bytes 1781768 | tf_op jit(solution)/shard_map/ppermute | solution.py:56
  60.4 20.9 %collective-permute-start.9 = (bf16[2320,128]{1,0:T(8,128)(2,1)S(1)}, bf16[2320,128]{1,0:T(8,128)(2,1)}, u32[]{:S(2)}, u32[]{:S(2)}) collective-permute-start(bf16[2320,128]{1,0:T(8,128)(2,1)S(1)} %pad_maximum_fusion.w0), channel_id=1, source_target_pairs={{0,8},{8,16},{16,24},{24,0},{1,9},{9,17},{17,25},{25,1},{2,10},{10... | collective-permute-start | bytes 1781768 | tf_op jit(solution)/shard_map/ppermute | solution.py:56
  70.2 1.7 collective-permute-start.7
  79.0 1.5 collective-permute-start.8
  81.3 34.2 %collective-permute-start.15 = (bf16[8,2,336,128]{3,2,1,0:T(8,128)(2,1)}, bf16[8,2,336,128]{3,2,1,0:T(8,128)(2,1)}, u32[]{:S(2)}, u32[]{:S(2)}) collective-permute-start(bf16[8,2,336,128]{3,2,1,0:T(8,128)(2,1)} %get-tuple-element.90), channel_id=1, source_target_pairs={{0,2},{1,3},{2,0},{3,1},{4,6},{5,7},{6,4},{7,5},{8,10},{9,11},{10,... | collective-permute-start | bytes 4128776 | tf_op jit(solution)/shard_map/ppermute | solution.py:31
  84.5 13.4 %all-to-all-start.2 = ((bf16[8,80,128]{2,1,0:T(8,128)(2,1)}), bf16[8,80,128]{2,1,0:T(8,128)(2,1)S(1)}, u32[]{:S(2)}, u32[]{:S(2)}) async-start(bf16[8,80,128]{2,1,0:T(8,128)(2,1)} %merge.1), calls=%async_computation.2 | async-start | bytes 327680 | tf_op jit(solution)/shard_map/all_to_all | solution.py:60
  87.9 23.8 %collective-permute-start.14 = (bf16[2320,128]{1,0:T(8,128)(2,1)S(1)}, bf16[2320,128]{1,0:T(8,128)(2,1)}, u32[]{:S(2)}, u32[]{:S(2)}) collective-permute-start(bf16[2320,128]{1,0:T(8,128)(2,1)S(1)} %pad_maximum_fusion.w0), channel_id=1, source_target_pairs={{0,16},{8,24},{16,0},{24,8},{1,17},{9,25},{17,1},{25,9},{2,18},{10... | collective-permute-start | bytes 1781768 | tf_op jit(solution)/shard_map/ppermute | solution.py:56
  115.5 4.5 %collective-permute-start.18 = (bf16[64,128]{1,0:T(8,128)(2,1)S(1)}, bf16[64,128]{1,0:T(8,128)(2,1)S(1)}, u32[]{:S(2)}, u32[]{:S(2)}) collective-permute-start(bf16[64,128]{1,0:T(8,128)(2,1)S(1)} %get-tuple-element.144), channel_id=1, source_target_pairs={{0,3},{1,0},{2,1},{3,2},{4,7},{5,4},{6,5},{7,6},{8,11},{9,8},{10,9... | collective-permute-start | bytes 49160 | tf_op jit(solution)/shard_map/ppermute | solution.py:31
  118.4 5.2 %collective-permute-start.17 = (bf16[64,128]{1,0:T(8,128)(2,1)S(1)}, bf16[64,128]{1,0:T(8,128)(2,1)S(1)}, u32[]{:S(2)}, u32[]{:S(2)}) collective-permute-start(bf16[64,128]{1,0:T(8,128)(2,1)S(1)} %get-tuple-element.145), channel_id=1, source_target_pairs={{0,2},{1,3},{2,0},{3,1},{4,6},{5,7},{6,4},{7,5},{8,10},{9,11},{10,... | collective-permute-start | bytes 49160 | tf_op jit(solution)/shard_map/ppermute | solution.py:31
  119.0 4.9 %collective-permute-start.16 = (bf16[64,128]{1,0:T(8,128)(2,1)S(1)}, bf16[64,128]{1,0:T(8,128)(2,1)S(1)}, u32[]{:S(2)}, u32[]{:S(2)}) collective-permute-start(bf16[64,128]{1,0:T(8,128)(2,1)S(1)} %get-tuple-element.146), channel_id=1, source_target_pairs={{0,1},{1,2},{2,3},{3,0},{4,5},{5,6},{6,7},{7,4},{8,9},{9,10},{10,1... | collective-permute-start | bytes 49160 | tf_op jit(solution)/shard_map/ppermute | solution.py:31
  125.5 22.5 %all-to-all-start.4 = ((bf16[32,80,128]{2,1,0:T(8,128)(2,1)}), bf16[32,80,128]{2,1,0:T(8,128)(2,1)S(1)}, u32[]{:S(2)}, u32[]{:S(2)}) async-start(bf16[32,80,128]{2,1,0:T(8,128)(2,1)} %copy-done.5), calls=%async_computation.4 | async-start | bytes 1310720 | tf_op jit(solution)/shard_map/all_to_all | solution.py:44
  148.0 2.6 %collective-permute-start.19 = (bf16[32,80,128]{2,1,0:T(8,128)(2,1)S(1)}, bf16[32,80,128]{2,1,0:T(8,128)(2,1)S(1)}, u32[]{:S(2)}, u32[]{:S(2)}) collective-permute-start(bf16[32,80,128]{2,1,0:T(8,128)(2,1)S(1)} %all-to-all-done.4.own_ref), channel_id=1, source_target_pairs={{0,4},{4,0},{1,5},{5,1},{2,6},{6,2},{3,7},{7,3},{8,12},{12,8},{9,1... | collective-permute-start | bytes 1966088 | tf_op jit(solution)/shard_map/ppermute | solution.py:27
  153.2 6.2 %collective-permute-start.20 = (bf16[240,256]{1,0:T(8,128)(2,1)S(1)}, bf16[240,256]{1,0:T(8,128)(2,1)S(1)}, u32[]{:S(2)}, u32[]{:S(2)}) collective-permute-start(bf16[240,256]{1,0:T(8,128)(2,1)S(1)} %get-tuple-element.112), channel_id=1, source_target_pairs={{0,3},{1,0},{2,1},{3,2},{4,7},{5,4},{6,5},{7,6},{8,11},{9,8},{10,9... | collective-permute-start | bytes 368648 | tf_op jit(solution)/shard_map/ppermute | solution.py:31
  154.3 7.7 %collective-permute-start.21 = (bf16[240,256]{1,0:T(8,128)(2,1)S(1)}, bf16[240,256]{1,0:T(8,128)(2,1)S(1)}, u32[]{:S(2)}, u32[]{:S(2)}) collective-permute-start(bf16[240,256]{1,0:T(8,128)(2,1)S(1)} %get-tuple-element.113), channel_id=1, source_target_pairs={{0,2},{1,3},{2,0},{3,1},{4,6},{5,7},{6,4},{7,5},{8,10},{9,11},{10,... | collective-permute-start | bytes 368648 | tf_op jit(solution)/shard_map/ppermute | solution.py:31
  155.4 8.5 %collective-permute-start.22 = (bf16[240,256]{1,0:T(8,128)(2,1)S(1)}, bf16[240,256]{1,0:T(8,128)(2,1)S(1)}, u32[]{:S(2)}, u32[]{:S(2)}) collective-permute-start(bf16[240,256]{1,0:T(8,128)(2,1)S(1)} %get-tuple-element.114), channel_id=1, source_target_pairs={{0,1},{1,2},{2,3},{3,0},{4,5},{5,6},{6,7},{7,4},{8,9},{9,10},{10,1... | collective-permute-start | bytes 368648 | tf_op jit(solution)/shard_map/ppermute | solution.py:31
  164.0 4.5 %collective-permute-start.25 = (bf16[112,256]{1,0:T(8,128)(2,1)S(1)}, bf16[112,256]{1,0:T(8,128)(2,1)S(1)}, u32[]{:S(2)}, u32[]{:S(2)}) collective-permute-start(bf16[112,256]{1,0:T(8,128)(2,1)S(1)} %act.1.a0), channel_id=1, source_target_pairs={{0,3},{1,0},{2,1},{3,2},{4,7},{5,4},{6,5},{7,6},{8,11},{9,8},{10,9... | collective-permute-start | bytes 172040 | tf_op jit(solution)/shard_map/ppermute | solution.py:31
  164.7 5.8 %collective-permute-start.24 = (bf16[112,256]{1,0:T(8,128)(2,1)S(1)}, bf16[112,256]{1,0:T(8,128)(2,1)S(1)}, u32[]{:S(2)}, u32[]{:S(2)}) collective-permute-start(bf16[112,256]{1,0:T(8,128)(2,1)S(1)} %act.1.a0), channel_id=1, source_target_pairs={{0,2},{1,3},{2,0},{3,1},{4,6},{5,7},{6,4},{7,5},{8,10},{9,11},{10,... | collective-permute-start | bytes 172040 | tf_op jit(solution)/shard_map/ppermute | solution.py:31
  165.7 5.4 %collective-permute-start.23 = (bf16[112,256]{1,0:T(8,128)(2,1)S(1)}, bf16[112,256]{1,0:T(8,128)(2,1)S(1)}, u32[]{:S(2)}, u32[]{:S(2)}) collective-permute-start(bf16[112,256]{1,0:T(8,128)(2,1)S(1)} %act.1.a0), channel_id=1, source_target_pairs={{0,1},{1,2},{2,3},{3,0},{4,5},{5,6},{6,7},{7,4},{8,9},{9,10},{10,1... | collective-permute-start | bytes 172040 | tf_op jit(solution)/shard_map/ppermute | solution.py:31
  173.3 2.0 collective-permute-start.26
  178.6 34.1 %all-to-all-start.5 = ((bf16[32,128,128]{2,1,0:T(8,128)(2,1)}), bf16[32,128,128]{2,1,0:T(8,128)(2,1)S(1)}, u32[]{:S(2)}, u32[]{:S(2)}) async-start(bf16[32,128,128]{2,1,0:T(8,128)(2,1)} %copy-done), calls=%async_computation.5 | async-start | bytes 2097152 | tf_op jit(solution)/shard_map/all_to_all | solution.py:44
  213.4 9.5 %collective-permute-start.27 = (bf16[64,128]{1,0:T(8,128)(2,1)S(1)}, bf16[64,128]{1,0:T(8,128)(2,1)S(1)}, u32[]{:S(2)}, u32[]{:S(2)}) collective-permute-start(bf16[64,128]{1,0:T(8,128)(2,1)S(1)} %add_convert_fusion), channel_id=1, source_target_pairs={{0,0},{1,8},{2,16},{3,24},{8,1},{9,9},{10,17},{11,25},{16,2},{17,1... | collective-permute-start | bytes 49160 | tf_op jit(solution)/shard_map/ppermute | solution.py:40
  (20 other events, 49.2 us)
